TPU v7x, 32 devices: a whole 2x2x4 slice. The times are simulated.
32 devices in a mesh: groups: 2 (over x), ctx: 8 (over z, y), head: 2 (over core).
Axes of the slice: x: 2, y: 2, z: 4, core: 2. Of those that a mesh axis runs over, the one named last changes fastest.
Arguments:
- query_nope: bfloat16 [32, 128, 128], P('groups', ('ctx', 'head')), parts along dimension 0, may hold values from -6 to 6
- query_rope: bfloat16 [32, 8192], P('groups', ('ctx', 'head')), parts along dimension 0, may hold values from -31 to 31
- key_absorb: bfloat16 [128, 128, 512], P(('ctx', 'head')), may hold values from -0.5 to 0.5
- value_absorb: bfloat16 [128, 512, 128], P(('ctx', 'head')), may hold values from -4 to 4
- output_weight: bfloat16 [16384, 7168], P(('ctx', 'head')), may hold values from -0.0625 to 0.0625
- latent_cache: bfloat16 [3584, 64, 576], P(('groups', 'ctx')), parts along dimension 0, may hold values from -4 to 4
- page_owner: int32 [3584], P(('groups', 'ctx')), parts along dimension 0, may hold values from -1 to 15, as said below
Outputs:
- layer_output: bfloat16 [32, 7168], P('groups', ('ctx', 'head')), parts along dimension 0
There are 2 independent parts, one for each index of `groups`. A program takes and returns all parts, laid end to end along the dimension named above; an argument that names none is the same for every part. Nothing has to cross between parts.
Inputs may be any that keep to these rules, and one draw needn't show every extreme that they name: `page_owner`: a slot's request, or -1 for an unused slot; every request owns at least one slot; every index of ctx has an eighth of its 224 slots or more in use, and some index has all 224 in use.
All inputs are finite; a program needn't handle non-finite values.
Results may differ from a plain program's by a relative error of at most 0.03.
Values may be sent and summed in bfloat16 or wider, within the bound.
No kernel may reach another device: no remote copies, remote signals or barrier semaphores. Data moves between devices by JAX's collectives and lax.ppermute only.
A program may use at most 128 MiB of HBM per device.

v0:
```python
import jax
import jax.numpy as jnp
from jax import lax
from jax.sharding import PartitionSpec as P

BLOCK_PAGES = 8


masked_score = -1e30


def body(query_nope, query_rope, key_absorb, value_absorb, output_weight, latent_cache, page_owner):
    requests, heads_here, nope_size = query_nope.shape
    latent_size = key_absorb.shape[2]
    rope_size = query_rope.shape[1] // heads_here
    pages_here, page_len, entry_size = latent_cache.shape
    score_scale = (nope_size + rope_size) ** (-0.5)
    query_latent = jnp.einsum(
        "rhn,hnl->rhl", query_nope, key_absorb, preferred_element_type=jnp.float32
    ).astype(jnp.bfloat16)
    all_latent, all_rope = (
        lax.all_gather(query_latent, "ctx", axis=1, tiled=True),
        lax.all_gather(query_rope, "ctx", axis=1, tiled=True),
    )
    heads_ctx = all_latent.shape[1]
    query_full = jnp.concatenate(
        [all_latent, all_rope.reshape(requests, heads_ctx, rope_size)], axis=2
    )
    block_count = pages_here // BLOCK_PAGES
    cache_blocks = latent_cache.reshape(block_count, BLOCK_PAGES, page_len, entry_size)
    owner_blocks = page_owner.reshape(block_count, BLOCK_PAGES)
    request_ids = jnp.arange(requests, dtype=jnp.int32)

    def score_block(inputs):
        page_rows, owner_ids = inputs
        page_query = query_full[jnp.clip(owner_ids, 0, requests - 1)]
        scores = (
            jnp.einsum("ptk,phk->pth", page_rows, page_query, preferred_element_type=jnp.float32)
            * score_scale
        )
        return jnp.where((owner_ids >= 0)[:, None, None], scores, masked_score)

    block_scores = lax.map(score_block, (cache_blocks, owner_blocks))
    page_max = jnp.max(block_scores, axis=2).reshape(pages_here, heads_ctx)
    owner_hot = page_owner[:, None] == request_ids[None, :]
    local_max = jnp.max(
        jnp.where(owner_hot[:, :, None], page_max[:, None, :], masked_score), axis=0
    )

    def sum_block(state, inputs):
        running_sum, running_total = state
        page_rows, owner_ids, scores = inputs
        offset = local_max[jnp.clip(owner_ids, 0, requests - 1)]
        weights = jnp.where(
            (owner_ids >= 0)[:, None, None], jnp.exp(scores - offset[:, None, :]), 0.0
        )
        weight_half = weights.astype(jnp.bfloat16)
        page_out = jnp.einsum(
            "pth,ptl->phl",
            weight_half,
            page_rows[:, :, :latent_size],
            preferred_element_type=jnp.float32,
        )
        target = jnp.where(owner_ids >= 0, owner_ids, requests)
        running_sum = running_sum.at[target].add(page_out, mode="drop")
        running_total = running_total.at[target].add(jnp.sum(weights, axis=1), mode="drop")
        return ((running_sum, running_total), None)

    start_state = (
        jnp.zeros((requests, heads_ctx, latent_size), jnp.float32),
        jnp.zeros((requests, heads_ctx), jnp.float32),
    )
    (latent_sum, weight_total), _ = lax.scan(
        sum_block, start_state, (cache_blocks, owner_blocks, block_scores)
    )
    got_max, got_total, got_sum = (
        lax.all_to_all(
            local_max[None].astype(jnp.bfloat16), "ctx", split_axis=2, concat_axis=0, tiled=True
        ).astype(jnp.float32),
        lax.all_to_all(
            weight_total[None].astype(jnp.bfloat16), "ctx", split_axis=2, concat_axis=0, tiled=True
        ).astype(jnp.float32),
        lax.all_to_all(
            latent_sum[None].astype(jnp.bfloat16), "ctx", split_axis=2, concat_axis=0, tiled=True
        ).astype(jnp.float32),
    )
    top_max = jnp.max(got_max, axis=0)
    factor = jnp.exp(got_max - top_max[None])
    mine_total = jnp.sum(factor * got_total, axis=0)
    mine_sum = jnp.sum(factor[..., None] * got_sum, axis=0)
    attended = (mine_sum / mine_total[..., None]).astype(jnp.bfloat16)
    head_out = jnp.einsum(
        "rhl,hlv->rhv", attended, value_absorb, preferred_element_type=jnp.float32
    ).astype(jnp.bfloat16)
    partial_out = jnp.dot(
        head_out.reshape(requests, -1), output_weight, preferred_element_type=jnp.float32
    )
    return lax.psum_scatter(
        partial_out.astype(jnp.bfloat16), ("ctx", "head"), scatter_dimension=1, tiled=True
    )


def solution(mesh):
    return jax.shard_map(
        body,
        mesh=mesh,
        in_specs=(
            P("groups", ("ctx", "head"), None),
            P("groups", ("ctx", "head")),
            P(("ctx", "head"), None, None),
            P(("ctx", "head"), None, None),
            P(("ctx", "head"), None),
            P(("groups", "ctx"), None, None),
            P(("groups", "ctx")),
        ),
        out_specs=P("groups", ("ctx", "head")),
        check_vma=False,
    )
```

profile of v0, /device:TPU:0, one launch (start us, length us, event | category | flops | bytes accessed | tf_op | source)
XLA Modules:
  0.0 473.9 jit_solution(9024620244627577398)
XLA Ops:
  10.2 32.6 %all_gather.7 = bf16[16,4096]{1,0:T(8,128)(2,1)S(1)} all-gather(bf16[16,512]{1,0:T(8,128)(2,1)} %param.12), channel_id=1, replica_groups=mesh['groups'=2,'ctx'=8,'head'=2] {'ctx'}, dimensions={1}, use_global_device_ids=true | all-gather | bytes 147456 | tf_op jit(solution)/shard_map/all_gather | solution.py:23
  44.0 8.7 %all-gather.2.cloned.1.call-done = bf16[16,64,512]{2,0,1:T(8,128)(2,1)} async-done(((bf16[16,8,512]{2,0,1:T(8,128)(2,1)}), bf16[16,64,512]{2,0,1:T(8,128)(2,1)}) %all-gather.2.cloned.1.call-update) | async-done | bytes 1048592 | tf_op jit(solution)/shard_map/all_gather | solution.py:22
  54.3 80.9 %while.22 = (s32[]{:T(128)}, f32[28,8,64,64]{3,2,1,0:T(8,128)}, s32[28,8]{1,0:T(8,128)S(1)}, bf16[28,8,64,576]{3,2,1,0:T(8,128)(2,1)}, bf16[16,64,576]{2,1,0:T(8,128)(2,1)S(1)}, /*index=5*/s32[]{:T(128)}) while((s32[]{:T(128)}, f32[28,8,64,64]{3,2,1,0:T(8,128)}, s32[28,8]{1,0:T(8,128)S(1)}, bf16[28,8,64,576]{3,2,1,0:T(8,128)(2,1)}, ...), condition=%wide.region_1.2_spmd, body=%wide.region_0.1_spmd.sunk | while | flops 37815336 | bytes 2692349 | solution.py:43
  135.2 4.8 %reduce_max.32 = f32[28,8,64]{2,1,0:T(8,128)S(1)} reduce(f32[28,8,64,64]{3,2,1,0:T(8,128)} %get-tuple-element.285, f32[]{:T(128)} %constant.33.clone.1), dimensions={2}, to_apply=%region_2.3 | reduce | flops 903168 | bytes 3727364 | tf_op jit(solution)/shard_map/reduce_max | solution.py:44
  142.0 205.1 %while.23 = (s32[]{:T(128)}, f32[16,64,512]{2,1,0:T(8,128)}, f32[16,64]{1,0:T(8,128)S(1)}, s32[28,8]{1,0:T(8,128)S(1)}, f32[28,8,64,64]{3,2,1,0:T(8,128)}, /*ind...) while((s32[]{:T(128)}, f32[16,64,512]{2,1,0:T(8,128)}, f32[16,64]{1,0:T(8,128)S(1)}, ...), condition=%wide.region_9.10_spmd, body=%wide.region_5.9_spmd.sunk | while | flops 34014288 | bytes 6839157 | solution.py:73
  145.2 3.3 scatter_fusion
  160.1 3.3 scatter_fusion
  175.0 3.3 scatter_fusion
  182.4 3.3 scatter_fusion
  204.7 3.3 scatter_fusion
  212.2 3.3 scatter_fusion
  219.7 3.4 scatter_fusion
  227.3 3.3 scatter_fusion
  234.7 3.3 scatter_fusion
  242.2 3.3 scatter_fusion
  249.6 3.3 scatter_fusion
  347.8 5.4 %all-to-all-start.2 = ((bf16[1,16,64]{1,0,2:T(2,128)(2,1)}), bf16[1,16,64]{1,0,2:T(2,128)(2,1)S(1)}, u32[]{:S(2)}, u32[]{:S(2)}) async-start(bf16[1,16,64]{1,0,2:T(2,128)(2,1)} %copy.78), calls=%async_computation.2 | async-start | bytes 65536 | tf_op jit(solution)/shard_map/all_to_all | solution.py:80
  353.8 6.0 %all-to-all-done.2 = bf16[1,16,64]{1,0,2:T(2,128)(2,1)S(1)} async-done(((bf16[1,16,64]{1,0,2:T(2,128)(2,1)}), bf16[1,16,64]{1,0,2:T(2,128)(2,1)S(1)}, u32[]{:S(2)}, u32[]{:S(2)}) %all-to-all-start.2) | async-done | bytes 2080 | tf_op jit(solution)/shard_map/all_to_all | solution.py:80
  359.8 3.3 all-to-all-start
  363.2 3.7 copy.104
  369.8 3.6 all-to-all-start.1
  373.6 22.5 %all-to-all-done.1 = bf16[1,16,64,512]{3,1,0,2:T(8,128)(2,1)S(1)} async-done(((bf16[1,16,64,512]{3,1,0,2:T(8,128)(2,1)}), bf16[1,16,64,512]{3,1,0,2:T(8,128)(2,1)S(1)}, u32[]{:S(2)}, u32[]{:S(2)}) %all-to-all-start.1) | async-done | bytes 1048608 | tf_op jit(solution)/shard_map/all_to_all | solution.py:83
  398.0 7.2 %convolution_convert_fusion = bf16[16,7168]{1,0:T(8,128)(2,1)S(1)} fusion(bf16[1024,7168]{1,0:T(8,128)(2,1)} %param.15, bf16[8,2,8,128]{3,2,1,0:T(8,128)(2,1)S(1)} %fusion.22), kind=kOutput, calls=%fused_computation.38 | convolution fusion | flops 234995712 | bytes 14942208 | tf_op jit(solution)/shard_map/dot_general | solution.py:95
  406.9 58.6 %reduce-scatter.4.cloned.1.call-done = bf16[448,16]{1,0:T(8,128)(2,1)} async-done(((bf16[7168,16]{1,0:T(8,128)(2,1)}), bf16[448,16]{1,0:T(8,128)(2,1)}) %reduce-scatter.4.cloned.1.call-update) | async-done | bytes 14352
  (473 shorter events, 264.9 us)
Async XLA Ops:
  6.5 1.2 copy-start
  6.5 46.1 %all-gather.2.cloned.1.call-start = ((), (), s32[]{:S(2)}) async-start(), calls=%async_computation.4 | async-start | bytes 1179648 | tf_op jit(solution)/shard_map/all_gather | solution.py:22
  347.8 12.1 %all-to-all-start.2 = ((bf16[1,16,64]{1,0,2:T(2,128)(2,1)}), bf16[1,16,64]{1,0,2:T(2,128)(2,1)S(1)}, u32[]{:S(2)}, u32[]{:S(2)}) async-start(bf16[1,16,64]{1,0,2:T(2,128)(2,1)} %copy.78), calls=%async_computation.2 | async-start | bytes 65536 | tf_op jit(solution)/shard_map/all_to_all | solution.py:80
  359.8 10.0 %all-to-all-start = ((bf16[1,16,64]{1,0,2:T(2,128)(2,1)}), bf16[1,16,64]{1,0,2:T(2,128)(2,1)S(1)}, u32[]{:S(2)}, u32[]{:S(2)}) async-start(bf16[1,16,64]{1,0,2:T(2,128)(2,1)} %copy.73), calls=%async_computation | async-start | bytes 65536 | tf_op jit(solution)/shard_map/all_to_all | solution.py:77
  369.8 26.3 %all-to-all-start.1 = ((bf16[1,16,64,512]{3,1,0,2:T(8,128)(2,1)}), bf16[1,16,64,512]{3,1,0,2:T(8,128)(2,1)S(1)}, u32[]{:S(2)}, u32[]{:S(2)}) async-start(bf16[1,16,64,512]{3,1,0,2:T(8,128)(2,1)} %bitcast.86), calls=%async_computation.1 | async-start | bytes 2097152 | tf_op jit(solution)/shard_map/all_to_all | solution.py:83
  373.3 92.2 %reduce-scatter.4.cloned.1.call-start = ((), (), s32[]{:S(2)}) async-start(), calls=%async_computation.5 | async-start | bytes 1949696
  396.1 1.7 copy-start.1
Sparse Core Ops, SparseCore 0:
  9.6 43.0 all-gather.1
  407.0 58.4 reduce-scatter.3
where the time goes:
time: 480 us; the launch traced here: 474 us
  other arithmetic  124 us (26%)
  local copies, waits for them, and re-layouts  110 us (23%)
  waiting for transfers between devices  98.7 us (21%)
  matrix products  79.9 us (17%)
  blocking collectives  32.6 us (7%)
  between operations  13.6 us (3%)
  starting transfers between devices  12.3 us (3%)
    scatter-add x28, other arithmetic, sum_block(): running_sum = running_sum.at[target].add(page_out, mode='drop')  88.2 us
    dot_general x28, matrix products, score_block(): jnp.einsum('ptk,phk->pth', page_rows, page_query, preferred_element_type=...  60.8 us
    unnamed x3, waiting for transfers between devices  58.6 us
    all_gather x1, blocking collectives, body(): lax.all_gather(query_rope, 'ctx', axis=1, tiled=True)  32.6 us
    squeeze x28, local copies, waits for them, and re-layouts, body(): block_scores = lax.map(score_block, (cache_blocks, owner_blocks))  32.2 us
    dynamic_slice x56, local copies, waits for them, and re-layouts, body(): lax.scan(sum_block, start_state, (cache_blocks, owner_blocks, block_scores))  30.9 us
    all_to_all x1, waiting for transfers between devices, body(): lax.all_to_all(latent_sum[None].astype(jnp.bfloat16), 'ctx', split_axis=2...  22.5 us
    gather x28, local copies, waits for them, and re-layouts, score_block(): page_query = query_full[jnp.clip(owner_ids, 0, requests - 1)]  18.6 us
  transfers between devices with their start and end apart: 5, of which 5 were waited for; matrix products, arithmetic and copies ran while one was open for 1% of the time, Pallas kernels for 0%

commit v1 on v0

v1 whole, which is shorter than its diff:
```python
import functools

import jax
import jax.numpy as jnp
from jax import lax
from jax.experimental import pallas as pl
from jax.experimental.pallas import tpu as pltpu
from jax.sharding import PartitionSpec as P

masked_score = -1e30


def ring_order(count):
    if count % 2:
        return list(range(count))
    return list(range(0, count, 2)) + list(range(count - 1, 0, -2))


def attend_kernel(
    score_scale, group_pages, owner_ref, place_ref, query_ref, cache_ref, out_ref, stat_ref,
    score_scr, max_scr, total_scr, sum_scr,
):
    requests, heads, entry_size = query_ref.shape
    pages, page_len, _ = cache_ref.shape
    latent_size = out_ref.shape[3]
    blocks, _, heads_here, _ = out_ref.shape
    pair_len = 2 * page_len
    pair_count = group_pages // 2
    groups = pages // group_pages
    first_half = lax.broadcasted_iota(jnp.int32, (heads, pair_len), 1) < page_len

    for r in range(requests + 1):
        max_scr[r] = jnp.full((heads, pair_len), masked_score, jnp.float32)
        total_scr[r] = jnp.zeros((heads, pair_len), jnp.float32)
        sum_scr[r] = jnp.zeros((heads, latent_size), jnp.float32)

    def owners_of(g):
        raw = [owner_ref[g * group_pages + k] for k in range(group_pages)]
        return [jnp.where(o < 0, requests, o) for o in raw]

    def score_group(g, carry):
        owners = owners_of(g)
        keys = cache_ref[pl.ds(g * group_pages, group_pages)].reshape(
            group_pages * page_len, entry_size
        )
        queries = jnp.concatenate(
            [query_ref[jnp.minimum(o, requests - 1)] for o in owners], axis=0
        )
        scores = (
            lax.dot_general(
                queries, keys, (((1,), (1,)), ((), ())), preferred_element_type=jnp.float32
            )
            * score_scale
        )
        for p in range(pair_count):
            left, right = 2 * p, 2 * p + 1
            columns = slice(p * pair_len, (p + 1) * pair_len)
            pair = jnp.where(
                first_half,
                scores[left * heads : (left + 1) * heads, columns],
                scores[right * heads : (right + 1) * heads, columns],
            )
            score_scr[g * pair_count + p] = pair
            max_scr[owners[left]] = jnp.maximum(
                max_scr[owners[left]], jnp.where(first_half, pair, masked_score)
            )
            max_scr[owners[right]] = jnp.maximum(
                max_scr[owners[right]], jnp.where(first_half, masked_score, pair)
            )
        return carry

    lax.fori_loop(0, groups, score_group, 0, unroll=2)

    for r in range(requests + 1):
        top = jnp.max(max_scr[r], axis=1, keepdims=True)
        max_scr[r] = jnp.broadcast_to(top, (heads, pair_len))

    def sum_group(g, carry):
        owners = owners_of(g)
        values = cache_ref[pl.ds(g * group_pages, group_pages)].reshape(
            group_pages * page_len, entry_size
        )[:, :latent_size]
        rows = []
        for p in range(pair_count):
            left, right = owners[2 * p], owners[2 * p + 1]
            offset = jnp.where(first_half, max_scr[left], max_scr[right])
            weight = jnp.exp(score_scr[g * pair_count + p] - offset)
            left_weight = jnp.where(first_half, weight, 0.0)
            right_weight = jnp.where(first_half, 0.0, weight)
            total_scr[left] += left_weight
            total_scr[right] += right_weight
            for part in (left_weight, right_weight):
                half = part.astype(jnp.bfloat16)
                pieces = [
                    half if q == p else jnp.zeros_like(half) for q in range(pair_count)
                ]
                rows.append(jnp.concatenate(pieces, axis=1))
        added = jnp.dot(
            jnp.concatenate(rows, axis=0), values, preferred_element_type=jnp.float32
        )
        for k in range(group_pages):
            sum_scr[owners[k]] += added[k * heads : (k + 1) * heads]
        return carry

    lax.fori_loop(0, groups, sum_group, 0, unroll=2)

    lane = lax.broadcasted_iota(jnp.int32, (heads, 128), 1)
    stats = jnp.full((heads, 128), masked_score, jnp.float32)
    for r in range(requests):
        total = jnp.sum(total_scr[r], axis=1, keepdims=True)
        present = total > 0.0
        safe = jnp.where(present, total, 1.0)
        mean = (sum_scr[r] * (1.0 / safe)).astype(jnp.bfloat16)
        level = jnp.where(present, max_scr[r][:, :1] + jnp.log(safe), masked_score)
        stats = jnp.where(lane == r, level, stats)
        for b in range(blocks):
            out_ref[place_ref[b], r] = mean[b * heads_here : (b + 1) * heads_here]
    for b in range(blocks):
        stat_ref[place_ref[b]] = stats[b * heads_here : (b + 1) * heads_here]


def attend(query_full, latent_cache, page_owner, places, score_scale, latent_size):
    requests, heads, entry_size = query_full.shape
    pages, page_len, _ = latent_cache.shape
    blocks = places.shape[0]
    heads_here = heads // blocks
    group_pages = 4
    vmem = pl.BlockSpec(memory_space=pltpu.VMEM)
    smem = pl.BlockSpec(memory_space=pltpu.SMEM)
    pair_len = 2 * page_len
    return pl.pallas_call(
        functools.partial(attend_kernel, score_scale, group_pages),
        out_shape=(
            jax.ShapeDtypeStruct((blocks, requests, heads_here, latent_size), jnp.bfloat16),
            jax.ShapeDtypeStruct((blocks, heads_here, 128), jnp.float32),
        ),
        in_specs=[smem, smem, vmem, vmem],
        out_specs=(vmem, vmem),
        scratch_shapes=[
            pltpu.VMEM((pages // 2, heads, pair_len), jnp.float32),
            pltpu.VMEM((requests + 1, heads, pair_len), jnp.float32),
            pltpu.VMEM((requests + 1, heads, pair_len), jnp.float32),
            pltpu.VMEM((requests + 1, heads, latent_size), jnp.float32),
        ],
        compiler_params=pltpu.CompilerParams(vmem_limit_bytes=VMEM_LIMIT),
        cost_estimate=pl.CostEstimate(
            flops=2 * pages * page_len * heads * (entry_size + latent_size) * 4,
            bytes_accessed=pages * page_len * entry_size * 2,
            transcendentals=pages * page_len * heads,
        ),
        name="attend",
    )(page_owner, places, query_full, pltpu.with_memory_space_constraint(latent_cache, pltpu.VMEM))


VMEM_LIMIT = 40 * 1024 * 1024


def body(query_nope, query_rope, key_absorb, value_absorb, output_weight, latent_cache, page_owner, ring):
    requests, heads_here, nope_size = query_nope.shape
    latent_size = key_absorb.shape[2]
    rope_size = query_rope.shape[1] // heads_here
    score_scale = (nope_size + rope_size) ** (-0.5)
    count = len(ring)
    query_latent = jnp.einsum(
        "rhn,hnl->rhl", query_nope, key_absorb, preferred_element_type=jnp.float32
    ).astype(jnp.bfloat16)
    own = jnp.concatenate(
        [query_latent, query_rope.reshape(requests, heads_here, rope_size)], axis=2
    )

    after = [(ring[i], ring[(i + 1) % count]) for i in range(count)]
    before = [(b, a) for a, b in after]
    blocks, offsets = [own], [0]
    forward = backward = own
    for step in range(1, count // 2 + 1):
        forward = lax.ppermute(forward, "ctx", after)
        blocks.append(forward)
        offsets.append(-step)
        if 2 * step < count:
            backward = lax.ppermute(backward, "ctx", before)
            blocks.append(backward)
            offsets.append(step)
    query_full = jnp.concatenate(blocks, axis=1)

    position = jnp.array([ring.index(i) for i in range(count)], jnp.int32)[lax.axis_index("ctx")]
    places = jnp.array(ring, jnp.int32)[
        (position + jnp.array(offsets, jnp.int32) + count) % count
    ]
    mean, stats = attend(query_full, latent_cache, page_owner, places, score_scale, latent_size)

    got_stats = lax.all_to_all(stats, "ctx", split_axis=0, concat_axis=0, tiled=True)
    got_mean = lax.all_to_all(mean, "ctx", split_axis=0, concat_axis=0, tiled=True)
    level = got_stats[:, :, :requests]
    share = jnp.exp(level - jnp.max(level, axis=0, keepdims=True))
    share = share / jnp.sum(share, axis=0, keepdims=True)
    attended = jnp.sum(
        share.transpose(0, 2, 1)[..., None] * got_mean.astype(jnp.float32), axis=0
    ).astype(jnp.bfloat16)
    head_out = jnp.einsum(
        "rhl,hlv->rhv", attended, value_absorb, preferred_element_type=jnp.float32
    ).astype(jnp.bfloat16)
    partial_out = jnp.dot(
        head_out.reshape(requests, -1), output_weight, preferred_element_type=jnp.float32
    ).astype(jnp.bfloat16)
    owners = lax.axis_size(("ctx", "head"))
    pieces = partial_out.reshape(requests, owners, -1).transpose(1, 0, 2)
    pieces = lax.all_to_all(pieces, ("ctx", "head"), split_axis=0, concat_axis=0, tiled=True)
    return jnp.sum(pieces.astype(jnp.float32), axis=0).astype(jnp.bfloat16)


def solution(mesh):
    return jax.shard_map(
        functools.partial(body, ring=ring_order(mesh.shape["ctx"])),
        mesh=mesh,
        in_specs=(
            P("groups", ("ctx", "head"), None),
            P("groups", ("ctx", "head")),
            P(("ctx", "head"), None, None),
            P(("ctx", "head"), None, None),
            P(("ctx", "head"), None),
            P(("groups", "ctx"), None, None),
            P(("groups", "ctx")),
        ),
        out_specs=P("groups", ("ctx", "head")),
        check_vma=False,
    )
```

time: 480 us -> 117 us (0.24); the launches traced: 474 us -> 117 us
  other arithmetic: 124 us -> 1.66 us
  local copies, waits for them, and re-layouts: 110 us -> 11.2 us
  matrix products: 79.9 us -> 8.46 us
  waiting for transfers between devices: 98.7 us -> 32.1 us
  Pallas kernels: 0 us -> 23.7 us
  between operations: 13.6 us -> 0.21 us
  blocking collectives: 32.6 us -> 26.6 us
    scatter-add x56 -> x0, other arithmetic: 106 us -> none  [the longest x28 88.2 us: sum_block(): running_sum = running_sum.at[target].add(page_out, mode='drop')]
    dot_general x56 -> x0, matrix products: 70.8 us -> none  [the longest x28 60.8 us: score_block(): jnp.einsum('ptk,phk->pth', page_rows, page_query, preferred_element_type=...]
    unnamed x3 -> x0, waiting for transfers between devices: 58.6 us -> none
    gather x56 -> x1, local copies, waits for them, and re-layouts: 34.2 us -> 1.15 us  [body(): jnp.array(ring, jnp.int32)]
    all_gather x1 -> x0, blocking collectives: 32.6 us -> none  [body(): lax.all_gather(query_rope, 'ctx', axis=1, tiled=True)]
    squeeze x28 -> x0, local copies, waits for them, and re-layouts: 32.2 us -> none  [body(): block_scores = lax.map(score_block, (cache_blocks, owner_blocks))]
    dynamic_slice x56 -> x1, local copies, waits for them, and re-layouts: 30.9 us -> 0.58 us  [body(): jnp.array([ring.index(i) for i in range(count)], jnp.int32)]
    all_to_all x0 -> x2, blocking collectives: none -> 26.6 us  [the longest x1 13.4 us: body(): lax.all_to_all(pieces, ('ctx', 'head'), split_axis=0, concat_axis=0, tile...]
  transfers between devices with their start and end apart: 5 -> 8, of which waited for: 5 -> 6; matrix products, arithmetic and copies ran while one was open for 1% -> 2% of each run, Pallas kernels for 0% -> 0%
where the time goes in v1:
time: 117 us
  waiting for transfers between devices  32.1 us (27%)
  blocking collectives  26.6 us (23%)
  Pallas kernels  23.7 us (20%)
  starting transfers between devices  12.9 us (11%)
  local copies, waits for them, and re-layouts  11.2 us (10%)
  matrix products  8.46 us (7%)
  other arithmetic  1.66 us (1%)
    pallas_call x1, Pallas kernels, attend(): pl.pallas_call(functools.partial(attend_kernel, score_scale, group_pages)...  23.7 us
    all_to_all x1, waiting for transfers between devices, body(): lax.all_to_all(mean, 'ctx', split_axis=0, concat_axis=0, tiled=True)  20.3 us
    all_to_all x1, blocking collectives, body(): lax.all_to_all(pieces, ('ctx', 'head'), split_axis=0, concat_axis=0, tile...  13.4 us
    all_to_all x1, blocking collectives, body(): lax.all_to_all(stats, 'ctx', split_axis=0, concat_axis=0, tiled=True)  13.2 us
    ppermute x4, waiting for transfers between devices, body(): forward = lax.ppermute(forward, 'ctx', after)  11.8 us
    unnamed x22, local copies, waits for them, and re-layouts  8.66 us
    ppermute x4, starting transfers between devices, body(): forward = lax.ppermute(forward, 'ctx', after)  8.62 us
    dot_general x1, matrix products, body(): jnp.dot(head_out.reshape(requests, -1), output_weight, preferred_element_...  7.21 us
  transfers between devices with their start and end apart: 8, of which 6 were waited for; matrix products, arithmetic and copies ran while one was open for 2% of the time, Pallas kernels for 0%

profile of v1, /device:TPU:0, one launch (start us, length us, event | category | flops | bytes accessed | tf_op | source)
XLA Modules:
  0.0 116.7 jit_solution(6104445597492057532)
XLA Ops:
  0.0 1.2 %copy-done = bf16[8,128,512]{2,1,0:T(8,128)(2,1)S(1)} copy-done((bf16[8,128,512]{2,1,0:T(8,128)(2,1)S(1)}, bf16[8,128,512]{2,1,0:T(8,128)(2,1)}, u32[]{:S(2)}) %copy-start) | copy-done | bytes 1048600
  1.2 1.0 fusion.5
  2.5 3.1 %collective-permute-start = (bf16[16,8,576]{2,1,0:T(8,128)(2,1)S(1)}, bf16[16,8,576]{2,1,0:T(8,128)(2,1)S(1)}, u32[]{:S(2)}, u32[]{:S(2)}) collective-permute-start(bf16[16,8,576]{2,1,0:T(8,128)(2,1)S(1)} %get-tuple-element.9), channel_id=1, source_target_pairs={{0,4},{4,8},{8,12},{12,14},{14,10},{10,6},{6,2},{2,0},{1,5},{5,9},... | collective-permute-start | bytes 442376 | tf_op jit(solution)/shard_map/ppermute | solution.py:176
  5.6 0.6 dynamic_slice.3
  6.1 0.7 compare_select_fusion
  6.8 1.2 gather_fusion
  8.0 1.7 %collective-permute-done = bf16[16,8,576]{2,1,0:T(8,128)(2,1)S(1)} collective-permute-done((bf16[16,8,576]{2,1,0:T(8,128)(2,1)S(1)}, bf16[16,8,576]{2,1,0:T(8,128)(2,1)S(1)}, u32[]{:S(2)}, u32[]{:S(2)}) %collective-permute-start) | collective-permute-done | bytes 147488 | tf_op jit(solution)/shard_map/ppermute | solution.py:176
  9.7 1.8 %collective-permute-start.2 = (bf16[16,8,576]{2,1,0:T(8,128)(2,1)S(1)}, bf16[16,8,576]{2,1,0:T(8,128)(2,1)S(1)}, u32[]{:S(2)}, u32[]{:S(2)}) collective-permute-start(bf16[16,8,576]{2,1,0:T(8,128)(2,1)S(1)} %collective-permute-done), channel_id=1, source_target_pairs={{0,4},{4,8},{8,12},{12,14},{14,10},{10,6},{6,2},{2,0},{1,5},{5,9},... | collective-permute-start | bytes 442376 | tf_op jit(solution)/shard_map/ppermute | solution.py:176
  11.8 3.2 %collective-permute-done.2 = bf16[16,8,576]{2,1,0:T(8,128)(2,1)S(1)} collective-permute-done((bf16[16,8,576]{2,1,0:T(8,128)(2,1)S(1)}, bf16[16,8,576]{2,1,0:T(8,128)(2,1)S(1)}, u32[]{:S(2)}, u32[]{:S(2)}) %collective-permute-start.2) | collective-permute-done | bytes 147488 | tf_op jit(solution)/shard_map/ppermute | solution.py:176
  15.1 1.7 %collective-permute-start.4 = (bf16[16,8,576]{2,1,0:T(8,128)(2,1)S(1)}, bf16[16,8,576]{2,1,0:T(8,128)(2,1)S(1)}, u32[]{:S(2)}, u32[]{:S(2)}) collective-permute-start(bf16[16,8,576]{2,1,0:T(8,128)(2,1)S(1)} %collective-permute-done.2), channel_id=1, source_target_pairs={{0,4},{4,8},{8,12},{12,14},{14,10},{10,6},{6,2},{2,0},{1,5},{5,9},... | collective-permute-start | bytes 442376 | tf_op jit(solution)/shard_map/ppermute | solution.py:176
  16.9 0.3 collective-permute-start.5
  17.2 3.6 %collective-permute-done.4 = bf16[16,8,576]{2,1,0:T(8,128)(2,1)S(1)} collective-permute-done((bf16[16,8,576]{2,1,0:T(8,128)(2,1)S(1)}, bf16[16,8,576]{2,1,0:T(8,128)(2,1)S(1)}, u32[]{:S(2)}, u32[]{:S(2)}) %collective-permute-start.4) | collective-permute-done | bytes 147488 | tf_op jit(solution)/shard_map/ppermute | solution.py:176
  20.9 2.0 %collective-permute-start.6 = (bf16[16,8,576]{2,1,0:T(8,128)(2,1)S(1)}, bf16[16,8,576]{2,1,0:T(8,128)(2,1)S(1)}, u32[]{:S(2)}, u32[]{:S(2)}) collective-permute-start(bf16[16,8,576]{2,1,0:T(8,128)(2,1)S(1)} %collective-permute-done.4), channel_id=1, source_target_pairs={{0,4},{4,8},{8,12},{12,14},{14,10},{10,6},{6,2},{2,0},{1,5},{5,9},... | collective-permute-start | bytes 442376 | tf_op jit(solution)/shard_map/ppermute | solution.py:176
  22.9 3.2 %collective-permute-done.6 = bf16[16,8,576]{2,1,0:T(8,128)(2,1)S(1)} collective-permute-done((bf16[16,8,576]{2,1,0:T(8,128)(2,1)S(1)}, bf16[16,8,576]{2,1,0:T(8,128)(2,1)S(1)}, u32[]{:S(2)}, u32[]{:S(2)}) %collective-permute-start.6) | collective-permute-done | bytes 147488 | tf_op jit(solution)/shard_map/ppermute | solution.py:176
  26.2 1.1 copy-done.4
  27.3 6.2 %copy-done.1 = bf16[224,64,576]{2,1,0:T(8,128)(2,1)S(1)} copy-done((bf16[224,64,576]{2,1,0:T(8,128)(2,1)S(1)}, bf16[224,64,576]{2,1,0:T(8,128)(2,1)}, u32[]{:S(2)}) %copy-start.1) | copy-done | bytes 16515096
  33.5 23.7 %attend.1 = (bf16[8,16,8,512]{3,2,1,0:T(8,128)(2,1)}, f32[8,8,128]{2,1,0:T(8,128)}) custom-call(s32[224]{0:T(256)} %owner_ref.1, s32[8]{0:T(128)} %gather_fusion, bf16[16,64,576]{2,1,0:T(8,128)(2,1)} %copy-done.4, bf16[224,64,576]{2,1,0:T(8,128)(2,1)S(1)} %copy-done.1), custom_call_target="tpu_custom_call" | custom-call | flops 7985954816 | bytes 16515072 | tf_op jit(solution)/shard_map/attend/pallas_call | solution.py:131
  57.2 13.2 %all_to_all.15 = f32[8,8,128]{2,1,0:T(8,128)S(1)} all-to-all(f32[8,8,128]{2,1,0:T(8,128)} %get-tuple-element.7), channel_id=1, replica_groups=mesh['groups'=2,'ctx'=8,'head'=2] {'ctx'}, dimensions={0} | all-to-all | bytes 65536 | tf_op jit(solution)/shard_map/all_to_all | solution.py:191
  70.3 3.7 %all-to-all-start.1 = ((bf16[8,16,8,512]{3,2,1,0:T(8,128)(2,1)}), bf16[8,16,8,512]{3,2,1,0:T(8,128)(2,1)S(1)}, u32[]{:S(2)}, u32[]{:S(2)}) async-start(bf16[8,16,8,512]{3,2,1,0:T(8,128)(2,1)} %get-tuple-element.8), calls=%async_computation.1 | async-start | bytes 2097152 | tf_op jit(solution)/shard_map/all_to_all | solution.py:192
  74.2 20.3 %all-to-all-done.1 = bf16[8,16,8,512]{3,2,1,0:T(8,128)(2,1)S(1)} async-done(((bf16[8,16,8,512]{3,2,1,0:T(8,128)(2,1)}), bf16[8,16,8,512]{3,2,1,0:T(8,128)(2,1)S(1)}, u32[]{:S(2)}, u32[]{:S(2)}) %all-to-all-start.1) | async-done | bytes 1048608 | tf_op jit(solution)/shard_map/all_to_all | solution.py:192
  95.0 7.2 %convolution_convert_fusion = bf16[16,7168]{1,0:T(8,128)(2,1)S(1)} fusion(bf16[1024,7168]{1,0:T(8,128)(2,1)} %param.14, bf16[8,2,8,128]{3,2,1,0:T(8,128)(2,1)S(1)} %fusion), kind=kOutput, calls=%fused_computation.1 | convolution fusion | flops 234995712 | bytes 14942208 | tf_op jit(solution)/shard_map/dot_general | solution.py:202
  102.2 0.3 reshape.14
  102.7 13.4 %all_to_all.16 = bf16[16,16,448]{2,1,0:T(8,128)(2,1)S(1)} all-to-all(bf16[16,16,448]{2,1,0:T(8,128)(2,1)S(1)} %bitcast.18), channel_id=1, replica_groups=mesh['groups'=2,'ctx'=8,'head'=2] {'ctx','head'}, dimensions={0} | all-to-all | bytes 458752 | tf_op jit(solution)/shard_map/all_to_all | solution.py:207
  116.1 0.7 reduce_sum.32
  (36 shorter events, 1.6 us)
Async XLA Ops:
  0.0 1.2 %copy-start = (bf16[8,128,512]{2,1,0:T(8,128)(2,1)S(1)}, bf16[8,128,512]{2,1,0:T(8,128)(2,1)}, u32[]{:S(2)}) copy-start(bf16[8,128,512]{2,1,0:T(8,128)(2,1)} %param.12) | copy-start | bytes 3145732
  0.0 5.6 %copy-start.7 = (s32[8]{0:T(128)S(1)}, s32[8]{0:T(128)}, u32[]{:S(2)}) copy-start(s32[8]{0:T(128)} %constant.36.clone) | copy-start | bytes 100
  0.0 6.1 %copy-start.6 = (s32[8]{0:T(128)S(1)}, s32[8]{0:T(128)}, u32[]{:S(2)}) copy-start(s32[8]{0:T(128)} %constant.38.clone) | copy-start | bytes 100
  0.0 6.8 %copy-start.2 = (s32[8]{0:T(128)S(1)}, s32[8]{0:T(128)}, u32[]{:S(2)}) copy-start(s32[8]{0:T(128)} %constant.37.clone) | copy-start | bytes 100
  0.0 2.3 %copy-start.5 = (bf16[16,512]{1,0:T(8,128)(2,1)S(1)}, bf16[16,512]{1,0:T(8,128)(2,1)}, u32[]{:S(2)}) copy-start(bf16[16,512]{1,0:T(8,128)(2,1)} %param.11) | copy-start | bytes 49156
  2.5 7.2 %collective-permute-start = (bf16[16,8,576]{2,1,0:T(8,128)(2,1)S(1)}, bf16[16,8,576]{2,1,0:T(8,128)(2,1)S(1)}, u32[]{:S(2)}, u32[]{:S(2)}) collective-permute-start(bf16[16,8,576]{2,1,0:T(8,128)(2,1)S(1)} %get-tuple-element.9), channel_id=1, source_target_pairs={{0,4},{4,8},{8,12},{12,14},{14,10},{10,6},{6,2},{2,0},{1,5},{5,9},... | collective-permute-start | bytes 442376 | tf_op jit(solution)/shard_map/ppermute | solution.py:176
  5.6 6.0 %collective-permute-start.1 = (bf16[16,8,576]{2,1,0:T(8,128)(2,1)S(1)}, bf16[16,8,576]{2,1,0:T(8,128)(2,1)S(1)}, u32[]{:S(2)}, u32[]{:S(2)}) collective-permute-start(bf16[16,8,576]{2,1,0:T(8,128)(2,1)S(1)} %get-tuple-element.9), channel_id=1, source_target_pairs={{4,0},{8,4},{12,8},{14,12},{10,14},{6,10},{2,6},{0,2},{5,1},{9,5},... | collective-permute-start | bytes 442376 | tf_op jit(solution)/shard_map/ppermute | solution.py:180
  9.7 5.4 %collective-permute-start.2 = (bf16[16,8,576]{2,1,0:T(8,128)(2,1)S(1)}, bf16[16,8,576]{2,1,0:T(8,128)(2,1)S(1)}, u32[]{:S(2)}, u32[]{:S(2)}) collective-permute-start(bf16[16,8,576]{2,1,0:T(8,128)(2,1)S(1)} %collective-permute-done), channel_id=1, source_target_pairs={{0,4},{4,8},{8,12},{12,14},{14,10},{10,6},{6,2},{2,0},{1,5},{5,9},... | collective-permute-start | bytes 442376 | tf_op jit(solution)/shard_map/ppermute | solution.py:176
  11.5 5.4 %collective-permute-start.3 = (bf16[16,8,576]{2,1,0:T(8,128)(2,1)S(1)}, bf16[16,8,576]{2,1,0:T(8,128)(2,1)S(1)}, u32[]{:S(2)}, u32[]{:S(2)}) collective-permute-start(bf16[16,8,576]{2,1,0:T(8,128)(2,1)S(1)} %collective-permute-done.1), channel_id=1, source_target_pairs={{4,0},{8,4},{12,8},{14,12},{10,14},{6,10},{2,6},{0,2},{5,1},{9,5},... | collective-permute-start | bytes 442376 | tf_op jit(solution)/shard_map/ppermute | solution.py:180
  15.1 5.8 %collective-permute-start.4 = (bf16[16,8,576]{2,1,0:T(8,128)(2,1)S(1)}, bf16[16,8,576]{2,1,0:T(8,128)(2,1)S(1)}, u32[]{:S(2)}, u32[]{:S(2)}) collective-permute-start(bf16[16,8,576]{2,1,0:T(8,128)(2,1)S(1)} %collective-permute-done.2), channel_id=1, source_target_pairs={{0,4},{4,8},{8,12},{12,14},{14,10},{10,6},{6,2},{2,0},{1,5},{5,9},... | collective-permute-start | bytes 442376 | tf_op jit(solution)/shard_map/ppermute | solution.py:176
  16.9 6.0 %collective-permute-start.5 = (bf16[16,8,576]{2,1,0:T(8,128)(2,1)S(1)}, bf16[16,8,576]{2,1,0:T(8,128)(2,1)S(1)}, u32[]{:S(2)}, u32[]{:S(2)}) collective-permute-start(bf16[16,8,576]{2,1,0:T(8,128)(2,1)S(1)} %collective-permute-done.3), channel_id=1, source_target_pairs={{4,0},{8,4},{12,8},{14,12},{10,14},{6,10},{2,6},{0,2},{5,1},{9,5},... | collective-permute-start | bytes 442376 | tf_op jit(solution)/shard_map/ppermute | solution.py:180
  20.9 5.3 %collective-permute-start.6 = (bf16[16,8,576]{2,1,0:T(8,128)(2,1)S(1)}, bf16[16,8,576]{2,1,0:T(8,128)(2,1)S(1)}, u32[]{:S(2)}, u32[]{:S(2)}) collective-permute-start(bf16[16,8,576]{2,1,0:T(8,128)(2,1)S(1)} %collective-permute-done.4), channel_id=1, source_target_pairs={{0,4},{4,8},{8,12},{12,14},{14,10},{10,6},{6,2},{2,0},{1,5},{5,9},... | collective-permute-start | bytes 442376 | tf_op jit(solution)/shard_map/ppermute | solution.py:176
  26.2 1.1 copy-start.4
  27.3 6.2 %copy-start.1 = (bf16[224,64,576]{2,1,0:T(8,128)(2,1)S(1)}, bf16[224,64,576]{2,1,0:T(8,128)(2,1)}, u32[]{:S(2)}) copy-start(bf16[224,64,576]{2,1,0:T(8,128)(2,1)} %cache_ref.1) | copy-start | bytes 49545220
  70.3 24.4 %copy-start.3 = (bf16[8,512,128]{2,1,0:T(8,128)(2,1)S(1)}, bf16[8,512,128]{2,1,0:T(8,128)(2,1)}, u32[]{:S(2)}) copy-start(bf16[8,512,128]{2,1,0:T(8,128)(2,1)} %param.13) | copy-start | bytes 3145732
  70.3 24.1 %all-to-all-start.1 = ((bf16[8,16,8,512]{3,2,1,0:T(8,128)(2,1)}), bf16[8,16,8,512]{3,2,1,0:T(8,128)(2,1)S(1)}, u32[]{:S(2)}, u32[]{:S(2)}) async-start(bf16[8,16,8,512]{3,2,1,0:T(8,128)(2,1)} %get-tuple-element.8), calls=%async_computation.1 | async-start | bytes 2097152 | tf_op jit(solution)/shard_map/all_to_all | solution.py:192

commit v2 on v1

v2 whole, which is shorter than its diff:
```python
import functools

import jax
import jax.numpy as jnp
from jax import lax
from jax.experimental import pallas as pl
from jax.experimental.pallas import tpu as pltpu
from jax.sharding import PartitionSpec as P

masked_score = -1e30
LANES = 128
GROUP_PAGES = 4
MIB = 1024 * 1024

VMEM_SPEC = pl.BlockSpec(memory_space=pltpu.VMEM)
SMEM_SPEC = pl.BlockSpec(memory_space=pltpu.SMEM)


def in_vmem(x):
    return pltpu.with_memory_space_constraint(x, pltpu.VMEM)


def ring_order(count):
    if count % 2:
        return list(range(count))
    return list(range(0, count, 2)) + list(range(count - 1, 0, -2))


def split_level(level):
    high = level.astype(jnp.bfloat16)
    rest = level - high.astype(jnp.float32)
    middle = rest.astype(jnp.bfloat16)
    low = (rest - middle.astype(jnp.float32)).astype(jnp.bfloat16)
    return high, middle, low


def store_level(message_ref, row, level):
    for i, part in enumerate(split_level(level)):
        message_ref[row, :, i * LANES : (i + 1) * LANES] = part


def load_level(message_ref, row):
    parts = [
        message_ref[row, :, i * LANES : (i + 1) * LANES].astype(jnp.float32) for i in range(3)
    ]
    return (parts[0] + parts[1]) + parts[2]


def attend_kernel(score_scale, chunks, blocks, owner_ref, query_ref, cache_ref, weight_ref, *refs):
    message_refs = refs[:blocks]
    (
        weight_out, cache_scr, score_scr, max_scr, total_scr, sum_scr, cache_sem, weight_sem
    ) = refs[blocks:]
    requests, heads, entry_size = query_ref.shape
    pages, page_len, _ = cache_ref.shape
    _, heads_here, latent_size = message_refs[0].shape
    pair_len = 2 * page_len
    pair_count = GROUP_PAGES // 2
    groups_chunk = pages // GROUP_PAGES // chunks
    pages_chunk = pages // chunks
    group_len = GROUP_PAGES * page_len

    def cache_copy(c):
        rows = pl.ds(c * pages_chunk, pages_chunk)
        return pltpu.make_async_copy(cache_ref.at[rows], cache_scr.at[rows], cache_sem.at[c])

    for c in range(chunks):
        cache_copy(c).start()
    weight_copy = pltpu.make_async_copy(weight_ref, weight_out, weight_sem)
    weight_copy.start()

    first_half = lax.broadcasted_iota(jnp.int32, (heads, pair_len), 1) < page_len

    for r in range(requests + 1):
        max_scr[r] = jnp.full((heads, pair_len), masked_score, jnp.float32)
        total_scr[r] = jnp.zeros((heads, pair_len), jnp.float32)
        sum_scr[r] = jnp.zeros((heads, latent_size), jnp.float32)

    def owners_of(g):
        raw = [owner_ref[g * GROUP_PAGES + k] for k in range(GROUP_PAGES)]
        return [jnp.where(o < 0, requests, o) for o in raw]

    def score_group(g):
        owners = owners_of(g)
        keys = cache_scr[pl.ds(g * GROUP_PAGES, GROUP_PAGES)].reshape(group_len, entry_size)
        queries = jnp.concatenate(
            [query_ref[jnp.minimum(o, requests - 1)] for o in owners], axis=0
        )
        scores = lax.dot_general(
            queries, keys, (((1,), (1,)), ((), ())), preferred_element_type=jnp.float32
        )
        for p in range(pair_count):
            left, right = 2 * p, 2 * p + 1
            columns = slice(p * pair_len, (p + 1) * pair_len)
            pair = score_scale * jnp.where(
                first_half,
                scores[left * heads : (left + 1) * heads, columns],
                scores[right * heads : (right + 1) * heads, columns],
            )
            score_scr[g * pair_count + p] = pair
            max_scr[owners[left]] = jnp.maximum(
                max_scr[owners[left]], jnp.where(first_half, pair, masked_score)
            )
            max_scr[owners[right]] = jnp.maximum(
                max_scr[owners[right]], jnp.where(first_half, masked_score, pair)
            )

    def score_chunk(c, carry):
        cache_copy(c).wait()
        for i in range(groups_chunk):
            score_group(c * groups_chunk + i)
        return carry

    lax.fori_loop(0, chunks, score_chunk, 0)

    for r in range(requests + 1):
        top = jnp.max(max_scr[r], axis=1, keepdims=True)
        max_scr[r] = jnp.broadcast_to(top, (heads, pair_len))

    def sum_group(g):
        owners = owners_of(g)
        values = cache_scr[pl.ds(g * GROUP_PAGES, GROUP_PAGES)].reshape(group_len, entry_size)[
            :, :latent_size
        ]
        rows = []
        for p in range(pair_count):
            left, right = owners[2 * p], owners[2 * p + 1]
            offset = jnp.where(first_half, max_scr[left], max_scr[right])
            weight = jnp.exp(score_scr[g * pair_count + p] - offset)
            left_weight = jnp.where(first_half, weight, 0.0)
            right_weight = jnp.where(first_half, 0.0, weight)
            total_scr[left] += left_weight
            total_scr[right] += right_weight
            for part in (left_weight, right_weight):
                half = part.astype(jnp.bfloat16)
                pieces = [half if q == p else jnp.zeros_like(half) for q in range(pair_count)]
                rows.append(jnp.concatenate(pieces, axis=1))
        added = jnp.dot(
            jnp.concatenate(rows, axis=0), values, preferred_element_type=jnp.float32
        )
        for k in range(GROUP_PAGES):
            sum_scr[owners[k]] += added[k * heads : (k + 1) * heads]

    def sum_chunk(c, carry):
        for i in range(groups_chunk):
            sum_group(c * groups_chunk + i)
        return carry

    lax.fori_loop(0, chunks, sum_chunk, 0)

    lane = lax.broadcasted_iota(jnp.int32, (heads, LANES), 1)
    stats = jnp.full((heads, LANES), masked_score, jnp.float32)
    for r in range(requests):
        total = jnp.sum(total_scr[r], axis=1, keepdims=True)
        present = total > 0.0
        safe = jnp.where(present, total, 1.0)
        mean = (sum_scr[r] * (1.0 / safe)).astype(jnp.bfloat16)
        level = jnp.where(present, max_scr[r][:, :1] + jnp.log(safe), masked_score)
        stats = jnp.where(lane == r, level, stats)
        for b in range(blocks):
            message_refs[b][r] = mean[b * heads_here : (b + 1) * heads_here]
    for b in range(blocks):
        message_refs[b][requests] = jnp.zeros((heads_here, latent_size), jnp.bfloat16)
        store_level(message_refs[b], requests, stats[b * heads_here : (b + 1) * heads_here])
    weight_copy.wait()


def attend(query_full, latent_cache, page_owner, output_weight, score_scale, latent_size, blocks):
    requests, heads, entry_size = query_full.shape
    pages, page_len, _ = latent_cache.shape
    heads_here = heads // blocks
    pair_len = 2 * page_len
    groups = pages // GROUP_PAGES
    chunks = groups // max(d for d in range(1, 9) if groups % d == 0)
    any_spec = pl.BlockSpec(memory_space=pl.ANY)
    out = pl.pallas_call(
        functools.partial(attend_kernel, score_scale, chunks, blocks),
        out_shape=[
            pltpu.VMEM((requests + 1, heads_here, latent_size), jnp.bfloat16)
            for _ in range(blocks)
        ]
        + [pltpu.VMEM(output_weight.shape, output_weight.dtype)],
        in_specs=[SMEM_SPEC, VMEM_SPEC, any_spec, any_spec],
        out_specs=[VMEM_SPEC] * (blocks + 1),
        scratch_shapes=[
            pltpu.VMEM(latent_cache.shape, latent_cache.dtype),
            pltpu.VMEM((pages // 2, heads, pair_len), jnp.float32),
            pltpu.VMEM((requests + 1, heads, pair_len), jnp.float32),
            pltpu.VMEM((requests + 1, heads, pair_len), jnp.float32),
            pltpu.VMEM((requests + 1, heads, latent_size), jnp.float32),
            pltpu.SemaphoreType.DMA((chunks,)),
            pltpu.SemaphoreType.DMA,
        ],
        compiler_params=pltpu.CompilerParams(vmem_limit_bytes=34 * MIB),
        cost_estimate=pl.CostEstimate(
            flops=2 * pages * page_len * heads * (entry_size + latent_size) * 4,
            bytes_accessed=pages * page_len * entry_size * 2,
            transcendentals=pages * page_len * heads,
        ),
        name="attend",
    )(page_owner, in_vmem(query_full), latent_cache, output_weight)
    return out[:blocks], out[blocks]


def shares(levels):
    top = functools.reduce(jnp.maximum, levels)
    parts = [jnp.exp(level - top) for level in levels]
    total = functools.reduce(jnp.add, parts)
    return [part / total for part in parts], top + jnp.log(total)


def merge_kernel(own_ref, got_ref, out_ref):
    requests = own_ref.shape[0] - 1
    both = (own_ref, got_ref)
    weights, level = shares([load_level(ref, requests) for ref in both])
    for r in range(requests):
        out_ref[r] = sum(
            w[:, r : r + 1] * ref[r].astype(jnp.float32) for w, ref in zip(weights, both)
        ).astype(jnp.bfloat16)
    out_ref[requests] = jnp.zeros(out_ref.shape[1:], jnp.bfloat16)
    store_level(out_ref, requests, level)


def merge(own, got):
    return pl.pallas_call(
        merge_kernel,
        out_shape=pltpu.VMEM(own.shape, own.dtype),
        in_specs=[VMEM_SPEC] * 2,
        out_specs=VMEM_SPEC,
        cost_estimate=pl.CostEstimate(flops=4 * own.size, bytes_accessed=0, transcendentals=0),
        name="merge",
    )(in_vmem(own), in_vmem(got))


def finish_kernel(
    block_columns, here_ref, own_ref, forward_ref, backward_ref, value_ref, weight_ref, out_ref,
    attended_scr, head_scr,
):
    requests, heads_here = own_ref.shape[0] - 1, own_ref.shape[1]
    value_size = value_ref.shape[2]
    owners, _, width = out_ref.shape
    messages = (own_ref, forward_ref, backward_ref)
    weights, _ = shares([load_level(ref, requests) for ref in messages])
    for r in range(requests):
        attended_scr[r * heads_here : (r + 1) * heads_here] = sum(
            w[:, r : r + 1] * ref[r].astype(jnp.float32) for w, ref in zip(weights, messages)
        )
    attended = attended_scr[...].astype(jnp.bfloat16)
    row = lax.broadcasted_iota(jnp.int32, (requests, requests * heads_here), 0)
    column = lax.broadcasted_iota(jnp.int32, (requests, requests * heads_here), 1)
    for h in range(heads_here):
        pick = jnp.where(column == row * heads_here + h, 1.0, 0.0).astype(jnp.bfloat16)
        rows = jnp.dot(pick, attended, preferred_element_type=jnp.float32).astype(jnp.bfloat16)
        head_scr[:, h * value_size : (h + 1) * value_size] = jnp.dot(
            rows, value_ref[h], preferred_element_type=jnp.float32
        ).astype(jnp.bfloat16)
    head_out = head_scr[...]
    per_block = block_columns // width
    bits = owners.bit_length() - 1
    for j in range(owners // per_block):
        product = jnp.dot(
            head_out,
            weight_ref[:, j * block_columns : (j + 1) * block_columns],
            preferred_element_type=jnp.float32,
        ).astype(jnp.bfloat16)
        for i in range(per_block):
            distance = here_ref[0] ^ (j * per_block + i)
            place = sum(((distance >> b) & 1) << (bits - 1 - b) for b in range(bits))
            out_ref[place] = product[:, i * width : (i + 1) * width]


def finish(here, own, forward, backward, value_absorb, weight, owners):
    requests, heads_here = own.shape[0] - 1, own.shape[1]
    latent_size, value_size = value_absorb.shape[1:]
    depth, columns = weight.shape
    width = columns // owners
    block_columns = width
    while block_columns % LANES:
        block_columns *= 2
    return pl.pallas_call(
        functools.partial(finish_kernel, block_columns),
        out_shape=pltpu.VMEM((owners, requests, width), jnp.bfloat16),
        in_specs=[SMEM_SPEC] + [VMEM_SPEC] * 5,
        out_specs=VMEM_SPEC,
        scratch_shapes=[
            pltpu.VMEM((requests * heads_here, latent_size), jnp.float32),
            pltpu.VMEM((requests, heads_here * value_size), jnp.bfloat16),
        ],
        compiler_params=pltpu.CompilerParams(vmem_limit_bytes=8 * MIB),
        cost_estimate=pl.CostEstimate(
            flops=2 * 256 * depth * columns, bytes_accessed=0, transcendentals=0
        ),
        name="finish",
    )(here, *[in_vmem(x) for x in (own, forward, backward, value_absorb, weight)])


def body(
    query_nope, query_rope, key_absorb, value_absorb, output_weight, latent_cache, page_owner, ring
):
    requests, heads_here, nope_size = query_nope.shape
    latent_size = key_absorb.shape[2]
    rope_size = query_rope.shape[1] // heads_here
    score_scale = (nope_size + rope_size) ** (-0.5)
    count = len(ring)
    query_latent = jnp.einsum(
        "rhn,hnl->rhl", query_nope, key_absorb, preferred_element_type=jnp.float32
    ).astype(jnp.bfloat16)
    own = jnp.concatenate(
        [query_latent, query_rope.reshape(requests, heads_here, rope_size)], axis=2
    )

    after = [(ring[i], ring[(i + 1) % count]) for i in range(count)]
    before = [(b, a) for a, b in after]
    blocks, offsets = [own], [0]
    forward = backward = own
    for step in range(1, count // 2 + 1):
        forward = lax.ppermute(forward, "ctx", after)
        blocks.append(forward)
        offsets.append(-step)
        if 2 * step < count:
            backward = lax.ppermute(backward, "ctx", before)
            blocks.append(backward)
            offsets.append(step)
    query_full = jnp.concatenate(blocks, axis=1)

    messages, weight = attend(
        query_full, latent_cache, page_owner, output_weight, score_scale, latent_size, count
    )
    message_to = {offset % count: message for offset, message in zip(offsets, messages)}

    forward_steps, backward_steps = count // 2, (count - 1) // 2
    forward, backward = message_to[forward_steps], message_to[-backward_steps % count]
    for step in range(1, forward_steps + 1):
        forward = lax.ppermute(forward, "ctx", after)
        if step <= backward_steps:
            backward = lax.ppermute(backward, "ctx", before)
        if step < forward_steps:
            forward = merge(message_to[forward_steps - step], forward)
        if step < backward_steps:
            backward = merge(message_to[(step - backward_steps) % count], backward)

    axes = ("ctx", "head")
    owners = lax.axis_size(axes)
    here = lax.axis_index(axes).astype(jnp.int32).reshape(1)
    pieces = finish(here, message_to[0], forward, backward, value_absorb, weight, owners)
    distance = 1
    while distance < owners:
        pairs = [(i, i ^ distance) for i in range(owners)]
        half = pieces.shape[0] // 2
        got = lax.ppermute(pieces[half:], axes, pairs)
        pieces = (pieces[:half].astype(jnp.float32) + got.astype(jnp.float32)).astype(
            jnp.bfloat16
        )
        distance *= 2
    return pieces[0]


def solution(mesh):
    return jax.shard_map(
        functools.partial(body, ring=ring_order(mesh.shape["ctx"])),
        mesh=mesh,
        in_specs=(
            P("groups", ("ctx", "head"), None),
            P("groups", ("ctx", "head")),
            P(("ctx", "head"), None, None),
            P(("ctx", "head"), None, None),
            P(("ctx", "head"), None),
            P(("groups", "ctx"), None, None),
            P(("groups", "ctx")),
        ),
        out_specs=P("groups", ("ctx", "head")),
        check_vma=False,
    )
```

time: 117 us -> 92.8 us (0.79)
  blocking collectives: 26.6 us -> 0 us
  starting transfers between devices: 12.9 us -> 23 us
  matrix products: 8.46 us -> 0.99 us
  Pallas kernels: 23.7 us -> 20 us
  waiting for transfers between devices: 32.1 us -> 35.7 us
    all_to_all x2 -> x0, blocking collectives: 26.6 us -> none  [the longest x1 13.4 us: body(): lax.all_to_all(pieces, ('ctx', 'head'), split_axis=0, concat_axis=0, tile...]
    all_to_all x1 -> x0, waiting for transfers between devices: 20.3 us -> none  [body(): lax.all_to_all(mean, 'ctx', split_axis=0, concat_axis=0, tiled=True)]
    ppermute x4 -> x8, waiting for transfers between devices: 11.8 us -> 27.1 us  [body(): forward = lax.ppermute(forward, 'ctx', after)]
    ppermute x0 -> x4, waiting for transfers between devices: none -> 8.55 us  [body(): got = lax.ppermute(pieces[half:], axes, pairs)]
    dot_general x2 -> x0, matrix products: 7.47 us -> none  [the longest x1 7.21 us: body(): jnp.dot(head_out.reshape(requests, -1), output_weight, preferred_element_...]
    ppermute x4 -> x8, starting transfers between devices: 8.62 us -> 15.5 us  [body(): forward = lax.ppermute(forward, 'ctx', after)]
    ppermute x0 -> x4, starting transfers between devices: none -> 5.87 us  [body(): got = lax.ppermute(pieces[half:], axes, pairs)]
    pallas_call x1 -> x7, Pallas kernels: 23.7 us -> 20 us  [the longest x1 16 us: attend(): pl.pallas_call(functools.partial(attend_kernel, score_scale, chunks, bloc...]
  transfers between devices with their start and end apart: 8 -> 18, of which waited for: 6 -> 13; matrix products, arithmetic and copies ran while one was open for 2% -> 0% of each run, Pallas kernels for 0% -> 1%
where the time goes in v2:
time: 92.8 us; the launch traced here: 92.6 us
  waiting for transfers between devices  35.7 us (38%)
  starting transfers between devices  23 us (25%)
  Pallas kernels  20 us (22%)
  local copies, waits for them, and re-layouts  12 us (13%)
  matrix products  0.99 us (1%)
    ppermute x8, waiting for transfers between devices, body(): forward = lax.ppermute(forward, 'ctx', after)  27.1 us
    pallas_call x1, Pallas kernels, attend(): pl.pallas_call(functools.partial(attend_kernel, score_scale, chunks, bloc...  16 us
    ppermute x8, starting transfers between devices, body(): forward = lax.ppermute(forward, 'ctx', after)  15.5 us
    unnamed x18, local copies, waits for them, and re-layouts  11.7 us
    ppermute x4, waiting for transfers between devices, body(): got = lax.ppermute(pieces[half:], axes, pairs)  8.55 us
    ppermute x4, starting transfers between devices, body(): got = lax.ppermute(pieces[half:], axes, pairs)  5.87 us
    pallas_call x1, Pallas kernels, finish(): pl.pallas_call(functools.partial(finish_kernel, block_columns), out_shape...  3.3 us
  transfers between devices with their start and end apart: 18, of which 13 were waited for; matrix products, arithmetic and copies ran while one was open for 0% of the time, Pallas kernels for 1%

profile of v2, /device:TPU:0, one launch (start us, length us, event | category | flops | bytes accessed | tf_op | source)
XLA Modules:
  0.0 92.6 jit_solution(645944800667552325)
XLA Ops:
  2.5 3.1 %collective-permute-start = (bf16[16,8,576]{2,1,0:T(8,128)(2,1)S(1)}, bf16[16,8,576]{2,1,0:T(8,128)(2,1)S(1)}, u32[]{:S(2)}, u32[]{:S(2)}) collective-permute-start(bf16[16,8,576]{2,1,0:T(8,128)(2,1)S(1)} %get-tuple-element.23), channel_id=1, source_target_pairs={{0,4},{4,8},{8,12},{12,14},{14,10},{10,6},{6,2},{2,0},{1,5},{5,9},... | collective-permute-start | bytes 442376 | tf_op jit(solution)/shard_map/ppermute | solution.py:317
  5.6 4.1 %collective-permute-done = bf16[16,8,576]{2,1,0:T(8,128)(2,1)S(1)} collective-permute-done((bf16[16,8,576]{2,1,0:T(8,128)(2,1)S(1)}, bf16[16,8,576]{2,1,0:T(8,128)(2,1)S(1)}, u32[]{:S(2)}, u32[]{:S(2)}) %collective-permute-start) | collective-permute-done | bytes 147488 | tf_op jit(solution)/shard_map/ppermute | solution.py:317
  9.7 1.8 %collective-permute-start.2 = (bf16[16,8,576]{2,1,0:T(8,128)(2,1)S(1)}, bf16[16,8,576]{2,1,0:T(8,128)(2,1)S(1)}, u32[]{:S(2)}, u32[]{:S(2)}) collective-permute-start(bf16[16,8,576]{2,1,0:T(8,128)(2,1)S(1)} %collective-permute-done), channel_id=1, source_target_pairs={{0,4},{4,8},{8,12},{12,14},{14,10},{10,6},{6,2},{2,0},{1,5},{5,9},... | collective-permute-start | bytes 442376 | tf_op jit(solution)/shard_map/ppermute | solution.py:317
  11.8 3.2 %collective-permute-done.2 = bf16[16,8,576]{2,1,0:T(8,128)(2,1)S(1)} collective-permute-done((bf16[16,8,576]{2,1,0:T(8,128)(2,1)S(1)}, bf16[16,8,576]{2,1,0:T(8,128)(2,1)S(1)}, u32[]{:S(2)}, u32[]{:S(2)}) %collective-permute-start.2) | collective-permute-done | bytes 147488 | tf_op jit(solution)/shard_map/ppermute | solution.py:317
  15.1 1.7 %collective-permute-start.4 = (bf16[16,8,576]{2,1,0:T(8,128)(2,1)S(1)}, bf16[16,8,576]{2,1,0:T(8,128)(2,1)S(1)}, u32[]{:S(2)}, u32[]{:S(2)}) collective-permute-start(bf16[16,8,576]{2,1,0:T(8,128)(2,1)S(1)} %collective-permute-done.2), channel_id=1, source_target_pairs={{0,4},{4,8},{8,12},{12,14},{14,10},{10,6},{6,2},{2,0},{1,5},{5,9},... | collective-permute-start | bytes 442376 | tf_op jit(solution)/shard_map/ppermute | solution.py:317
  17.2 3.6 %collective-permute-done.4 = bf16[16,8,576]{2,1,0:T(8,128)(2,1)S(1)} collective-permute-done((bf16[16,8,576]{2,1,0:T(8,128)(2,1)S(1)}, bf16[16,8,576]{2,1,0:T(8,128)(2,1)S(1)}, u32[]{:S(2)}, u32[]{:S(2)}) %collective-permute-start.4) | collective-permute-done | bytes 147488 | tf_op jit(solution)/shard_map/ppermute | solution.py:317
  20.9 2.0 %collective-permute-start.6 = (bf16[16,8,576]{2,1,0:T(8,128)(2,1)S(1)}, bf16[16,8,576]{2,1,0:T(8,128)(2,1)S(1)}, u32[]{:S(2)}, u32[]{:S(2)}) collective-permute-start(bf16[16,8,576]{2,1,0:T(8,128)(2,1)S(1)} %collective-permute-done.4), channel_id=1, source_target_pairs={{0,4},{4,8},{8,12},{12,14},{14,10},{10,6},{6,2},{2,0},{1,5},{5,9},... | collective-permute-start | bytes 442376 | tf_op jit(solution)/shard_map/ppermute | solution.py:317
  22.9 3.2 %collective-permute-done.6 = bf16[16,8,576]{2,1,0:T(8,128)(2,1)S(1)} collective-permute-done((bf16[16,8,576]{2,1,0:T(8,128)(2,1)S(1)}, bf16[16,8,576]{2,1,0:T(8,128)(2,1)S(1)}, u32[]{:S(2)}, u32[]{:S(2)}) %collective-permute-start.6) | collective-permute-done | bytes 147488 | tf_op jit(solution)/shard_map/ppermute | solution.py:317
  26.2 16.0 %attend.1 = (bf16[17,8,512]{2,1,0:T(8,128)(2,1)S(1)}, bf16[17,8,512]{2,1,0:T(8,128)(2,1)S(1)}, bf16[17,8,512]{2,1,0:T(8,128)(2,1)S(1)}, bf16[17,8,512]{2,1,0:T(8...) custom-call(s32[224]{0:T(256)S(1)} %copy-done.4, ...), custom_call_target="tpu_custom_call" | custom-call | flops 7985954816 | bytes 16515072 | tf_op jit(solution)/shard_map/attend/pallas_call | solution.py:176
  42.2 5.2 %copy-done.1 = bf16[1024,7168]{1,0:T(8,128)(2,1)} copy-done((bf16[1024,7168]{1,0:T(8,128)(2,1)}, bf16[1024,7168]{1,0:T(8,128)(2,1)S(1)}, u32[]{:S(2)}) %copy-start.1) | copy-done | bytes 14680088
  47.4 2.0 %collective-permute-start.7 = (bf16[17,8,512]{2,1,0:T(8,128)(2,1)S(1)}, bf16[17,8,512]{2,1,0:T(8,128)(2,1)S(1)}, u32[]{:S(2)}, u32[]{:S(2)}) collective-permute-start(bf16[17,8,512]{2,1,0:T(8,128)(2,1)S(1)} %get-tuple-element.18), channel_id=1, source_target_pairs={{0,4},{4,8},{8,12},{12,14},{14,10},{10,6},{6,2},{2,0},{1,5},{5,9},... | collective-permute-start | bytes 417800 | tf_op jit(solution)/shard_map/ppermute | solution.py:334
  49.4 3.7 %collective-permute-done.7.got_ref = bf16[17,8,512]{2,1,0:T(8,128)(2,1)S(1)} collective-permute-done((bf16[17,8,512]{2,1,0:T(8,128)(2,1)S(1)}, bf16[17,8,512]{2,1,0:T(8,128)(2,1)S(1)}, u32[]{:S(2)}, u32[]{:S(2)}) %collective-permute-start.7) | collective-permute-done | bytes 139296 | tf_op jit(solution)/shard_map/ppermute | solution.py:334
  55.6 2.8 %collective-permute-done.8.got_ref = bf16[17,8,512]{2,1,0:T(8,128)(2,1)S(1)} collective-permute-done((bf16[17,8,512]{2,1,0:T(8,128)(2,1)S(1)}, bf16[17,8,512]{2,1,0:T(8,128)(2,1)S(1)}, u32[]{:S(2)}, u32[]{:S(2)}) %collective-permute-start.8) | collective-permute-done | bytes 139296 | tf_op jit(solution)/shard_map/ppermute | solution.py:334
  58.6 1.6 %collective-permute-start.9 = (bf16[17,8,512]{2,1,0:T(8,128)(2,1)S(1)}, bf16[17,8,512]{2,1,0:T(8,128)(2,1)S(1)}, u32[]{:S(2)}, u32[]{:S(2)}) collective-permute-start(bf16[17,8,512]{2,1,0:T(8,128)(2,1)S(1)} %merge.6), channel_id=1, source_target_pairs={{0,4},{4,8},{8,12},{12,14},{14,10},{10,6},{6,2},{2,0},{1,5},{5,9},... | collective-permute-start | bytes 417800 | tf_op jit(solution)/shard_map/ppermute | solution.py:334
  60.8 2.8 %collective-permute-done.9.got_ref = bf16[17,8,512]{2,1,0:T(8,128)(2,1)S(1)} collective-permute-done((bf16[17,8,512]{2,1,0:T(8,128)(2,1)S(1)}, bf16[17,8,512]{2,1,0:T(8,128)(2,1)S(1)}, u32[]{:S(2)}, u32[]{:S(2)}) %collective-permute-start.9) | collective-permute-done | bytes 139296 | tf_op jit(solution)/shard_map/ppermute | solution.py:334
  63.8 1.6 %collective-permute-start.10 = (bf16[17,8,512]{2,1,0:T(8,128)(2,1)S(1)}, bf16[17,8,512]{2,1,0:T(8,128)(2,1)S(1)}, u32[]{:S(2)}, u32[]{:S(2)}) collective-permute-start(bf16[17,8,512]{2,1,0:T(8,128)(2,1)S(1)} %merge.7), channel_id=1, source_target_pairs={{0,4},{4,8},{8,12},{12,14},{14,10},{10,6},{6,2},{2,0},{1,5},{5,9},... | collective-permute-start | bytes 417800 | tf_op jit(solution)/shard_map/ppermute | solution.py:334
  65.5 3.5 %collective-permute-done.10.forward_ref = bf16[17,8,512]{2,1,0:T(8,128)(2,1)S(1)} collective-permute-done((bf16[17,8,512]{2,1,0:T(8,128)(2,1)S(1)}, bf16[17,8,512]{2,1,0:T(8,128)(2,1)S(1)}, u32[]{:S(2)}, u32[]{:S(2)}) %collective-permute-start.10) | collective-permute-done | bytes 139296 | tf_op jit(solution)/shard_map/ppermute | solution.py:334
  68.9 5.2 %copy-done.2 = bf16[1024,7168]{1,0:T(8,128)(2,1)S(1)} copy-done((bf16[1024,7168]{1,0:T(8,128)(2,1)S(1)}, bf16[1024,7168]{1,0:T(8,128)(2,1)}, u32[]{:S(2)}) %copy-start.2) | copy-done | bytes 14680088
  74.1 3.3 %finish.1 = bf16[16,16,448]{2,1,0:T(8,128)(2,1)S(1)} custom-call(s32[1]{0:T(128)} %bitcast.here_ref, bf16[17,8,512]{2,1,0:T(8,128)(2,1)S(1)} %get-tuple-element.14.own_ref, bf16[17,8,512]{2,1,0:T(8,128)(2,1)S(1)} %collective-permute-done.10.forward_ref, bf16[17,8,512]{2,1,0:T(8,128)(2,1)S(1)} %collective-permute-done.13.backward_ref, ...), custom_call_target="tpu_custom_call" | custom-call | flops 3758096384 | tf_op jit(solution)/shard_map/finish/pallas_call | solution.py:280
  80.4 2.9 %collective-permute-done.15 = bf16[4,16,448]{2,1,0:T(8,128)(2,1)S(1)} collective-permute-done((bf16[4,16,448]{2,1,0:T(8,128)(2,1)S(1)}, bf16[4,16,448]{2,1,0:T(8,128)(2,1)S(1)}, u32[]{:S(2)}, u32[]{:S(2)}) %collective-permute-start.15) | collective-permute-done | bytes 57376 | tf_op jit(solution)/shard_map/ppermute | solution.py:350
  83.3 1.7 %collective-permute-start.16 = (bf16[2,16,448]{2,1,0:T(8,128)(2,1)S(1)}, bf16[2,16,448]{2,1,0:T(8,128)(2,1)S(1)}, u32[]{:S(2)}, u32[]{:S(2)}) collective-permute-start(bf16[2,16,448]{2,1,0:T(8,128)(2,1)S(1)} %slice.37), channel_id=1, source_target_pairs={{0,4},{1,5},{2,6},{3,7},{4,0},{5,1},{6,2},{7,3},{8,12},{9,13},{10,... | collective-permute-start | bytes 86024 | tf_op jit(solution)/shard_map/ppermute | solution.py:350
  84.9 2.3 %collective-permute-done.16 = bf16[2,16,448]{2,1,0:T(8,128)(2,1)S(1)} collective-permute-done((bf16[2,16,448]{2,1,0:T(8,128)(2,1)S(1)}, bf16[2,16,448]{2,1,0:T(8,128)(2,1)S(1)}, u32[]{:S(2)}, u32[]{:S(2)}) %collective-permute-start.16) | collective-permute-done | bytes 28704 | tf_op jit(solution)/shard_map/ppermute | solution.py:350
  87.3 2.7 %collective-permute-start.17 = (bf16[1,16,448]{2,1,0:T(8,128)(2,1)S(1)}, bf16[1,16,448]{2,1,0:T(8,128)(2,1)S(1)}, u32[]{:S(2)}, u32[]{:S(2)}) collective-permute-start(bf16[1,16,448]{2,1,0:T(8,128)(2,1)S(1)} %slice.39), channel_id=1, source_target_pairs={{0,8},{1,9},{2,10},{3,11},{4,12},{5,13},{6,14},{7,15},{8,0},{9,1},... | collective-permute-start | bytes 43016 | tf_op jit(solution)/shard_map/ppermute | solution.py:350
  90.0 2.0 %collective-permute-done.17 = bf16[1,16,448]{2,1,0:T(8,128)(2,1)S(1)} collective-permute-done((bf16[1,16,448]{2,1,0:T(8,128)(2,1)S(1)}, bf16[1,16,448]{2,1,0:T(8,128)(2,1)S(1)}, u32[]{:S(2)}, u32[]{:S(2)}) %collective-permute-start.17) | collective-permute-done | bytes 14368 | tf_op jit(solution)/shard_map/ppermute | solution.py:350
  (50 shorter events, 10.2 us)
Async XLA Ops:
  0.0 1.2 %copy-start = (bf16[8,128,512]{2,1,0:T(8,128)(2,1)S(1)}, bf16[8,128,512]{2,1,0:T(8,128)(2,1)}, u32[]{:S(2)}) copy-start(bf16[8,128,512]{2,1,0:T(8,128)(2,1)} %param.9) | copy-start | bytes 3145732
  0.0 2.3 %copy-start.5 = (bf16[16,512]{1,0:T(8,128)(2,1)S(1)}, bf16[16,512]{1,0:T(8,128)(2,1)}, u32[]{:S(2)}) copy-start(bf16[16,512]{1,0:T(8,128)(2,1)} %param.8) | copy-start | bytes 49156
  2.4 23.8 %copy-start.4 = (s32[224]{0:T(256)S(1)}, s32[224]{0:T(256)}, u32[]{:S(2)}) copy-start(s32[224]{0:T(256)} %owner_ref.1) | copy-start | bytes 2692
  2.5 7.2 %collective-permute-start = (bf16[16,8,576]{2,1,0:T(8,128)(2,1)S(1)}, bf16[16,8,576]{2,1,0:T(8,128)(2,1)S(1)}, u32[]{:S(2)}, u32[]{:S(2)}) collective-permute-start(bf16[16,8,576]{2,1,0:T(8,128)(2,1)S(1)} %get-tuple-element.23), channel_id=1, source_target_pairs={{0,4},{4,8},{8,12},{12,14},{14,10},{10,6},{6,2},{2,0},{1,5},{5,9},... | collective-permute-start | bytes 442376 | tf_op jit(solution)/shard_map/ppermute | solution.py:317
  5.5 6.0 %collective-permute-start.1 = (bf16[16,8,576]{2,1,0:T(8,128)(2,1)S(1)}, bf16[16,8,576]{2,1,0:T(8,128)(2,1)S(1)}, u32[]{:S(2)}, u32[]{:S(2)}) collective-permute-start(bf16[16,8,576]{2,1,0:T(8,128)(2,1)S(1)} %get-tuple-element.23), channel_id=1, source_target_pairs={{4,0},{8,4},{12,8},{14,12},{10,14},{6,10},{2,6},{0,2},{5,1},{9,5},... | collective-permute-start | bytes 442376 | tf_op jit(solution)/shard_map/ppermute | solution.py:321
  9.7 5.4 %collective-permute-start.2 = (bf16[16,8,576]{2,1,0:T(8,128)(2,1)S(1)}, bf16[16,8,576]{2,1,0:T(8,128)(2,1)S(1)}, u32[]{:S(2)}, u32[]{:S(2)}) collective-permute-start(bf16[16,8,576]{2,1,0:T(8,128)(2,1)S(1)} %collective-permute-done), channel_id=1, source_target_pairs={{0,4},{4,8},{8,12},{12,14},{14,10},{10,6},{6,2},{2,0},{1,5},{5,9},... | collective-permute-start | bytes 442376 | tf_op jit(solution)/shard_map/ppermute | solution.py:317
  11.5 5.4 %collective-permute-start.3 = (bf16[16,8,576]{2,1,0:T(8,128)(2,1)S(1)}, bf16[16,8,576]{2,1,0:T(8,128)(2,1)S(1)}, u32[]{:S(2)}, u32[]{:S(2)}) collective-permute-start(bf16[16,8,576]{2,1,0:T(8,128)(2,1)S(1)} %collective-permute-done.1), channel_id=1, source_target_pairs={{4,0},{8,4},{12,8},{14,12},{10,14},{6,10},{2,6},{0,2},{5,1},{9,5},... | collective-permute-start | bytes 442376 | tf_op jit(solution)/shard_map/ppermute | solution.py:321
  15.1 5.8 %collective-permute-start.4 = (bf16[16,8,576]{2,1,0:T(8,128)(2,1)S(1)}, bf16[16,8,576]{2,1,0:T(8,128)(2,1)S(1)}, u32[]{:S(2)}, u32[]{:S(2)}) collective-permute-start(bf16[16,8,576]{2,1,0:T(8,128)(2,1)S(1)} %collective-permute-done.2), channel_id=1, source_target_pairs={{0,4},{4,8},{8,12},{12,14},{14,10},{10,6},{6,2},{2,0},{1,5},{5,9},... | collective-permute-start | bytes 442376 | tf_op jit(solution)/shard_map/ppermute | solution.py:317
  16.9 6.0 %collective-permute-start.5 = (bf16[16,8,576]{2,1,0:T(8,128)(2,1)S(1)}, bf16[16,8,576]{2,1,0:T(8,128)(2,1)S(1)}, u32[]{:S(2)}, u32[]{:S(2)}) collective-permute-start(bf16[16,8,576]{2,1,0:T(8,128)(2,1)S(1)} %collective-permute-done.3), channel_id=1, source_target_pairs={{4,0},{8,4},{12,8},{14,12},{10,14},{6,10},{2,6},{0,2},{5,1},{9,5},... | collective-permute-start | bytes 442376 | tf_op jit(solution)/shard_map/ppermute | solution.py:321
  20.9 5.3 %collective-permute-start.6 = (bf16[16,8,576]{2,1,0:T(8,128)(2,1)S(1)}, bf16[16,8,576]{2,1,0:T(8,128)(2,1)S(1)}, u32[]{:S(2)}, u32[]{:S(2)}) collective-permute-start(bf16[16,8,576]{2,1,0:T(8,128)(2,1)S(1)} %collective-permute-done.4), channel_id=1, source_target_pairs={{0,4},{4,8},{8,12},{12,14},{14,10},{10,6},{6,2},{2,0},{1,5},{5,9},... | collective-permute-start | bytes 442376 | tf_op jit(solution)/shard_map/ppermute | solution.py:317
  42.2 5.2 %copy-start.1 = (bf16[1024,7168]{1,0:T(8,128)(2,1)}, bf16[1024,7168]{1,0:T(8,128)(2,1)S(1)}, u32[]{:S(2)}) copy-start(bf16[1024,7168]{1,0:T(8,128)(2,1)S(1)} %get-tuple-element.22.weight_ref) | copy-start | bytes 44040196
  47.4 21.5 %copy-start.3 = (bf16[8,512,128]{2,1,0:T(8,128)(2,1)S(1)}, bf16[8,512,128]{2,1,0:T(8,128)(2,1)}, u32[]{:S(2)}) copy-start(bf16[8,512,128]{2,1,0:T(8,128)(2,1)} %value_ref.1) | copy-start | bytes 3145732
  47.4 5.8 %collective-permute-start.7 = (bf16[17,8,512]{2,1,0:T(8,128)(2,1)S(1)}, bf16[17,8,512]{2,1,0:T(8,128)(2,1)S(1)}, u32[]{:S(2)}, u32[]{:S(2)}) collective-permute-start(bf16[17,8,512]{2,1,0:T(8,128)(2,1)S(1)} %get-tuple-element.18), channel_id=1, source_target_pairs={{0,4},{4,8},{8,12},{12,14},{14,10},{10,6},{6,2},{2,0},{1,5},{5,9},... | collective-permute-start | bytes 417800 | tf_op jit(solution)/shard_map/ppermute | solution.py:334
  49.4 5.6 %collective-permute-start.11 = (bf16[17,8,512]{2,1,0:T(8,128)(2,1)S(1)}, bf16[17,8,512]{2,1,0:T(8,128)(2,1)S(1)}, u32[]{:S(2)}, u32[]{:S(2)}) collective-permute-start(bf16[17,8,512]{2,1,0:T(8,128)(2,1)S(1)} %get-tuple-element.21), channel_id=1, source_target_pairs={{4,0},{8,4},{12,8},{14,12},{10,14},{6,10},{2,6},{0,2},{5,1},{9,5},... | collective-permute-start | bytes 417800 | tf_op jit(solution)/shard_map/ppermute | solution.py:336
  53.3 5.1 %collective-permute-start.8 = (bf16[17,8,512]{2,1,0:T(8,128)(2,1)S(1)}, bf16[17,8,512]{2,1,0:T(8,128)(2,1)S(1)}, u32[]{:S(2)}, u32[]{:S(2)}) collective-permute-start(bf16[17,8,512]{2,1,0:T(8,128)(2,1)S(1)} %merge.5), channel_id=1, source_target_pairs={{0,4},{4,8},{8,12},{12,14},{14,10},{10,6},{6,2},{2,0},{1,5},{5,9},... | collective-permute-start | bytes 417800 | tf_op jit(solution)/shard_map/ppermute | solution.py:334
  55.1 5.1 %collective-permute-start.12 = (bf16[17,8,512]{2,1,0:T(8,128)(2,1)S(1)}, bf16[17,8,512]{2,1,0:T(8,128)(2,1)S(1)}, u32[]{:S(2)}, u32[]{:S(2)}) collective-permute-start(bf16[17,8,512]{2,1,0:T(8,128)(2,1)S(1)} %merge.8), channel_id=1, source_target_pairs={{4,0},{8,4},{12,8},{14,12},{10,14},{6,10},{2,6},{0,2},{5,1},{9,5},... | collective-permute-start | bytes 417800 | tf_op jit(solution)/shard_map/ppermute | solution.py:336
  58.6 5.1 %collective-permute-start.9 = (bf16[17,8,512]{2,1,0:T(8,128)(2,1)S(1)}, bf16[17,8,512]{2,1,0:T(8,128)(2,1)S(1)}, u32[]{:S(2)}, u32[]{:S(2)}) collective-permute-start(bf16[17,8,512]{2,1,0:T(8,128)(2,1)S(1)} %merge.6), channel_id=1, source_target_pairs={{0,4},{4,8},{8,12},{12,14},{14,10},{10,6},{6,2},{2,0},{1,5},{5,9},... | collective-permute-start | bytes 417800 | tf_op jit(solution)/shard_map/ppermute | solution.py:334
  60.4 5.1 %collective-permute-start.13 = (bf16[17,8,512]{2,1,0:T(8,128)(2,1)S(1)}, bf16[17,8,512]{2,1,0:T(8,128)(2,1)S(1)}, u32[]{:S(2)}, u32[]{:S(2)}) collective-permute-start(bf16[17,8,512]{2,1,0:T(8,128)(2,1)S(1)} %merge.9), channel_id=1, source_target_pairs={{4,0},{8,4},{12,8},{14,12},{10,14},{6,10},{2,6},{0,2},{5,1},{9,5},... | collective-permute-start | bytes 417800 | tf_op jit(solution)/shard_map/ppermute | solution.py:336
  63.8 5.1 %collective-permute-start.10 = (bf16[17,8,512]{2,1,0:T(8,128)(2,1)S(1)}, bf16[17,8,512]{2,1,0:T(8,128)(2,1)S(1)}, u32[]{:S(2)}, u32[]{:S(2)}) collective-permute-start(bf16[17,8,512]{2,1,0:T(8,128)(2,1)S(1)} %merge.7), channel_id=1, source_target_pairs={{0,4},{4,8},{8,12},{12,14},{14,10},{10,6},{6,2},{2,0},{1,5},{5,9},... | collective-permute-start | bytes 417800 | tf_op jit(solution)/shard_map/ppermute | solution.py:334
  68.9 5.2 %copy-start.2 = (bf16[1024,7168]{1,0:T(8,128)(2,1)S(1)}, bf16[1024,7168]{1,0:T(8,128)(2,1)}, u32[]{:S(2)}) copy-start(bf16[1024,7168]{1,0:T(8,128)(2,1)} %copy-done.1) | copy-start | bytes 44040196
  77.4 1.4 %collective-permute-start.14 = (bf16[8,16,448]{2,1,0:T(8,128)(2,1)S(1)}, bf16[8,16,448]{2,1,0:T(8,128)(2,1)S(1)}, u32[]{:S(2)}, u32[]{:S(2)}) collective-permute-start(bf16[8,16,448]{2,1,0:T(8,128)(2,1)S(1)} %slice.33), channel_id=1, source_target_pairs={{0,1},{1,0},{2,3},{3,2},{4,5},{5,4},{6,7},{7,6},{8,9},{9,8},{10,11... | collective-permute-start | bytes 344072 | tf_op jit(solution)/shard_map/ppermute | solution.py:350
  78.9 4.3 %collective-permute-start.15 = (bf16[4,16,448]{2,1,0:T(8,128)(2,1)S(1)}, bf16[4,16,448]{2,1,0:T(8,128)(2,1)S(1)}, u32[]{:S(2)}, u32[]{:S(2)}) collective-permute-start(bf16[4,16,448]{2,1,0:T(8,128)(2,1)S(1)} %slice.35), channel_id=1, source_target_pairs={{0,2},{1,3},{2,0},{3,1},{4,6},{5,7},{6,4},{7,5},{8,10},{9,11},{10,... | collective-permute-start | bytes 172040 | tf_op jit(solution)/shard_map/ppermute | solution.py:350
  83.3 4.0 %collective-permute-start.16 = (bf16[2,16,448]{2,1,0:T(8,128)(2,1)S(1)}, bf16[2,16,448]{2,1,0:T(8,128)(2,1)S(1)}, u32[]{:S(2)}, u32[]{:S(2)}) collective-permute-start(bf16[2,16,448]{2,1,0:T(8,128)(2,1)S(1)} %slice.37), channel_id=1, source_target_pairs={{0,4},{1,5},{2,6},{3,7},{4,0},{5,1},{6,2},{7,3},{8,12},{9,13},{10,... | collective-permute-start | bytes 86024 | tf_op jit(solution)/shard_map/ppermute | solution.py:350
  87.3 4.7 %collective-permute-start.17 = (bf16[1,16,448]{2,1,0:T(8,128)(2,1)S(1)}, bf16[1,16,448]{2,1,0:T(8,128)(2,1)S(1)}, u32[]{:S(2)}, u32[]{:S(2)}) collective-permute-start(bf16[1,16,448]{2,1,0:T(8,128)(2,1)S(1)} %slice.39), channel_id=1, source_target_pairs={{0,8},{1,9},{2,10},{3,11},{4,12},{5,13},{6,14},{7,15},{8,0},{9,1},... | collective-permute-start | bytes 43016 | tf_op jit(solution)/shard_map/ppermute | solution.py:350

commit v3 on v2

--- a/solution.py
+++ b/solution.py
@@ -46,11 +46,11 @@
     return (parts[0] + parts[1]) + parts[2]
 
 
-def attend_kernel(score_scale, chunks, blocks, owner_ref, query_ref, cache_ref, weight_ref, *refs):
-    message_refs = refs[:blocks]
+def attend_kernel(score_scale, chunks, parts, owner_ref, query_ref, cache_ref, weight_ref, *refs):
+    message_refs = refs[: len(parts)]
     (
         weight_out, cache_scr, score_scr, max_scr, total_scr, sum_scr, cache_sem, weight_sem
-    ) = refs[blocks:]
+    ) = refs[len(parts) :]
     requests, heads, entry_size = query_ref.shape
     pages, page_len, _ = cache_ref.shape
     _, heads_here, latent_size = message_refs[0].shape
@@ -157,31 +157,33 @@
         mean = (sum_scr[r] * (1.0 / safe)).astype(jnp.bfloat16)
         level = jnp.where(present, max_scr[r][:, :1] + jnp.log(safe), masked_score)
         stats = jnp.where(lane == r, level, stats)
-        for b in range(blocks):
-            message_refs[b][r] = mean[b * heads_here : (b + 1) * heads_here]
-    for b in range(blocks):
-        message_refs[b][requests] = jnp.zeros((heads_here, latent_size), jnp.bfloat16)
-        store_level(message_refs[b], requests, stats[b * heads_here : (b + 1) * heads_here])
+        for ref, (block, low, high) in zip(message_refs, parts):
+            if low <= r < high:
+                ref[r - low] = mean[block * heads_here : (block + 1) * heads_here]
+    for ref, (block, low, high) in zip(message_refs, parts):
+        ref[high - low] = jnp.zeros((heads_here, latent_size), jnp.bfloat16)
+        level = jnp.where((lane >= low) & (lane < high), stats, masked_score)
+        store_level(ref, high - low, level[block * heads_here : (block + 1) * heads_here])
     weight_copy.wait()
 
 
-def attend(query_full, latent_cache, page_owner, output_weight, score_scale, latent_size, blocks):
+def attend(query_full, latent_cache, page_owner, output_weight, score_scale, latent_size, blocks, parts):
     requests, heads, entry_size = query_full.shape
     pages, page_len, _ = latent_cache.shape
     heads_here = heads // blocks
     pair_len = 2 * page_len
     groups = pages // GROUP_PAGES
-    chunks = groups // max(d for d in range(1, 9) if groups % d == 0)
+    chunks = groups // max(d for d in range(1, 15) if groups % d == 0)
     any_spec = pl.BlockSpec(memory_space=pl.ANY)
     out = pl.pallas_call(
-        functools.partial(attend_kernel, score_scale, chunks, blocks),
+        functools.partial(attend_kernel, score_scale, chunks, parts),
         out_shape=[
-            pltpu.VMEM((requests + 1, heads_here, latent_size), jnp.bfloat16)
-            for _ in range(blocks)
+            pltpu.VMEM((high - low + 1, heads_here, latent_size), jnp.bfloat16)
+            for _, low, high in parts
         ]
         + [pltpu.VMEM(output_weight.shape, output_weight.dtype)],
         in_specs=[SMEM_SPEC, VMEM_SPEC, any_spec, any_spec],
-        out_specs=[VMEM_SPEC] * (blocks + 1),
+        out_specs=[VMEM_SPEC] * (len(parts) + 1),
         scratch_shapes=[
             pltpu.VMEM(latent_cache.shape, latent_cache.dtype),
             pltpu.VMEM((pages // 2, heads, pair_len), jnp.float32),
@@ -199,7 +201,7 @@
         ),
         name="attend",
     )(page_owner, in_vmem(query_full), latent_cache, output_weight)
-    return out[:blocks], out[blocks]
+    return out[:-1], out[-1]
 
 
 def shares(levels):
@@ -209,31 +211,35 @@
     return [part / total for part in parts], top + jnp.log(total)
 
 
-def merge_kernel(own_ref, got_ref, out_ref):
-    requests = own_ref.shape[0] - 1
-    both = (own_ref, got_ref)
-    weights, level = shares([load_level(ref, requests) for ref in both])
+def merge_kernel(first, own_ref, got_ref, out_ref):
+    requests, got_rows = own_ref.shape[0] - 1, got_ref.shape[0] - 1
+    weights, level = shares([load_level(own_ref, requests), load_level(got_ref, got_rows)])
     for r in range(requests):
+        if not 0 <= r - first < got_rows:
+            out_ref[r] = own_ref[r]
+            continue
         out_ref[r] = sum(
-            w[:, r : r + 1] * ref[r].astype(jnp.float32) for w, ref in zip(weights, both)
+            w[:, r : r + 1] * rows.astype(jnp.float32)
+            for w, rows in zip(weights, (own_ref[r], got_ref[r - first]))
         ).astype(jnp.bfloat16)
     out_ref[requests] = jnp.zeros(out_ref.shape[1:], jnp.bfloat16)
     store_level(out_ref, requests, level)
 
 
-def merge(own, got):
+def merge(own, got, first=0):
     return pl.pallas_call(
-        merge_kernel,
+        functools.partial(merge_kernel, first),
         out_shape=pltpu.VMEM(own.shape, own.dtype),
         in_specs=[VMEM_SPEC] * 2,
         out_specs=VMEM_SPEC,
+        compiler_params=pltpu.CompilerParams(vmem_limit_bytes=2 * MIB),
         cost_estimate=pl.CostEstimate(flops=4 * own.size, bytes_accessed=0, transcendentals=0),
         name="merge",
     )(in_vmem(own), in_vmem(got))
 
 
 def finish_kernel(
-    block_columns, here_ref, own_ref, forward_ref, backward_ref, value_ref, weight_ref, out_ref,
+    block_columns, radices, here_ref, own_ref, forward_ref, backward_ref, value_ref, weight_ref, out_ref,
     attended_scr, head_scr,
 ):
     requests, heads_here = own_ref.shape[0] - 1, own_ref.shape[1]
@@ -256,7 +262,6 @@
         ).astype(jnp.bfloat16)
     head_out = head_scr[...]
     per_block = block_columns // width
-    bits = owners.bit_length() - 1
     for j in range(owners // per_block):
         product = jnp.dot(
             head_out,
@@ -265,20 +270,24 @@
         ).astype(jnp.bfloat16)
         for i in range(per_block):
             distance = here_ref[0] ^ (j * per_block + i)
-            place = sum(((distance >> b) & 1) << (bits - 1 - b) for b in range(bits))
+            place = 0
+            for radix in radices:
+                place = place * radix + (distance & (radix - 1))
+                distance = distance >> (radix.bit_length() - 1)
             out_ref[place] = product[:, i * width : (i + 1) * width]
 
 
-def finish(here, own, forward, backward, value_absorb, weight, owners):
+def finish(here, own, forward, backward, value_absorb, weight, radices):
     requests, heads_here = own.shape[0] - 1, own.shape[1]
     latent_size, value_size = value_absorb.shape[1:]
     depth, columns = weight.shape
+    owners = functools.reduce(lambda a, b: a * b, radices)
     width = columns // owners
     block_columns = width
     while block_columns % LANES:
         block_columns *= 2
     return pl.pallas_call(
-        functools.partial(finish_kernel, block_columns),
+        functools.partial(finish_kernel, block_columns, radices),
         out_shape=pltpu.VMEM((owners, requests, width), jnp.bfloat16),
         in_specs=[SMEM_SPEC] + [VMEM_SPEC] * 5,
         out_specs=VMEM_SPEC,
@@ -302,56 +311,80 @@
     rope_size = query_rope.shape[1] // heads_here
     score_scale = (nope_size + rope_size) ** (-0.5)
     count = len(ring)
+    steps, half = count // 2, requests // 2
     query_latent = jnp.einsum(
         "rhn,hnl->rhl", query_nope, key_absorb, preferred_element_type=jnp.float32
     ).astype(jnp.bfloat16)
     own = jnp.concatenate(
-        [query_latent, query_rope.reshape(requests, heads_here, rope_size)], axis=2
+        [query_latent, query_rope.reshape(-1, heads_here, latent_size)], axis=0
     )
 
     after = [(ring[i], ring[(i + 1) % count]) for i in range(count)]
     before = [(b, a) for a, b in after]
+    middle = own.shape[0] // 2
     blocks, offsets = [own], [0]
     forward = backward = own
-    for step in range(1, count // 2 + 1):
+    for step in range(1, steps):
         forward = lax.ppermute(forward, "ctx", after)
-        blocks.append(forward)
-        offsets.append(-step)
-        if 2 * step < count:
-            backward = lax.ppermute(backward, "ctx", before)
-            blocks.append(backward)
-            offsets.append(step)
-    query_full = jnp.concatenate(blocks, axis=1)
-
+        backward = lax.ppermute(backward, "ctx", before)
+        blocks += [forward, backward]
+        offsets += [-step, step]
+    far = [
+        lax.ppermute(forward[:middle], "ctx", after),
+        lax.ppermute(backward[middle:], "ctx", before),
+    ]
+    blocks.append(jnp.concatenate(far, axis=0))
+    offsets.append(steps)
+    query_full = jnp.concatenate(
+        [
+            jnp.concatenate(
+                [
+                    block[:requests],
+                    block[requests:].reshape(requests, heads_here, rope_size),
+                ],
+                axis=2,
+            )
+            for block in blocks
+        ],
+        axis=1,
+    )
+
+    parts = [(b, 0, requests) for b in range(count - 1)]
+    parts += [(count - 1, 0, half), (count - 1, half, requests)]
     messages, weight = attend(
-        query_full, latent_cache, page_owner, output_weight, score_scale, latent_size, count
+        query_full, latent_cache, page_owner, output_weight, score_scale, latent_size, count, parts
     )
-    message_to = {offset % count: message for offset, message in zip(offsets, messages)}
-
-    forward_steps, backward_steps = count // 2, (count - 1) // 2
-    forward, backward = message_to[forward_steps], message_to[-backward_steps % count]
-    for step in range(1, forward_steps + 1):
+    message_to = dict(zip(offsets[:-1], messages))
+
+    forward, backward = messages[-2:]
+    for step in range(1, steps + 1):
         forward = lax.ppermute(forward, "ctx", after)
-        if step <= backward_steps:
-            backward = lax.ppermute(backward, "ctx", before)
-        if step < forward_steps:
-            forward = merge(message_to[forward_steps - step], forward)
-        if step < backward_steps:
-            backward = merge(message_to[(step - backward_steps) % count], backward)
+        backward = lax.ppermute(backward, "ctx", before)
+        if step < steps:
+            forward = merge(message_to[steps - step], forward)
+            backward = merge(message_to[step - steps], backward, half if step == 1 else 0)
 
     axes = ("ctx", "head")
     owners = lax.axis_size(axes)
+    radices = []
+    while functools.reduce(lambda a, b: a * b, radices, 1) < owners:
+        left = owners // functools.reduce(lambda a, b: a * b, radices, 1)
+        radices.append(4 if left % 4 == 0 else 2)
     here = lax.axis_index(axes).astype(jnp.int32).reshape(1)
-    pieces = finish(here, message_to[0], forward, backward, value_absorb, weight, owners)
-    distance = 1
-    while distance < owners:
-        pairs = [(i, i ^ distance) for i in range(owners)]
-        half = pieces.shape[0] // 2
-        got = lax.ppermute(pieces[half:], axes, pairs)
-        pieces = (pieces[:half].astype(jnp.float32) + got.astype(jnp.float32)).astype(
-            jnp.bfloat16
-        )
-        distance *= 2
+    pieces = finish(here, message_to[0], forward, backward, value_absorb, weight, radices)
+    unit = 1
+    for radix in radices:
+        share = pieces.shape[0] // radix
+        got = [
+            lax.ppermute(
+                pieces[k * share : (k + 1) * share],
+                axes,
+                [(i, i ^ (k * unit)) for i in range(owners)],
+            )
+            for k in range(1, radix)
+        ]
+        pieces = sum(x.astype(jnp.float32) for x in [pieces[:share], *got]).astype(jnp.bfloat16)
+        unit *= radix
     return pieces[0]
 
 

time: 92.8 us -> 94.1 us (1.014)
  starting transfers between devices: 23 us -> 25.3 us
  Pallas kernels: 20 us -> 19 us
    ppermute x8 -> x7, waiting for transfers between devices: 27.1 us -> 12.7 us  [body(): forward = lax.ppermute(forward, 'ctx', after)]
    ppermute x6 -> x7, waiting for transfers between devices: 0.08 us -> 12.3 us  [body(): backward = lax.ppermute(backward, 'ctx', before)]
    ppermute x8 -> x7, starting transfers between devices: 15.5 us -> 6.95 us  [body(): forward = lax.ppermute(forward, 'ctx', after)]
    ppermute x6 -> x7, starting transfers between devices: 1.62 us -> 9.87 us  [body(): backward = lax.ppermute(backward, 'ctx', before)]
    ppermute x4 -> x8, starting transfers between devices: 5.87 us -> 8.46 us  [the longest x6 6.38 us: body(): lax.ppermute(pieces[k * share:(k + 1) * share], axes, [(i, i ^ k * unit)...]
    ppermute x4 -> x8, waiting for transfers between devices: 8.55 us -> 9.88 us  [the longest x6 7.43 us: body(): lax.ppermute(pieces[k * share:(k + 1) * share], axes, [(i, i ^ k * unit)...]
    pallas_call x7 -> x8, Pallas kernels: 20 us -> 19 us  [the longest x1 14.9 us: attend(): pl.pallas_call(functools.partial(attend_kernel, score_scale, chunks, part...]
    unnamed x18 -> x12, local copies, waits for them, and re-layouts: 11.7 us -> 11.6 us
  transfers between devices with their start and end apart: 18 -> 22, of which waited for: 13 -> 17; matrix products, arithmetic and copies ran while one was open for 0% -> 1% of each run, Pallas kernels for 1% -> 1%
where the time goes in v3:
time: 94.1 us; the launch traced here: 93.8 us
  waiting for transfers between devices  34.8 us (37%)
  starting transfers between devices  25.3 us (27%)
  Pallas kernels  19 us (20%)
  local copies, waits for them, and re-layouts  12.6 us (13%)
  matrix products  0.99 us (1%)
    pallas_call x1, Pallas kernels, attend(): pl.pallas_call(functools.partial(attend_kernel, score_scale, chunks, part...  14.9 us
    ppermute x7, waiting for transfers between devices, body(): forward = lax.ppermute(forward, 'ctx', after)  12.7 us
    ppermute x7, waiting for transfers between devices, body(): backward = lax.ppermute(backward, 'ctx', before)  12.3 us
    unnamed x12, local copies, waits for them, and re-layouts  11.6 us
    ppermute x7, starting transfers between devices, body(): backward = lax.ppermute(backward, 'ctx', before)  9.87 us
    ppermute x6, waiting for transfers between devices, body(): lax.ppermute(pieces[k * share:(k + 1) * share], axes, [(i, i ^ k * unit)...  7.43 us
    ppermute x7, starting transfers between devices, body(): forward = lax.ppermute(forward, 'ctx', after)  6.95 us
    ppermute x6, starting transfers between devices, body(): lax.ppermute(pieces[k * share:(k + 1) * share], axes, [(i, i ^ k * unit)...  6.38 us
  transfers between devices with their start and end apart: 22, of which 17 were waited for; matrix products, arithmetic and copies ran while one was open for 1% of the time, Pallas kernels for 1%

profile of v3, /device:TPU:0, one launch (start us, length us, event | category | flops | bytes accessed | tf_op | source)
XLA Modules:
  0.0 93.8 jit_solution(12203996200668950449)
XLA Ops:
  2.4 3.1 %collective-permute-start = (bf16[18,8,512]{2,1,0:T(8,128)(2,1)S(1)}, bf16[18,8,512]{2,1,0:T(8,128)(2,1)S(1)}, u32[]{:S(2)}, u32[]{:S(2)}) collective-permute-start(bf16[18,8,512]{2,1,0:T(8,128)(2,1)S(1)} %pad_maximum_fusion.1), channel_id=1, source_target_pairs={{0,4},{4,8},{8,12},{12,14},{14,10},{10,6},{6,2},{2,0},{1,5},{5,9},... | collective-permute-start | bytes 442376 | tf_op jit(solution)/shard_map/ppermute | solution.py:328
  5.6 3.7 %collective-permute-done = bf16[18,8,512]{2,1,0:T(8,128)(2,1)S(1)} collective-permute-done((bf16[18,8,512]{2,1,0:T(8,128)(2,1)S(1)}, bf16[18,8,512]{2,1,0:T(8,128)(2,1)S(1)}, u32[]{:S(2)}, u32[]{:S(2)}) %collective-permute-start) | collective-permute-done | bytes 147488 | tf_op jit(solution)/shard_map/ppermute | solution.py:328
  9.3 1.8 %collective-permute-start.2 = (bf16[18,8,512]{2,1,0:T(8,128)(2,1)S(1)}, bf16[18,8,512]{2,1,0:T(8,128)(2,1)S(1)}, u32[]{:S(2)}, u32[]{:S(2)}) collective-permute-start(bf16[18,8,512]{2,1,0:T(8,128)(2,1)S(1)} %collective-permute-done), channel_id=1, source_target_pairs={{0,4},{4,8},{8,12},{12,14},{14,10},{10,6},{6,2},{2,0},{1,5},{5,9},... | collective-permute-start | bytes 442376 | tf_op jit(solution)/shard_map/ppermute | solution.py:328
  11.6 2.9 %collective-permute-done.2 = bf16[18,8,512]{2,1,0:T(8,128)(2,1)S(1)} collective-permute-done((bf16[18,8,512]{2,1,0:T(8,128)(2,1)S(1)}, bf16[18,8,512]{2,1,0:T(8,128)(2,1)S(1)}, u32[]{:S(2)}, u32[]{:S(2)}) %collective-permute-start.2) | collective-permute-done | bytes 147488 | tf_op jit(solution)/shard_map/ppermute | solution.py:328
  16.9 2.9 %collective-permute-done.4 = bf16[18,8,512]{2,1,0:T(8,128)(2,1)S(1)} collective-permute-done((bf16[18,8,512]{2,1,0:T(8,128)(2,1)S(1)}, bf16[18,8,512]{2,1,0:T(8,128)(2,1)S(1)}, u32[]{:S(2)}, u32[]{:S(2)}) %collective-permute-start.4) | collective-permute-done | bytes 147488 | tf_op jit(solution)/shard_map/ppermute | solution.py:328
  19.9 2.1 %collective-permute-done.5 = bf16[18,8,512]{2,1,0:T(8,128)(2,1)S(1)} collective-permute-done((bf16[18,8,512]{2,1,0:T(8,128)(2,1)S(1)}, bf16[18,8,512]{2,1,0:T(8,128)(2,1)S(1)}, u32[]{:S(2)}, u32[]{:S(2)}) %collective-permute-start.5) | collective-permute-done | bytes 147488 | tf_op jit(solution)/shard_map/ppermute | solution.py:329
  22.4 1.9 %collective-permute-start.6 = (bf16[9,8,512]{2,1,0:T(8,128)(2,1)S(1)}, bf16[9,8,512]{2,1,0:T(8,128)(2,1)S(1)}, u32[]{:S(2)}, u32[]{:S(2)}) collective-permute-start(bf16[9,8,512]{2,1,0:T(8,128)(2,1)S(1)} %slice.108), channel_id=1, source_target_pairs={{0,4},{4,8},{8,12},{12,14},{14,10},{10,6},{6,2},{2,0},{1,5},{5,9},... | collective-permute-start | bytes 221192 | tf_op jit(solution)/shard_map/ppermute | solution.py:333
  24.4 2.2 %collective-permute-done.7 = bf16[9,8,512]{2,1,0:T(8,128)(2,1)S(1)} collective-permute-done((bf16[9,8,512]{2,1,0:T(8,128)(2,1)S(1)}, bf16[9,8,512]{2,1,0:T(8,128)(2,1)S(1)}, u32[]{:S(2)}, u32[]{:S(2)}) %collective-permute-start.7) | collective-permute-done | bytes 73760 | tf_op jit(solution)/shard_map/ppermute | solution.py:334
  26.9 14.9 %attend.1 = (bf16[17,8,512]{2,1,0:T(8,128)(2,1)S(1)}, bf16[17,8,512]{2,1,0:T(8,128)(2,1)S(1)}, bf16[17,8,512]{2,1,0:T(8,128)(2,1)S(1)}, bf16[17,8,512]{2,1,0:T(8...) custom-call(s32[224]{0:T(256)S(1)} %copy-done.4, ...), custom_call_target="tpu_custom_call" | custom-call | flops 7985954816 | bytes 16515072 | tf_op jit(solution)/shard_map/attend/pallas_call | solution.py:178
  41.9 5.2 %copy-done.1 = bf16[1024,7168]{1,0:T(8,128)(2,1)} copy-done((bf16[1024,7168]{1,0:T(8,128)(2,1)}, bf16[1024,7168]{1,0:T(8,128)(2,1)S(1)}, u32[]{:S(2)}) %copy-start.1) | copy-done | bytes 14680088
  47.1 2.1 %collective-permute-start.12 = (bf16[9,8,512]{2,1,0:T(8,128)(2,1)S(1)}, bf16[9,8,512]{2,1,0:T(8,128)(2,1)S(1)}, u32[]{:S(2)}, u32[]{:S(2)}) collective-permute-start(bf16[9,8,512]{2,1,0:T(8,128)(2,1)S(1)} %get-tuple-element.23), channel_id=1, source_target_pairs={{4,0},{8,4},{12,8},{14,12},{10,14},{6,10},{2,6},{0,2},{5,1},{9,5},... | collective-permute-start | bytes 221192 | tf_op jit(solution)/shard_map/ppermute | solution.py:362
  49.1 2.3 %collective-permute-done.12.got_ref = bf16[9,8,512]{2,1,0:T(8,128)(2,1)S(1)} collective-permute-done((bf16[9,8,512]{2,1,0:T(8,128)(2,1)S(1)}, bf16[9,8,512]{2,1,0:T(8,128)(2,1)S(1)}, u32[]{:S(2)}, u32[]{:S(2)}) %collective-permute-start.12) | collective-permute-done | bytes 73760 | tf_op jit(solution)/shard_map/ppermute | solution.py:362
  51.5 2.3 %collective-permute-start.13 = (bf16[17,8,512]{2,1,0:T(8,128)(2,1)S(1)}, bf16[17,8,512]{2,1,0:T(8,128)(2,1)S(1)}, u32[]{:S(2)}, u32[]{:S(2)}) collective-permute-start(bf16[17,8,512]{2,1,0:T(8,128)(2,1)S(1)} %merge.9), channel_id=1, source_target_pairs={{4,0},{8,4},{12,8},{14,12},{10,14},{6,10},{2,6},{0,2},{5,1},{9,5},... | collective-permute-start | bytes 417800 | tf_op jit(solution)/shard_map/ppermute | solution.py:362
  54.0 3.4 %collective-permute-done.13.got_ref = bf16[17,8,512]{2,1,0:T(8,128)(2,1)S(1)} collective-permute-done((bf16[17,8,512]{2,1,0:T(8,128)(2,1)S(1)}, bf16[17,8,512]{2,1,0:T(8,128)(2,1)S(1)}, u32[]{:S(2)}, u32[]{:S(2)}) %collective-permute-start.13) | collective-permute-done | bytes 139296 | tf_op jit(solution)/shard_map/ppermute | solution.py:362
  57.6 2.5 %collective-permute-start.14 = (bf16[17,8,512]{2,1,0:T(8,128)(2,1)S(1)}, bf16[17,8,512]{2,1,0:T(8,128)(2,1)S(1)}, u32[]{:S(2)}, u32[]{:S(2)}) collective-permute-start(bf16[17,8,512]{2,1,0:T(8,128)(2,1)S(1)} %merge.10), channel_id=1, source_target_pairs={{4,0},{8,4},{12,8},{14,12},{10,14},{6,10},{2,6},{0,2},{5,1},{9,5},... | collective-permute-start | bytes 417800 | tf_op jit(solution)/shard_map/ppermute | solution.py:362
  60.5 2.2 %collective-permute-done.14.got_ref = bf16[17,8,512]{2,1,0:T(8,128)(2,1)S(1)} collective-permute-done((bf16[17,8,512]{2,1,0:T(8,128)(2,1)S(1)}, bf16[17,8,512]{2,1,0:T(8,128)(2,1)S(1)}, u32[]{:S(2)}, u32[]{:S(2)}) %collective-permute-start.14) | collective-permute-done | bytes 139296 | tf_op jit(solution)/shard_map/ppermute | solution.py:362
  62.9 2.5 %collective-permute-start.15 = (bf16[17,8,512]{2,1,0:T(8,128)(2,1)S(1)}, bf16[17,8,512]{2,1,0:T(8,128)(2,1)S(1)}, u32[]{:S(2)}, u32[]{:S(2)}) collective-permute-start(bf16[17,8,512]{2,1,0:T(8,128)(2,1)S(1)} %merge.11), channel_id=1, source_target_pairs={{4,0},{8,4},{12,8},{14,12},{10,14},{6,10},{2,6},{0,2},{5,1},{9,5},... | collective-permute-start | bytes 417800 | tf_op jit(solution)/shard_map/ppermute | solution.py:362
  65.8 2.2 %collective-permute-done.15.backward_ref = bf16[17,8,512]{2,1,0:T(8,128)(2,1)S(1)} collective-permute-done((bf16[17,8,512]{2,1,0:T(8,128)(2,1)S(1)}, bf16[17,8,512]{2,1,0:T(8,128)(2,1)S(1)}, u32[]{:S(2)}, u32[]{:S(2)}) %collective-permute-start.15) | collective-permute-done | bytes 139296 | tf_op jit(solution)/shard_map/ppermute | solution.py:362
  68.0 2.8 %collective-permute-done.11.forward_ref = bf16[17,8,512]{2,1,0:T(8,128)(2,1)S(1)} collective-permute-done((bf16[17,8,512]{2,1,0:T(8,128)(2,1)S(1)}, bf16[17,8,512]{2,1,0:T(8,128)(2,1)S(1)}, u32[]{:S(2)}, u32[]{:S(2)}) %collective-permute-start.11) | collective-permute-done | bytes 139296 | tf_op jit(solution)/shard_map/ppermute | solution.py:361
  70.8 5.2 %copy-done.2 = bf16[1024,7168]{1,0:T(8,128)(2,1)S(1)} copy-done((bf16[1024,7168]{1,0:T(8,128)(2,1)S(1)}, bf16[1024,7168]{1,0:T(8,128)(2,1)}, u32[]{:S(2)}) %copy-start.2) | copy-done | bytes 14680088
  76.0 3.3 %finish.1 = bf16[16,16,448]{2,1,0:T(8,128)(2,1)S(1)} custom-call(s32[1]{0:T(128)} %bitcast.here_ref, bf16[17,8,512]{2,1,0:T(8,128)(2,1)S(1)} %get-tuple-element.15.own_ref, bf16[17,8,512]{2,1,0:T(8,128)(2,1)S(1)} %collective-permute-done.11.forward_ref, bf16[17,8,512]{2,1,0:T(8,128)(2,1)S(1)} %collective-permute-done.15.backward_ref, ...), custom_call_target="tpu_custom_call" | custom-call | flops 3758096384 | tf_op jit(solution)/shard_map/finish/pallas_call | solution.py:289
  81.3 2.6 %collective-permute-done.17 = bf16[4,16,448]{2,1,0:T(8,128)(2,1)S(1)} collective-permute-done((bf16[4,16,448]{2,1,0:T(8,128)(2,1)S(1)}, bf16[4,16,448]{2,1,0:T(8,128)(2,1)S(1)}, u32[]{:S(2)}, u32[]{:S(2)}) %collective-permute-start.17) | collective-permute-done | bytes 57376 | tf_op jit(solution)/shard_map/ppermute | solution.py:379
  87.7 1.9 %collective-permute-start.21 = (bf16[1,16,448]{2,1,0:T(8,128)(2,1)S(1)}, bf16[1,16,448]{2,1,0:T(8,128)(2,1)S(1)}, u32[]{:S(2)}, u32[]{:S(2)}) collective-permute-start(bf16[1,16,448]{2,1,0:T(8,128)(2,1)S(1)} %get-tuple-element.29), channel_id=1, source_target_pairs={{0,12},{1,13},{2,14},{3,15},{4,8},{5,9},{6,10},{7,11},{8,4},{9,5},... | collective-permute-start | bytes 43016 | tf_op jit(solution)/shard_map/ppermute | solution.py:379
  89.5 2.0 %collective-permute-done.20 = bf16[1,16,448]{2,1,0:T(8,128)(2,1)S(1)} collective-permute-done((bf16[1,16,448]{2,1,0:T(8,128)(2,1)S(1)}, bf16[1,16,448]{2,1,0:T(8,128)(2,1)S(1)}, u32[]{:S(2)}, u32[]{:S(2)}) %collective-permute-start.20) | collective-permute-done | bytes 14368 | tf_op jit(solution)/shard_map/ppermute | solution.py:379
  (78 shorter events, 15.4 us)
Async XLA Ops:
  2.4 6.9 %collective-permute-start = (bf16[18,8,512]{2,1,0:T(8,128)(2,1)S(1)}, bf16[18,8,512]{2,1,0:T(8,128)(2,1)S(1)}, u32[]{:S(2)}, u32[]{:S(2)}) collective-permute-start(bf16[18,8,512]{2,1,0:T(8,128)(2,1)S(1)} %pad_maximum_fusion.1), channel_id=1, source_target_pairs={{0,4},{4,8},{8,12},{12,14},{14,10},{10,6},{6,2},{2,0},{1,5},{5,9},... | collective-permute-start | bytes 442376 | tf_op jit(solution)/shard_map/ppermute | solution.py:328
  5.4 5.8 %collective-permute-start.1 = (bf16[18,8,512]{2,1,0:T(8,128)(2,1)S(1)}, bf16[18,8,512]{2,1,0:T(8,128)(2,1)S(1)}, u32[]{:S(2)}, u32[]{:S(2)}) collective-permute-start(bf16[18,8,512]{2,1,0:T(8,128)(2,1)S(1)} %pad_maximum_fusion.1), channel_id=1, source_target_pairs={{4,0},{8,4},{12,8},{14,12},{10,14},{6,10},{2,6},{0,2},{5,1},{9,5},... | collective-permute-start | bytes 442376 | tf_op jit(solution)/shard_map/ppermute | solution.py:329
  9.3 5.2 %collective-permute-start.2 = (bf16[18,8,512]{2,1,0:T(8,128)(2,1)S(1)}, bf16[18,8,512]{2,1,0:T(8,128)(2,1)S(1)}, u32[]{:S(2)}, u32[]{:S(2)}) collective-permute-start(bf16[18,8,512]{2,1,0:T(8,128)(2,1)S(1)} %collective-permute-done), channel_id=1, source_target_pairs={{0,4},{4,8},{8,12},{12,14},{14,10},{10,6},{6,2},{2,0},{1,5},{5,9},... | collective-permute-start | bytes 442376 | tf_op jit(solution)/shard_map/ppermute | solution.py:328
  11.2 5.3 %collective-permute-start.3 = (bf16[18,8,512]{2,1,0:T(8,128)(2,1)S(1)}, bf16[18,8,512]{2,1,0:T(8,128)(2,1)S(1)}, u32[]{:S(2)}, u32[]{:S(2)}) collective-permute-start(bf16[18,8,512]{2,1,0:T(8,128)(2,1)S(1)} %collective-permute-done.1), channel_id=1, source_target_pairs={{4,0},{8,4},{12,8},{14,12},{10,14},{6,10},{2,6},{0,2},{5,1},{9,5},... | collective-permute-start | bytes 442376 | tf_op jit(solution)/shard_map/ppermute | solution.py:329
  14.7 5.2 %collective-permute-start.4 = (bf16[18,8,512]{2,1,0:T(8,128)(2,1)S(1)}, bf16[18,8,512]{2,1,0:T(8,128)(2,1)S(1)}, u32[]{:S(2)}, u32[]{:S(2)}) collective-permute-start(bf16[18,8,512]{2,1,0:T(8,128)(2,1)S(1)} %collective-permute-done.2), channel_id=1, source_target_pairs={{0,4},{4,8},{8,12},{12,14},{14,10},{10,6},{6,2},{2,0},{1,5},{5,9},... | collective-permute-start | bytes 442376 | tf_op jit(solution)/shard_map/ppermute | solution.py:328
  16.5 5.6 %collective-permute-start.5 = (bf16[18,8,512]{2,1,0:T(8,128)(2,1)S(1)}, bf16[18,8,512]{2,1,0:T(8,128)(2,1)S(1)}, u32[]{:S(2)}, u32[]{:S(2)}) collective-permute-start(bf16[18,8,512]{2,1,0:T(8,128)(2,1)S(1)} %collective-permute-done.3), channel_id=1, source_target_pairs={{4,0},{8,4},{12,8},{14,12},{10,14},{6,10},{2,6},{0,2},{5,1},{9,5},... | collective-permute-start | bytes 442376 | tf_op jit(solution)/shard_map/ppermute | solution.py:329
  16.9 10.1 %copy-start.4 = (s32[224]{0:T(256)S(1)}, s32[224]{0:T(256)}, u32[]{:S(2)}) copy-start(s32[224]{0:T(256)} %owner_ref.1) | copy-start | bytes 2692
  22.2 4.4 %collective-permute-start.7 = (bf16[9,8,512]{2,1,0:T(8,128)(2,1)S(1)}, bf16[9,8,512]{2,1,0:T(8,128)(2,1)S(1)}, u32[]{:S(2)}, u32[]{:S(2)}) collective-permute-start(bf16[9,8,512]{2,1,0:T(8,128)(2,1)S(1)} %slice.109), channel_id=1, source_target_pairs={{4,0},{8,4},{12,8},{14,12},{10,14},{6,10},{2,6},{0,2},{5,1},{9,5},... | collective-permute-start | bytes 221192 | tf_op jit(solution)/shard_map/ppermute | solution.py:334
  22.4 4.5 %collective-permute-start.6 = (bf16[9,8,512]{2,1,0:T(8,128)(2,1)S(1)}, bf16[9,8,512]{2,1,0:T(8,128)(2,1)S(1)}, u32[]{:S(2)}, u32[]{:S(2)}) collective-permute-start(bf16[9,8,512]{2,1,0:T(8,128)(2,1)S(1)} %slice.108), channel_id=1, source_target_pairs={{0,4},{4,8},{8,12},{12,14},{14,10},{10,6},{6,2},{2,0},{1,5},{5,9},... | collective-permute-start | bytes 221192 | tf_op jit(solution)/shard_map/ppermute | solution.py:333
  47.1 23.7 %copy-start.3 = (bf16[8,512,128]{2,1,0:T(8,128)(2,1)S(1)}, bf16[8,512,128]{2,1,0:T(8,128)(2,1)}, u32[]{:S(2)}) copy-start(bf16[8,512,128]{2,1,0:T(8,128)(2,1)} %value_ref.1) | copy-start | bytes 3145732
  47.1 4.4 %collective-permute-start.12 = (bf16[9,8,512]{2,1,0:T(8,128)(2,1)S(1)}, bf16[9,8,512]{2,1,0:T(8,128)(2,1)S(1)}, u32[]{:S(2)}, u32[]{:S(2)}) collective-permute-start(bf16[9,8,512]{2,1,0:T(8,128)(2,1)S(1)} %get-tuple-element.23), channel_id=1, source_target_pairs={{4,0},{8,4},{12,8},{14,12},{10,14},{6,10},{2,6},{0,2},{5,1},{9,5},... | collective-permute-start | bytes 221192 | tf_op jit(solution)/shard_map/ppermute | solution.py:362
  49.1 4.7 %collective-permute-start.8 = (bf16[9,8,512]{2,1,0:T(8,128)(2,1)S(1)}, bf16[9,8,512]{2,1,0:T(8,128)(2,1)S(1)}, u32[]{:S(2)}, u32[]{:S(2)}) collective-permute-start(bf16[9,8,512]{2,1,0:T(8,128)(2,1)S(1)} %get-tuple-element.19), channel_id=1, source_target_pairs={{0,4},{4,8},{8,12},{12,14},{14,10},{10,6},{6,2},{2,0},{1,5},{5,9},... | collective-permute-start | bytes 221192 | tf_op jit(solution)/shard_map/ppermute | solution.py:361
  51.5 5.9 %collective-permute-start.13 = (bf16[17,8,512]{2,1,0:T(8,128)(2,1)S(1)}, bf16[17,8,512]{2,1,0:T(8,128)(2,1)S(1)}, u32[]{:S(2)}, u32[]{:S(2)}) collective-permute-start(bf16[17,8,512]{2,1,0:T(8,128)(2,1)S(1)} %merge.9), channel_id=1, source_target_pairs={{4,0},{8,4},{12,8},{14,12},{10,14},{6,10},{2,6},{0,2},{5,1},{9,5},... | collective-permute-start | bytes 417800 | tf_op jit(solution)/shard_map/ppermute | solution.py:362
  53.9 6.4 %collective-permute-start.9 = (bf16[17,8,512]{2,1,0:T(8,128)(2,1)S(1)}, bf16[17,8,512]{2,1,0:T(8,128)(2,1)S(1)}, u32[]{:S(2)}, u32[]{:S(2)}) collective-permute-start(bf16[17,8,512]{2,1,0:T(8,128)(2,1)S(1)} %merge.6), channel_id=1, source_target_pairs={{0,4},{4,8},{8,12},{12,14},{14,10},{10,6},{6,2},{2,0},{1,5},{5,9},... | collective-permute-start | bytes 417800 | tf_op jit(solution)/shard_map/ppermute | solution.py:361
  57.6 5.1 %collective-permute-start.14 = (bf16[17,8,512]{2,1,0:T(8,128)(2,1)S(1)}, bf16[17,8,512]{2,1,0:T(8,128)(2,1)S(1)}, u32[]{:S(2)}, u32[]{:S(2)}) collective-permute-start(bf16[17,8,512]{2,1,0:T(8,128)(2,1)S(1)} %merge.10), channel_id=1, source_target_pairs={{4,0},{8,4},{12,8},{14,12},{10,14},{6,10},{2,6},{0,2},{5,1},{9,5},... | collective-permute-start | bytes 417800 | tf_op jit(solution)/shard_map/ppermute | solution.py:362
  60.4 5.1 %collective-permute-start.10 = (bf16[17,8,512]{2,1,0:T(8,128)(2,1)S(1)}, bf16[17,8,512]{2,1,0:T(8,128)(2,1)S(1)}, u32[]{:S(2)}, u32[]{:S(2)}) collective-permute-start(bf16[17,8,512]{2,1,0:T(8,128)(2,1)S(1)} %merge.7), channel_id=1, source_target_pairs={{0,4},{4,8},{8,12},{12,14},{14,10},{10,6},{6,2},{2,0},{1,5},{5,9},... | collective-permute-start | bytes 417800 | tf_op jit(solution)/shard_map/ppermute | solution.py:361
  62.9 5.1 %collective-permute-start.15 = (bf16[17,8,512]{2,1,0:T(8,128)(2,1)S(1)}, bf16[17,8,512]{2,1,0:T(8,128)(2,1)S(1)}, u32[]{:S(2)}, u32[]{:S(2)}) collective-permute-start(bf16[17,8,512]{2,1,0:T(8,128)(2,1)S(1)} %merge.11), channel_id=1, source_target_pairs={{4,0},{8,4},{12,8},{14,12},{10,14},{6,10},{2,6},{0,2},{5,1},{9,5},... | collective-permute-start | bytes 417800 | tf_op jit(solution)/shard_map/ppermute | solution.py:362
  65.7 5.1 %collective-permute-start.11 = (bf16[17,8,512]{2,1,0:T(8,128)(2,1)S(1)}, bf16[17,8,512]{2,1,0:T(8,128)(2,1)S(1)}, u32[]{:S(2)}, u32[]{:S(2)}) collective-permute-start(bf16[17,8,512]{2,1,0:T(8,128)(2,1)S(1)} %merge.8), channel_id=1, source_target_pairs={{0,4},{4,8},{8,12},{12,14},{14,10},{10,6},{6,2},{2,0},{1,5},{5,9},... | collective-permute-start | bytes 417800 | tf_op jit(solution)/shard_map/ppermute | solution.py:361
  79.3 1.9 %collective-permute-start.16 = (bf16[4,16,448]{2,1,0:T(8,128)(2,1)S(1)}, bf16[4,16,448]{2,1,0:T(8,128)(2,1)S(1)}, u32[]{:S(2)}, u32[]{:S(2)}) collective-permute-start(bf16[4,16,448]{2,1,0:T(8,128)(2,1)S(1)} %get-tuple-element.25), channel_id=1, source_target_pairs={{0,1},{1,0},{2,3},{3,2},{4,5},{5,4},{6,7},{7,6},{8,9},{9,8},{10,11... | collective-permute-start | bytes 172040 | tf_op jit(solution)/shard_map/ppermute | solution.py:379
  79.4 4.5 %collective-permute-start.17 = (bf16[4,16,448]{2,1,0:T(8,128)(2,1)S(1)}, bf16[4,16,448]{2,1,0:T(8,128)(2,1)S(1)}, u32[]{:S(2)}, u32[]{:S(2)}) collective-permute-start(bf16[4,16,448]{2,1,0:T(8,128)(2,1)S(1)} %get-tuple-element.27), channel_id=1, source_target_pairs={{0,2},{1,3},{2,0},{3,1},{4,6},{5,7},{6,4},{7,5},{8,10},{9,11},{10,... | collective-permute-start | bytes 172040 | tf_op jit(solution)/shard_map/ppermute | solution.py:379
  81.0 4.0 %collective-permute-start.18 = (bf16[4,16,448]{2,1,0:T(8,128)(2,1)S(1)}, bf16[4,16,448]{2,1,0:T(8,128)(2,1)S(1)}, u32[]{:S(2)}, u32[]{:S(2)}) collective-permute-start(bf16[4,16,448]{2,1,0:T(8,128)(2,1)S(1)} %get-tuple-element.26), channel_id=1, source_target_pairs={{0,3},{1,2},{2,1},{3,0},{4,7},{5,6},{6,5},{7,4},{8,11},{9,10},{10,... | collective-permute-start | bytes 172040 | tf_op jit(solution)/shard_map/ppermute | solution.py:379
  85.1 4.5 %collective-permute-start.19 = (bf16[1,16,448]{2,1,0:T(8,128)(2,1)S(1)}, bf16[1,16,448]{2,1,0:T(8,128)(2,1)S(1)}, u32[]{:S(2)}, u32[]{:S(2)}) collective-permute-start(bf16[1,16,448]{2,1,0:T(8,128)(2,1)S(1)} %get-tuple-element.28), channel_id=1, source_target_pairs={{0,4},{1,5},{2,6},{3,7},{4,0},{5,1},{6,2},{7,3},{8,12},{9,13},{10,... | collective-permute-start | bytes 43016 | tf_op jit(solution)/shard_map/ppermute | solution.py:379
  86.6 4.9 %collective-permute-start.20 = (bf16[1,16,448]{2,1,0:T(8,128)(2,1)S(1)}, bf16[1,16,448]{2,1,0:T(8,128)(2,1)S(1)}, u32[]{:S(2)}, u32[]{:S(2)}) collective-permute-start(bf16[1,16,448]{2,1,0:T(8,128)(2,1)S(1)} %get-tuple-element.30), channel_id=1, source_target_pairs={{0,8},{1,9},{2,10},{3,11},{4,12},{5,13},{6,14},{7,15},{8,0},{9,1},... | collective-permute-start | bytes 43016 | tf_op jit(solution)/shard_map/ppermute | solution.py:379
  87.7 5.5 %collective-permute-start.21 = (bf16[1,16,448]{2,1,0:T(8,128)(2,1)S(1)}, bf16[1,16,448]{2,1,0:T(8,128)(2,1)S(1)}, u32[]{:S(2)}, u32[]{:S(2)}) collective-permute-start(bf16[1,16,448]{2,1,0:T(8,128)(2,1)S(1)} %get-tuple-element.29), channel_id=1, source_target_pairs={{0,12},{1,13},{2,14},{3,15},{4,8},{5,9},{6,10},{7,11},{8,4},{9,5},... | collective-permute-start | bytes 43016 | tf_op jit(solution)/shard_map/ppermute | solution.py:379
  (4 other events, 13.9 us)

commit v4 on v2

--- a/solution.py
+++ b/solution.py
@@ -18,12 +18,6 @@
 
 def in_vmem(x):
     return pltpu.with_memory_space_constraint(x, pltpu.VMEM)
-
-
-def ring_order(count):
-    if count % 2:
-        return list(range(count))
-    return list(range(0, count, 2)) + list(range(count - 1, 0, -2))
 
 
 def split_level(level):
@@ -171,7 +165,7 @@
     heads_here = heads // blocks
     pair_len = 2 * page_len
     groups = pages // GROUP_PAGES
-    chunks = groups // max(d for d in range(1, 9) if groups % d == 0)
+    chunks = groups // max(d for d in range(1, 15) if groups % d == 0)
     any_spec = pl.BlockSpec(memory_space=pl.ANY)
     out = pl.pallas_call(
         functools.partial(attend_kernel, score_scale, chunks, blocks),
@@ -199,7 +193,7 @@
         ),
         name="attend",
     )(page_owner, in_vmem(query_full), latent_cache, output_weight)
-    return out[:blocks], out[blocks]
+    return out[:-1], out[-1]
 
 
 def shares(levels):
@@ -227,19 +221,19 @@
         out_shape=pltpu.VMEM(own.shape, own.dtype),
         in_specs=[VMEM_SPEC] * 2,
         out_specs=VMEM_SPEC,
+        compiler_params=pltpu.CompilerParams(vmem_limit_bytes=2 * MIB),
         cost_estimate=pl.CostEstimate(flops=4 * own.size, bytes_accessed=0, transcendentals=0),
         name="merge",
     )(in_vmem(own), in_vmem(got))
 
 
 def finish_kernel(
-    block_columns, here_ref, own_ref, forward_ref, backward_ref, value_ref, weight_ref, out_ref,
-    attended_scr, head_scr,
+    block_columns, radices, here_ref, value_ref, weight_ref, *refs
 ):
-    requests, heads_here = own_ref.shape[0] - 1, own_ref.shape[1]
+    messages, (out_ref, attended_scr, head_scr) = refs[:-3], refs[-3:]
+    requests, heads_here = messages[0].shape[0] - 1, messages[0].shape[1]
     value_size = value_ref.shape[2]
     owners, _, width = out_ref.shape
-    messages = (own_ref, forward_ref, backward_ref)
     weights, _ = shares([load_level(ref, requests) for ref in messages])
     for r in range(requests):
         attended_scr[r * heads_here : (r + 1) * heads_here] = sum(
@@ -256,7 +250,6 @@
         ).astype(jnp.bfloat16)
     head_out = head_scr[...]
     per_block = block_columns // width
-    bits = owners.bit_length() - 1
     for j in range(owners // per_block):
         product = jnp.dot(
             head_out,
@@ -265,22 +258,26 @@
         ).astype(jnp.bfloat16)
         for i in range(per_block):
             distance = here_ref[0] ^ (j * per_block + i)
-            place = sum(((distance >> b) & 1) << (bits - 1 - b) for b in range(bits))
+            place = 0
+            for radix in radices:
+                place = place * radix + (distance & (radix - 1))
+                distance = distance >> (radix.bit_length() - 1)
             out_ref[place] = product[:, i * width : (i + 1) * width]
 
 
-def finish(here, own, forward, backward, value_absorb, weight, owners):
-    requests, heads_here = own.shape[0] - 1, own.shape[1]
+def finish(here, messages, value_absorb, weight, radices):
+    requests, heads_here = messages[0].shape[0] - 1, messages[0].shape[1]
     latent_size, value_size = value_absorb.shape[1:]
     depth, columns = weight.shape
+    owners = functools.reduce(lambda a, b: a * b, radices)
     width = columns // owners
     block_columns = width
     while block_columns % LANES:
         block_columns *= 2
     return pl.pallas_call(
-        functools.partial(finish_kernel, block_columns),
+        functools.partial(finish_kernel, block_columns, radices),
         out_shape=pltpu.VMEM((owners, requests, width), jnp.bfloat16),
-        in_specs=[SMEM_SPEC] + [VMEM_SPEC] * 5,
+        in_specs=[SMEM_SPEC] + [VMEM_SPEC] * (2 + len(messages)),
         out_specs=VMEM_SPEC,
         scratch_shapes=[
             pltpu.VMEM((requests * heads_here, latent_size), jnp.float32),
@@ -291,73 +288,86 @@
             flops=2 * 256 * depth * columns, bytes_accessed=0, transcendentals=0
         ),
         name="finish",
-    )(here, *[in_vmem(x) for x in (own, forward, backward, value_absorb, weight)])
+    )(here, *[in_vmem(x) for x in (value_absorb, weight, *messages)])
 
 
 def body(
-    query_nope, query_rope, key_absorb, value_absorb, output_weight, latent_cache, page_owner, ring
+    query_nope, query_rope, key_absorb, value_absorb, output_weight, latent_cache, page_owner
 ):
     requests, heads_here, nope_size = query_nope.shape
     latent_size = key_absorb.shape[2]
     rope_size = query_rope.shape[1] // heads_here
     score_scale = (nope_size + rope_size) ** (-0.5)
-    count = len(ring)
+    count = lax.axis_size("ctx")
+    axes = ("ctx", "head")
+    here = lax.axis_index(axes).astype(jnp.int32).reshape(1)
+
+    def exchange(x, distance):
+        return lax.ppermute(x, "ctx", [(i, i ^ distance) for i in range(count)])
+
     query_latent = jnp.einsum(
         "rhn,hnl->rhl", query_nope, key_absorb, preferred_element_type=jnp.float32
     ).astype(jnp.bfloat16)
     own = jnp.concatenate(
-        [query_latent, query_rope.reshape(requests, heads_here, rope_size)], axis=2
+        [query_latent, query_rope.reshape(-1, heads_here, latent_size)], axis=0
     )
-
-    after = [(ring[i], ring[(i + 1) % count]) for i in range(count)]
-    before = [(b, a) for a, b in after]
-    blocks, offsets = [own], [0]
-    forward = backward = own
-    for step in range(1, count // 2 + 1):
-        forward = lax.ppermute(forward, "ctx", after)
-        blocks.append(forward)
-        offsets.append(-step)
-        if 2 * step < count:
-            backward = lax.ppermute(backward, "ctx", before)
-            blocks.append(backward)
-            offsets.append(step)
-    query_full = jnp.concatenate(blocks, axis=1)
-
-    messages, weight = attend(
+    own, here = lax.optimization_barrier((own, here))
+
+    even = [*range(4, count, 2), 2] if count > 2 else []
+    block_at = {0: own}
+    for distance in even:
+        block_at[distance] = exchange(own, distance)
+    for distance in [0, *even]:
+        block_at[distance ^ 1] = exchange(block_at[distance], 1)
+    query_full = jnp.concatenate(
+        [
+            jnp.concatenate(
+                [
+                    block_at[d][:requests],
+                    block_at[d][requests:].reshape(requests, heads_here, rope_size),
+                ],
+                axis=2,
+            )
+            for d in range(count)
+        ],
+        axis=1,
+    )
+
+    message_to, weight = attend(
         query_full, latent_cache, page_owner, output_weight, score_scale, latent_size, count
     )
-    message_to = {offset % count: message for offset, message in zip(offsets, messages)}
-
-    forward_steps, backward_steps = count // 2, (count - 1) // 2
-    forward, backward = message_to[forward_steps], message_to[-backward_steps % count]
-    for step in range(1, forward_steps + 1):
-        forward = lax.ppermute(forward, "ctx", after)
-        if step <= backward_steps:
-            backward = lax.ppermute(backward, "ctx", before)
-        if step < forward_steps:
-            forward = merge(message_to[forward_steps - step], forward)
-        if step < backward_steps:
-            backward = merge(message_to[(step - backward_steps) % count], backward)
-
-    axes = ("ctx", "head")
+
+    across = {distance: exchange(message_to[distance ^ 1], 1) for distance in [*even, 0]}
+    arrived = [
+        exchange(merge(message_to[distance], across[distance]), distance) for distance in even
+    ]
+    messages = [message_to[0], across[0], *arrived]
+
     owners = lax.axis_size(axes)
-    here = lax.axis_index(axes).astype(jnp.int32).reshape(1)
-    pieces = finish(here, message_to[0], forward, backward, value_absorb, weight, owners)
-    distance = 1
-    while distance < owners:
-        pairs = [(i, i ^ distance) for i in range(owners)]
-        half = pieces.shape[0] // 2
-        got = lax.ppermute(pieces[half:], axes, pairs)
-        pieces = (pieces[:half].astype(jnp.float32) + got.astype(jnp.float32)).astype(
-            jnp.bfloat16
-        )
-        distance *= 2
+    radices = []
+    while functools.reduce(lambda a, b: a * b, radices, 1) < owners:
+        left = owners // functools.reduce(lambda a, b: a * b, radices, 1)
+        radices.append(4 if left % 4 == 0 else 2)
+    pieces = finish(here, messages, value_absorb, weight, radices)
+    unit = 1
+    for radix in radices:
+        share = pieces.shape[0] // radix
+        got = [
+            lax.ppermute(
+                pieces[k * share : (k + 1) * share],
+                axes,
+                [(i, i ^ (k * unit)) for i in range(owners)],
+            )
+            for k in range(1, radix)
+        ]
+        pieces = sum(x.astype(jnp.float32) for x in [pieces[:share], *got]).astype(jnp.bfloat16)
+        unit *= radix
     return pieces[0]
 
 
 def solution(mesh):
     return jax.shard_map(
-        functools.partial(body, ring=ring_order(mesh.shape["ctx"])),
+        body,
         mesh=mesh,
         in_specs=(
             P("groups", ("ctx", "head"), None),

time: 92.8 us -> 80.6 us (0.87)
  local copies, waits for them, and re-layouts: 12 us -> 4.02 us
  waiting for transfers between devices: 35.7 us -> 31.7 us
  other arithmetic: 0.71 us -> 2.35 us
  Pallas kernels: 20 us -> 18.7 us
    unnamed x18 -> x10, local copies, waits for them, and re-layouts: 11.7 us -> 1.24 us
    ppermute x18 -> x20, waiting for transfers between devices: 35.7 us -> 31.7 us  [the longest x14 24.7 us: exchange(): return lax.ppermute(x, 'ctx', [(i, i ^ distance) for i in range(count)])]
    reshape x1 -> x8, local copies, waits for them, and re-layouts: 0.09 us -> 2.54 us  [body(): block_at[d][requests:].reshape(requests, heads_here, rope_size)]
    unnamed x0 -> x7, other arithmetic: none -> 1.66 us
    pallas_call x1, Pallas kernels: 16 us -> 14.9 us  [attend(): pl.pallas_call(functools.partial(attend_kernel, score_scale, chunks, bloc...]
    ppermute x18 -> x20, starting transfers between devices: 23 us -> 22.2 us  [the longest x14 16.5 us: exchange(): return lax.ppermute(x, 'ctx', [(i, i ^ distance) for i in range(count)])]
  transfers between devices with their start and end apart: 18 -> 20, of which waited for: 13 -> 15; matrix products, arithmetic and copies ran while one was open for 0% -> 4% of each run, Pallas kernels for 1% -> 1%
where the time goes in v4:
time: 80.6 us; the launch traced here: 80.3 us
  waiting for transfers between devices  31.7 us (39%)
  starting transfers between devices  22.2 us (28%)
  Pallas kernels  18.7 us (23%)
  local copies, waits for them, and re-layouts  4.02 us (5%)
  other arithmetic  2.35 us (3%)
  matrix products  0.99 us (1%)
    ppermute x14, waiting for transfers between devices, exchange(): return lax.ppermute(x, 'ctx', [(i, i ^ distance) for i in range(count)])  24.7 us
    ppermute x14, starting transfers between devices, exchange(): return lax.ppermute(x, 'ctx', [(i, i ^ distance) for i in range(count)])  16.5 us
    pallas_call x1, Pallas kernels, attend(): pl.pallas_call(functools.partial(attend_kernel, score_scale, chunks, bloc...  14.9 us
    ppermute x6, waiting for transfers between devices, body(): lax.ppermute(pieces[k * share:(k + 1) * share], axes, [(i, i ^ k * unit)...  6.97 us
    ppermute x6, starting transfers between devices, body(): lax.ppermute(pieces[k * share:(k + 1) * share], axes, [(i, i ^ k * unit)...  5.76 us
    pallas_call x1, Pallas kernels, finish(): pl.pallas_call(functools.partial(finish_kernel, block_columns, radices),...  3.36 us
    reshape x8, local copies, waits for them, and re-layouts, body(): block_at[d][requests:].reshape(requests, heads_here, rope_size)  2.54 us
    unnamed x7, other arithmetic  1.66 us
  transfers between devices with their start and end apart: 20, of which 15 were waited for; matrix products, arithmetic and copies ran while one was open for 4% of the time, Pallas kernels for 1%

profile of v4, /device:TPU:0, one launch (start us, length us, event | category | flops | bytes accessed | tf_op | source)
XLA Modules:
  0.0 80.3 jit_solution(16186116850749067829)
XLA Ops:
  0.0 1.2 %copy-done = bf16[8,128,512]{2,1,0:T(8,128)(2,1)S(1)} copy-done((bf16[8,128,512]{2,1,0:T(8,128)(2,1)S(1)}, bf16[8,128,512]{2,1,0:T(8,128)(2,1)}, u32[]{:S(2)}) %copy-start) | copy-done | bytes 1048600
  2.4 3.0 %collective-permute-start = (bf16[18,8,512]{2,1,0:T(8,128)(2,1)S(1)}, bf16[18,8,512]{2,1,0:T(8,128)(2,1)S(1)}, u32[]{:S(2)}, u32[]{:S(2)}) collective-permute-start(bf16[18,8,512]{2,1,0:T(8,128)(2,1)S(1)} %pad_maximum_fusion), channel_id=1, source_target_pairs={{0,2},{2,0},{4,6},{6,4},{8,10},{10,8},{12,14},{14,12},{1,3},{3,1},... | collective-permute-start | bytes 442376 | tf_op jit(solution)/shard_map/ppermute | solution.py:306
  5.4 3.6 %collective-permute-start.5 = (bf16[18,8,512]{2,1,0:T(8,128)(2,1)S(1)}, bf16[18,8,512]{2,1,0:T(8,128)(2,1)S(1)}, u32[]{:S(2)}, u32[]{:S(2)}) collective-permute-start(bf16[18,8,512]{2,1,0:T(8,128)(2,1)S(1)} %pad_maximum_fusion), channel_id=1, source_target_pairs={{0,12},{2,14},{4,8},{6,10},{8,4},{10,6},{12,0},{14,2},{1,13},{3,15... | collective-permute-start | bytes 442376 | tf_op jit(solution)/shard_map/ppermute | solution.py:306
  10.0 4.0 %collective-permute-done.5 = bf16[18,8,512]{2,1,0:T(8,128)(2,1)S(1)} collective-permute-done((bf16[18,8,512]{2,1,0:T(8,128)(2,1)S(1)}, bf16[18,8,512]{2,1,0:T(8,128)(2,1)S(1)}, u32[]{:S(2)}, u32[]{:S(2)}) %collective-permute-start.5) | collective-permute-done | bytes 147488 | tf_op jit(solution)/shard_map/ppermute | solution.py:306
  14.3 6.9 %collective-permute-done.3 = bf16[18,8,512]{2,1,0:T(8,128)(2,1)S(1)} collective-permute-done((bf16[18,8,512]{2,1,0:T(8,128)(2,1)S(1)}, bf16[18,8,512]{2,1,0:T(8,128)(2,1)S(1)}, u32[]{:S(2)}, u32[]{:S(2)}) %collective-permute-start.3) | collective-permute-done | bytes 147488 | tf_op jit(solution)/shard_map/ppermute | solution.py:306
  21.7 1.5 %collective-permute-start.2 = (bf16[18,8,512]{2,1,0:T(8,128)(2,1)S(1)}, bf16[18,8,512]{2,1,0:T(8,128)(2,1)S(1)}, u32[]{:S(2)}, u32[]{:S(2)}) collective-permute-start(bf16[18,8,512]{2,1,0:T(8,128)(2,1)S(1)} %collective-permute-done.1), channel_id=1, source_target_pairs={{0,2},{2,0},{4,6},{6,4},{8,10},{10,8},{12,14},{14,12},{1,3},{3,1},... | collective-permute-start | bytes 442376 | tf_op jit(solution)/shard_map/ppermute | solution.py:306
  26.3 1.3 %collective-permute-done.4 = bf16[18,8,512]{2,1,0:T(8,128)(2,1)S(1)} collective-permute-done((bf16[18,8,512]{2,1,0:T(8,128)(2,1)S(1)}, bf16[18,8,512]{2,1,0:T(8,128)(2,1)S(1)}, u32[]{:S(2)}, u32[]{:S(2)}) %collective-permute-start.4) | collective-permute-done | bytes 147488 | tf_op jit(solution)/shard_map/ppermute | solution.py:306
  27.7 1.5 %collective-permute-done.2 = bf16[18,8,512]{2,1,0:T(8,128)(2,1)S(1)} collective-permute-done((bf16[18,8,512]{2,1,0:T(8,128)(2,1)S(1)}, bf16[18,8,512]{2,1,0:T(8,128)(2,1)S(1)}, u32[]{:S(2)}, u32[]{:S(2)}) %collective-permute-start.2) | collective-permute-done | bytes 147488 | tf_op jit(solution)/shard_map/ppermute | solution.py:306
  30.3 14.9 %attend.1 = (bf16[17,8,512]{2,1,0:T(8,128)(2,1)S(1)}, bf16[17,8,512]{2,1,0:T(8,128)(2,1)S(1)}, bf16[17,8,512]{2,1,0:T(8,128)(2,1)S(1)}, bf16[17,8,512]{2,1,0:T(8...) custom-call(s32[224]{0:T(256)S(1)} %copy-done.2, ...), custom_call_target="tpu_custom_call" | custom-call | flops 7985954816 | bytes 16515072 | tf_op jit(solution)/shard_map/attend/pallas_call | solution.py:170
  45.9 1.5 %collective-permute-start.10 = (bf16[17,8,512]{2,1,0:T(8,128)(2,1)S(1)}, bf16[17,8,512]{2,1,0:T(8,128)(2,1)S(1)}, u32[]{:S(2)}, u32[]{:S(2)}) collective-permute-start(bf16[17,8,512]{2,1,0:T(8,128)(2,1)S(1)} %get-tuple-element.24), channel_id=1, source_target_pairs={{0,2},{2,0},{4,6},{6,4},{8,10},{10,8},{12,14},{14,12},{1,3},{3,1},... | collective-permute-start | bytes 417800 | tf_op jit(solution)/shard_map/ppermute | solution.py:306
  47.9 1.5 %collective-permute-start.7 = (bf16[17,8,512]{2,1,0:T(8,128)(2,1)S(1)}, bf16[17,8,512]{2,1,0:T(8,128)(2,1)S(1)}, u32[]{:S(2)}, u32[]{:S(2)}) collective-permute-start(bf16[17,8,512]{2,1,0:T(8,128)(2,1)S(1)} %get-tuple-element.20), channel_id=1, source_target_pairs={{0,2},{2,0},{4,6},{6,4},{8,10},{10,8},{12,14},{14,12},{1,3},{3,1},... | collective-permute-start | bytes 417800 | tf_op jit(solution)/shard_map/ppermute | solution.py:306
  49.4 2.6 %collective-permute-done.8.got_ref = bf16[17,8,512]{2,1,0:T(8,128)(2,1)S(1)} collective-permute-done((bf16[17,8,512]{2,1,0:T(8,128)(2,1)S(1)}, bf16[17,8,512]{2,1,0:T(8,128)(2,1)S(1)}, u32[]{:S(2)}, u32[]{:S(2)}) %collective-permute-start.8) | collective-permute-done | bytes 139296 | tf_op jit(solution)/shard_map/ppermute | solution.py:306
  53.0 1.9 %collective-permute-done.10.got_ref = bf16[17,8,512]{2,1,0:T(8,128)(2,1)S(1)} collective-permute-done((bf16[17,8,512]{2,1,0:T(8,128)(2,1)S(1)}, bf16[17,8,512]{2,1,0:T(8,128)(2,1)S(1)}, u32[]{:S(2)}, u32[]{:S(2)}) %collective-permute-start.10) | collective-permute-done | bytes 139296 | tf_op jit(solution)/shard_map/ppermute | solution.py:306
  55.0 1.6 %collective-permute-start.11 = (bf16[17,8,512]{2,1,0:T(8,128)(2,1)S(1)}, bf16[17,8,512]{2,1,0:T(8,128)(2,1)S(1)}, u32[]{:S(2)}, u32[]{:S(2)}) collective-permute-start(bf16[17,8,512]{2,1,0:T(8,128)(2,1)S(1)} %merge.4), channel_id=1, source_target_pairs={{0,12},{2,14},{4,8},{6,10},{8,4},{10,6},{12,0},{14,2},{1,13},{3,15... | collective-permute-start | bytes 417800 | tf_op jit(solution)/shard_map/ppermute | solution.py:306
  58.0 1.5 %collective-permute-done.9.refs_2_ = bf16[17,8,512]{2,1,0:T(8,128)(2,1)S(1)} collective-permute-done((bf16[17,8,512]{2,1,0:T(8,128)(2,1)S(1)}, bf16[17,8,512]{2,1,0:T(8,128)(2,1)S(1)}, u32[]{:S(2)}, u32[]{:S(2)}) %collective-permute-start.9) | collective-permute-done | bytes 139296 | tf_op jit(solution)/shard_map/ppermute | solution.py:306
  59.6 2.5 %collective-permute-done.11.refs_3_ = bf16[17,8,512]{2,1,0:T(8,128)(2,1)S(1)} collective-permute-done((bf16[17,8,512]{2,1,0:T(8,128)(2,1)S(1)}, bf16[17,8,512]{2,1,0:T(8,128)(2,1)S(1)}, u32[]{:S(2)}, u32[]{:S(2)}) %collective-permute-start.11) | collective-permute-done | bytes 139296 | tf_op jit(solution)/shard_map/ppermute | solution.py:306
  62.1 1.3 %collective-permute-done.13.refs_4_ = bf16[17,8,512]{2,1,0:T(8,128)(2,1)S(1)} collective-permute-done((bf16[17,8,512]{2,1,0:T(8,128)(2,1)S(1)}, bf16[17,8,512]{2,1,0:T(8,128)(2,1)S(1)}, u32[]{:S(2)}, u32[]{:S(2)}) %collective-permute-start.13) | collective-permute-done | bytes 139296 | tf_op jit(solution)/shard_map/ppermute | solution.py:306
  63.4 3.4 %finish.1 = bf16[16,16,448]{2,1,0:T(8,128)(2,1)S(1)} custom-call(s32[1]{0:T(128)} %bitcast.2.here_ref, bf16[8,512,128]{2,1,0:T(8,128)(2,1)S(1)} %copy-done.1, bf16[1024,7168]{1,0:T(8,128)(2,1)S(1)} %get-tuple-element.18.weight_ref, bf16[17,8,512]{2,1,0:T(8,128)(2,1)S(1)} %get-tuple-element.19.refs_0_, ...), custom_call_target="tpu_custom_call" | custom-call | flops 3758096384 | tf_op jit(solution)/shard_map/finish/pallas_call | solution.py:277
  67.7 1.4 %collective-permute-start.15 = (bf16[4,16,448]{2,1,0:T(8,128)(2,1)S(1)}, bf16[4,16,448]{2,1,0:T(8,128)(2,1)S(1)}, u32[]{:S(2)}, u32[]{:S(2)}) collective-permute-start(bf16[4,16,448]{2,1,0:T(8,128)(2,1)S(1)} %get-tuple-element.29), channel_id=1, source_target_pairs={{0,2},{1,3},{2,0},{3,1},{4,6},{5,7},{6,4},{7,5},{8,10},{9,11},{10,... | collective-permute-start | bytes 172040 | tf_op jit(solution)/shard_map/ppermute | solution.py:356
  69.1 1.7 %collective-permute-done.16 = bf16[4,16,448]{2,1,0:T(8,128)(2,1)S(1)} collective-permute-done((bf16[4,16,448]{2,1,0:T(8,128)(2,1)S(1)}, bf16[4,16,448]{2,1,0:T(8,128)(2,1)S(1)}, u32[]{:S(2)}, u32[]{:S(2)}) %collective-permute-start.16) | collective-permute-done | bytes 57376 | tf_op jit(solution)/shard_map/ppermute | solution.py:356
  70.8 2.0 %collective-permute-done.15 = bf16[4,16,448]{2,1,0:T(8,128)(2,1)S(1)} collective-permute-done((bf16[4,16,448]{2,1,0:T(8,128)(2,1)S(1)}, bf16[4,16,448]{2,1,0:T(8,128)(2,1)S(1)}, u32[]{:S(2)}, u32[]{:S(2)}) %collective-permute-start.15) | collective-permute-done | bytes 57376 | tf_op jit(solution)/shard_map/ppermute | solution.py:356
  72.9 2.1 %collective-permute-start.19 = (bf16[1,16,448]{2,1,0:T(8,128)(2,1)S(1)}, bf16[1,16,448]{2,1,0:T(8,128)(2,1)S(1)}, u32[]{:S(2)}, u32[]{:S(2)}) collective-permute-start(bf16[1,16,448]{2,1,0:T(8,128)(2,1)S(1)} %get-tuple-element.31), channel_id=1, source_target_pairs={{0,12},{1,13},{2,14},{3,15},{4,8},{5,9},{6,10},{7,11},{8,4},{9,5},... | collective-permute-start | bytes 43016 | tf_op jit(solution)/shard_map/ppermute | solution.py:356
  75.0 1.4 %collective-permute-start.18 = (bf16[1,16,448]{2,1,0:T(8,128)(2,1)S(1)}, bf16[1,16,448]{2,1,0:T(8,128)(2,1)S(1)}, u32[]{:S(2)}, u32[]{:S(2)}) collective-permute-start(bf16[1,16,448]{2,1,0:T(8,128)(2,1)S(1)} %get-tuple-element.32), channel_id=1, source_target_pairs={{0,8},{1,9},{2,10},{3,11},{4,12},{5,13},{6,14},{7,15},{8,0},{9,1},... | collective-permute-start | bytes 43016 | tf_op jit(solution)/shard_map/ppermute | solution.py:356
  76.6 1.9 %collective-permute-done.19 = bf16[1,16,448]{2,1,0:T(8,128)(2,1)S(1)} collective-permute-done((bf16[1,16,448]{2,1,0:T(8,128)(2,1)S(1)}, bf16[1,16,448]{2,1,0:T(8,128)(2,1)S(1)}, u32[]{:S(2)}, u32[]{:S(2)}) %collective-permute-start.19) | collective-permute-done | bytes 14368 | tf_op jit(solution)/shard_map/ppermute | solution.py:356
  (70 shorter events, 13.7 us)
Async XLA Ops:
  0.0 2.3 %copy-start.4 = (bf16[16,512]{1,0:T(8,128)(2,1)S(1)}, bf16[16,512]{1,0:T(8,128)(2,1)}, u32[]{:S(2)}) copy-start(bf16[16,512]{1,0:T(8,128)(2,1)} %param.8) | copy-start | bytes 49156
  2.4 7.6 %collective-permute-start = (bf16[18,8,512]{2,1,0:T(8,128)(2,1)S(1)}, bf16[18,8,512]{2,1,0:T(8,128)(2,1)S(1)}, u32[]{:S(2)}, u32[]{:S(2)}) collective-permute-start(bf16[18,8,512]{2,1,0:T(8,128)(2,1)S(1)} %pad_maximum_fusion), channel_id=1, source_target_pairs={{0,2},{2,0},{4,6},{6,4},{8,10},{10,8},{12,14},{14,12},{1,3},{3,1},... | collective-permute-start | bytes 442376 | tf_op jit(solution)/shard_map/ppermute | solution.py:306
  5.4 8.6 %collective-permute-start.5 = (bf16[18,8,512]{2,1,0:T(8,128)(2,1)S(1)}, bf16[18,8,512]{2,1,0:T(8,128)(2,1)S(1)}, u32[]{:S(2)}, u32[]{:S(2)}) collective-permute-start(bf16[18,8,512]{2,1,0:T(8,128)(2,1)S(1)} %pad_maximum_fusion), channel_id=1, source_target_pairs={{0,12},{2,14},{4,8},{6,10},{8,4},{10,6},{12,0},{14,2},{1,13},{3,15... | collective-permute-start | bytes 442376 | tf_op jit(solution)/shard_map/ppermute | solution.py:306
  9.0 12.2 %collective-permute-start.3 = (bf16[18,8,512]{2,1,0:T(8,128)(2,1)S(1)}, bf16[18,8,512]{2,1,0:T(8,128)(2,1)S(1)}, u32[]{:S(2)}, u32[]{:S(2)}) collective-permute-start(bf16[18,8,512]{2,1,0:T(8,128)(2,1)S(1)} %pad_maximum_fusion), channel_id=1, source_target_pairs={{0,8},{2,10},{4,12},{6,14},{8,0},{10,2},{12,4},{14,6},{1,9},{3,11}... | collective-permute-start | bytes 442376 | tf_op jit(solution)/shard_map/ppermute | solution.py:306
  9.0 12.7 %collective-permute-start.1 = (bf16[18,8,512]{2,1,0:T(8,128)(2,1)S(1)}, bf16[18,8,512]{2,1,0:T(8,128)(2,1)S(1)}, u32[]{:S(2)}, u32[]{:S(2)}) collective-permute-start(bf16[18,8,512]{2,1,0:T(8,128)(2,1)S(1)} %pad_maximum_fusion), channel_id=1, source_target_pairs={{0,4},{2,6},{4,0},{6,2},{8,12},{10,14},{12,8},{14,10},{1,5},{3,7},... | collective-permute-start | bytes 442376 | tf_op jit(solution)/shard_map/ppermute | solution.py:306
  14.0 11.6 %collective-permute-start.6 = (bf16[18,8,512]{2,1,0:T(8,128)(2,1)S(1)}, bf16[18,8,512]{2,1,0:T(8,128)(2,1)S(1)}, u32[]{:S(2)}, u32[]{:S(2)}) collective-permute-start(bf16[18,8,512]{2,1,0:T(8,128)(2,1)S(1)} %collective-permute-done.5), channel_id=1, source_target_pairs={{0,2},{2,0},{4,6},{6,4},{8,10},{10,8},{12,14},{14,12},{1,3},{3,1},... | collective-permute-start | bytes 442376 | tf_op jit(solution)/shard_map/ppermute | solution.py:306
  21.2 6.4 %collective-permute-start.4 = (bf16[18,8,512]{2,1,0:T(8,128)(2,1)S(1)}, bf16[18,8,512]{2,1,0:T(8,128)(2,1)S(1)}, u32[]{:S(2)}, u32[]{:S(2)}) collective-permute-start(bf16[18,8,512]{2,1,0:T(8,128)(2,1)S(1)} %collective-permute-done.3), channel_id=1, source_target_pairs={{0,2},{2,0},{4,6},{6,4},{8,10},{10,8},{12,14},{14,12},{1,3},{3,1},... | collective-permute-start | bytes 442376 | tf_op jit(solution)/shard_map/ppermute | solution.py:306
  21.7 7.5 %collective-permute-start.2 = (bf16[18,8,512]{2,1,0:T(8,128)(2,1)S(1)}, bf16[18,8,512]{2,1,0:T(8,128)(2,1)S(1)}, u32[]{:S(2)}, u32[]{:S(2)}) collective-permute-start(bf16[18,8,512]{2,1,0:T(8,128)(2,1)S(1)} %collective-permute-done.1), channel_id=1, source_target_pairs={{0,2},{2,0},{4,6},{6,4},{8,10},{10,8},{12,14},{14,12},{1,3},{3,1},... | collective-permute-start | bytes 442376 | tf_op jit(solution)/shard_map/ppermute | solution.py:306
  25.6 4.7 %copy-start.2 = (s32[224]{0:T(256)S(1)}, s32[224]{0:T(256)}, u32[]{:S(2)}) copy-start(s32[224]{0:T(256)} %owner_ref.1) | copy-start | bytes 2692
  27.6 2.6 %copy-start.3 = (bf16[16,8,64]{2,1,0:T(8,128)(2,1)S(1)}, bf16[16,8,64]{2,1,0:T(8,128)(2,1)}, u32[]{:S(2)}) copy-start(bf16[16,8,64]{2,1,0:T(8,128)(2,1)} %reshape.39) | copy-start | bytes 49156
  45.2 18.2 %copy-start.1 = (bf16[8,512,128]{2,1,0:T(8,128)(2,1)S(1)}, bf16[8,512,128]{2,1,0:T(8,128)(2,1)}, u32[]{:S(2)}) copy-start(bf16[8,512,128]{2,1,0:T(8,128)(2,1)} %value_ref.1) | copy-start | bytes 3145732
  45.2 6.7 %collective-permute-start.8 = (bf16[17,8,512]{2,1,0:T(8,128)(2,1)S(1)}, bf16[17,8,512]{2,1,0:T(8,128)(2,1)S(1)}, u32[]{:S(2)}, u32[]{:S(2)}) collective-permute-start(bf16[17,8,512]{2,1,0:T(8,128)(2,1)S(1)} %get-tuple-element.22), channel_id=1, source_target_pairs={{0,2},{2,0},{4,6},{6,4},{8,10},{10,8},{12,14},{14,12},{1,3},{3,1},... | collective-permute-start | bytes 417800 | tf_op jit(solution)/shard_map/ppermute | solution.py:306
  45.9 9.0 %collective-permute-start.10 = (bf16[17,8,512]{2,1,0:T(8,128)(2,1)S(1)}, bf16[17,8,512]{2,1,0:T(8,128)(2,1)S(1)}, u32[]{:S(2)}, u32[]{:S(2)}) collective-permute-start(bf16[17,8,512]{2,1,0:T(8,128)(2,1)S(1)} %get-tuple-element.24), channel_id=1, source_target_pairs={{0,2},{2,0},{4,6},{6,4},{8,10},{10,8},{12,14},{14,12},{1,3},{3,1},... | collective-permute-start | bytes 417800 | tf_op jit(solution)/shard_map/ppermute | solution.py:306
  47.3 9.3 %collective-permute-start.12 = (bf16[17,8,512]{2,1,0:T(8,128)(2,1)S(1)}, bf16[17,8,512]{2,1,0:T(8,128)(2,1)S(1)}, u32[]{:S(2)}, u32[]{:S(2)}) collective-permute-start(bf16[17,8,512]{2,1,0:T(8,128)(2,1)S(1)} %get-tuple-element.26), channel_id=1, source_target_pairs={{0,2},{2,0},{4,6},{6,4},{8,10},{10,8},{12,14},{14,12},{1,3},{3,1},... | collective-permute-start | bytes 417800 | tf_op jit(solution)/shard_map/ppermute | solution.py:306
  47.9 10.1 %collective-permute-start.7 = (bf16[17,8,512]{2,1,0:T(8,128)(2,1)S(1)}, bf16[17,8,512]{2,1,0:T(8,128)(2,1)S(1)}, u32[]{:S(2)}, u32[]{:S(2)}) collective-permute-start(bf16[17,8,512]{2,1,0:T(8,128)(2,1)S(1)} %get-tuple-element.20), channel_id=1, source_target_pairs={{0,2},{2,0},{4,6},{6,4},{8,10},{10,8},{12,14},{14,12},{1,3},{3,1},... | collective-permute-start | bytes 417800 | tf_op jit(solution)/shard_map/ppermute | solution.py:306
  52.1 7.5 %collective-permute-start.9 = (bf16[17,8,512]{2,1,0:T(8,128)(2,1)S(1)}, bf16[17,8,512]{2,1,0:T(8,128)(2,1)S(1)}, u32[]{:S(2)}, u32[]{:S(2)}) collective-permute-start(bf16[17,8,512]{2,1,0:T(8,128)(2,1)S(1)} %merge.3), channel_id=1, source_target_pairs={{0,8},{2,10},{4,12},{6,14},{8,0},{10,2},{12,4},{14,6},{1,9},{3,11}... | collective-permute-start | bytes 417800 | tf_op jit(solution)/shard_map/ppermute | solution.py:306
  55.0 7.1 %collective-permute-start.11 = (bf16[17,8,512]{2,1,0:T(8,128)(2,1)S(1)}, bf16[17,8,512]{2,1,0:T(8,128)(2,1)S(1)}, u32[]{:S(2)}, u32[]{:S(2)}) collective-permute-start(bf16[17,8,512]{2,1,0:T(8,128)(2,1)S(1)} %merge.4), channel_id=1, source_target_pairs={{0,12},{2,14},{4,8},{6,10},{8,4},{10,6},{12,0},{14,2},{1,13},{3,15... | collective-permute-start | bytes 417800 | tf_op jit(solution)/shard_map/ppermute | solution.py:306
  56.8 6.6 %collective-permute-start.13 = (bf16[17,8,512]{2,1,0:T(8,128)(2,1)S(1)}, bf16[17,8,512]{2,1,0:T(8,128)(2,1)S(1)}, u32[]{:S(2)}, u32[]{:S(2)}) collective-permute-start(bf16[17,8,512]{2,1,0:T(8,128)(2,1)S(1)} %merge.5), channel_id=1, source_target_pairs={{0,4},{2,6},{4,0},{6,2},{8,12},{10,14},{12,8},{14,10},{1,5},{3,7},... | collective-permute-start | bytes 417800 | tf_op jit(solution)/shard_map/ppermute | solution.py:306
  66.8 2.2 %collective-permute-start.14 = (bf16[4,16,448]{2,1,0:T(8,128)(2,1)S(1)}, bf16[4,16,448]{2,1,0:T(8,128)(2,1)S(1)}, u32[]{:S(2)}, u32[]{:S(2)}) collective-permute-start(bf16[4,16,448]{2,1,0:T(8,128)(2,1)S(1)} %get-tuple-element.27), channel_id=1, source_target_pairs={{0,1},{1,0},{2,3},{3,2},{4,5},{5,4},{6,7},{7,6},{8,9},{9,8},{10,11... | collective-permute-start | bytes 172040 | tf_op jit(solution)/shard_map/ppermute | solution.py:356
  66.9 3.9 %collective-permute-start.16 = (bf16[4,16,448]{2,1,0:T(8,128)(2,1)S(1)}, bf16[4,16,448]{2,1,0:T(8,128)(2,1)S(1)}, u32[]{:S(2)}, u32[]{:S(2)}) collective-permute-start(bf16[4,16,448]{2,1,0:T(8,128)(2,1)S(1)} %get-tuple-element.28), channel_id=1, source_target_pairs={{0,3},{1,2},{2,1},{3,0},{4,7},{5,6},{6,5},{7,4},{8,11},{9,10},{10,... | collective-permute-start | bytes 172040 | tf_op jit(solution)/shard_map/ppermute | solution.py:356
  67.7 5.1 %collective-permute-start.15 = (bf16[4,16,448]{2,1,0:T(8,128)(2,1)S(1)}, bf16[4,16,448]{2,1,0:T(8,128)(2,1)S(1)}, u32[]{:S(2)}, u32[]{:S(2)}) collective-permute-start(bf16[4,16,448]{2,1,0:T(8,128)(2,1)S(1)} %get-tuple-element.29), channel_id=1, source_target_pairs={{0,2},{1,3},{2,0},{3,1},{4,6},{5,7},{6,4},{7,5},{8,10},{9,11},{10,... | collective-permute-start | bytes 172040 | tf_op jit(solution)/shard_map/ppermute | solution.py:356
  72.8 3.8 %collective-permute-start.17 = (bf16[1,16,448]{2,1,0:T(8,128)(2,1)S(1)}, bf16[1,16,448]{2,1,0:T(8,128)(2,1)S(1)}, u32[]{:S(2)}, u32[]{:S(2)}) collective-permute-start(bf16[1,16,448]{2,1,0:T(8,128)(2,1)S(1)} %get-tuple-element.30), channel_id=1, source_target_pairs={{0,4},{1,5},{2,6},{3,7},{4,0},{5,1},{6,2},{7,3},{8,12},{9,13},{10,... | collective-permute-start | bytes 43016 | tf_op jit(solution)/shard_map/ppermute | solution.py:356
  72.9 5.6 %collective-permute-start.19 = (bf16[1,16,448]{2,1,0:T(8,128)(2,1)S(1)}, bf16[1,16,448]{2,1,0:T(8,128)(2,1)S(1)}, u32[]{:S(2)}, u32[]{:S(2)}) collective-permute-start(bf16[1,16,448]{2,1,0:T(8,128)(2,1)S(1)} %get-tuple-element.31), channel_id=1, source_target_pairs={{0,12},{1,13},{2,14},{3,15},{4,8},{5,9},{6,10},{7,11},{8,4},{9,5},... | collective-permute-start | bytes 43016 | tf_op jit(solution)/shard_map/ppermute | solution.py:356
  75.0 4.6 %collective-permute-start.18 = (bf16[1,16,448]{2,1,0:T(8,128)(2,1)S(1)}, bf16[1,16,448]{2,1,0:T(8,128)(2,1)S(1)}, u32[]{:S(2)}, u32[]{:S(2)}) collective-permute-start(bf16[1,16,448]{2,1,0:T(8,128)(2,1)S(1)} %get-tuple-element.32), channel_id=1, source_target_pairs={{0,8},{1,9},{2,10},{3,11},{4,12},{5,13},{6,14},{7,15},{8,0},{9,1},... | collective-permute-start | bytes 43016 | tf_op jit(solution)/shard_map/ppermute | solution.py:356
  (1 other events, 1.2 us)

commit v5 on v4

--- a/solution.py
+++ b/solution.py
@@ -10,6 +10,7 @@
 masked_score = -1e30
 LANES = 128
 GROUP_PAGES = 4
+CACHE_PARTS = 2
 MIB = 1024 * 1024
 
 VMEM_SPEC = pl.BlockSpec(memory_space=pltpu.VMEM)
@@ -40,28 +41,54 @@
     return (parts[0] + parts[1]) + parts[2]
 
 
-def attend_kernel(score_scale, chunks, blocks, owner_ref, query_ref, cache_ref, weight_ref, *refs):
-    message_refs = refs[:blocks]
-    (
-        weight_out, cache_scr, score_scr, max_scr, total_scr, sum_scr, cache_sem, weight_sem
-    ) = refs[blocks:]
-    requests, heads, entry_size = query_ref.shape
-    pages, page_len, _ = cache_ref.shape
+def load_kernel(first, cache_ref, after_ref, out_ref, sem):
+    copy = pltpu.make_async_copy(cache_ref.at[pl.ds(first, out_ref.shape[0])], out_ref, sem)
+    copy.start()
+    copy.wait()
+
+
+def load(cache, part, parts, after):
+    pages = cache.shape[0] // parts
+    return pl.pallas_call(
+        functools.partial(load_kernel, part * pages),
+        out_shape=pltpu.VMEM((pages, *cache.shape[1:]), cache.dtype),
+        in_specs=[pl.BlockSpec(memory_space=pltpu.HBM), pl.BlockSpec(memory_space=pl.ANY)],
+        out_specs=VMEM_SPEC,
+        scratch_shapes=[pltpu.SemaphoreType.DMA],
+        compiler_params=pltpu.CompilerParams(vmem_limit_bytes=MIB),
+        cost_estimate=pl.CostEstimate(
+            flops=0, bytes_accessed=2 * cache.size // parts, transcendentals=0
+        ),
+        name="load",
+    )(pltpu.with_memory_space_constraint(cache, pltpu.HBM), after)
+
+
+def attend_kernel(score_scale, steps, blocks, owner_ref, weight_ref, *refs):
+    cache_refs, refs = refs[:CACHE_PARTS], refs[CACHE_PARTS:]
+    query_refs, message_refs = refs[:blocks], refs[blocks : 2 * blocks]
+    weight_out, query_scr, score_scr, max_scr, total_scr, sum_scr, weight_sem = refs[2 * blocks :]
+    requests, heads, entry_size = query_scr.shape
+    pages_part, page_len, _ = cache_refs[0].shape
     _, heads_here, latent_size = message_refs[0].shape
+    rope_size = entry_size - latent_size
+    ropes_row = latent_size // rope_size
     pair_len = 2 * page_len
     pair_count = GROUP_PAGES // 2
-    groups_chunk = pages // GROUP_PAGES // chunks
-    pages_chunk = pages // chunks
+    groups_part = pages_part // GROUP_PAGES
+    groups_step = groups_part // steps
     group_len = GROUP_PAGES * page_len
 
-    def cache_copy(c):
-        rows = pl.ds(c * pages_chunk, pages_chunk)
-        return pltpu.make_async_copy(cache_ref.at[rows], cache_scr.at[rows], cache_sem.at[c])
-
-    for c in range(chunks):
-        cache_copy(c).start()
     weight_copy = pltpu.make_async_copy(weight_ref, weight_out, weight_sem)
     weight_copy.start()
+
+    for b, ref in enumerate(query_refs):
+        rows = slice(b * heads_here, (b + 1) * heads_here)
+        for r in range(requests):
+            start = r % ropes_row * rope_size
+            query_scr[r, rows, :latent_size] = ref[r]
+            query_scr[r, rows, latent_size:] = ref[requests + r // ropes_row][
+                :, start : start + rope_size
+            ]
 
     first_half = lax.broadcasted_iota(jnp.int32, (heads, pair_len), 1) < page_len
 
@@ -74,11 +101,12 @@
         raw = [owner_ref[g * GROUP_PAGES + k] for k in range(GROUP_PAGES)]
         return [jnp.where(o < 0, requests, o) for o in raw]
 
-    def score_group(g):
+    def score_group(part, local):
+        g = part * groups_part + local
         owners = owners_of(g)
-        keys = cache_scr[pl.ds(g * GROUP_PAGES, GROUP_PAGES)].reshape(group_len, entry_size)
+        keys = cache_refs[part][pl.ds(local * GROUP_PAGES, GROUP_PAGES)].reshape(group_len, entry_size)
         queries = jnp.concatenate(
-            [query_ref[jnp.minimum(o, requests - 1)] for o in owners], axis=0
+            [query_scr[jnp.minimum(o, requests - 1)] for o in owners], axis=0
         )
         scores = lax.dot_general(
             queries, keys, (((1,), (1,)), ((), ())), preferred_element_type=jnp.float32
@@ -99,21 +127,22 @@
                 max_scr[owners[right]], jnp.where(first_half, masked_score, pair)
             )
 
-    def score_chunk(c, carry):
-        cache_copy(c).wait()
-        for i in range(groups_chunk):
-            score_group(c * groups_chunk + i)
+    def score_step(part, c, carry):
+        for i in range(groups_step):
+            score_group(part, c * groups_step + i)
         return carry
 
-    lax.fori_loop(0, chunks, score_chunk, 0)
+    for part in range(CACHE_PARTS):
+        lax.fori_loop(0, steps, functools.partial(score_step, part), 0)
 
     for r in range(requests + 1):
         top = jnp.max(max_scr[r], axis=1, keepdims=True)
         max_scr[r] = jnp.broadcast_to(top, (heads, pair_len))
 
-    def sum_group(g):
+    def sum_group(part, local):
+        g = part * groups_part + local
         owners = owners_of(g)
-        values = cache_scr[pl.ds(g * GROUP_PAGES, GROUP_PAGES)].reshape(group_len, entry_size)[
+        values = cache_refs[part][pl.ds(local * GROUP_PAGES, GROUP_PAGES)].reshape(group_len, entry_size)[
             :, :latent_size
         ]
         rows = []
@@ -135,12 +164,13 @@
         for k in range(GROUP_PAGES):
             sum_scr[owners[k]] += added[k * heads : (k + 1) * heads]
 
-    def sum_chunk(c, carry):
-        for i in range(groups_chunk):
-            sum_group(c * groups_chunk + i)
+    def sum_step(part, c, carry):
+        for i in range(groups_step):
+            sum_group(part, c * groups_step + i)
         return carry
 
-    lax.fori_loop(0, chunks, sum_chunk, 0)
+    for part in range(CACHE_PARTS):
+        lax.fori_loop(0, steps, functools.partial(sum_step, part), 0)
 
     lane = lax.broadcasted_iota(jnp.int32, (heads, LANES), 1)
     stats = jnp.full((heads, LANES), masked_score, jnp.float32)
@@ -159,41 +189,43 @@
     weight_copy.wait()
 
 
-def attend(query_full, latent_cache, page_owner, output_weight, score_scale, latent_size, blocks):
-    requests, heads, entry_size = query_full.shape
-    pages, page_len, _ = latent_cache.shape
-    heads_here = heads // blocks
+def attend(query_blocks, cache_parts, page_owner, output_weight, score_scale, latent_size):
+    pages_part, page_len, entry_size = cache_parts[0].shape
+    pages = pages_part * CACHE_PARTS
+    blocks = len(query_blocks)
+    heads_here = query_blocks[0].shape[1]
+    requests = query_blocks[0].shape[0] * latent_size // entry_size
+    heads = heads_here * blocks
     pair_len = 2 * page_len
-    groups = pages // GROUP_PAGES
-    chunks = groups // max(d for d in range(1, 15) if groups % d == 0)
-    any_spec = pl.BlockSpec(memory_space=pl.ANY)
+    groups = pages_part // GROUP_PAGES
+    steps = groups // max(d for d in range(1, 15) if groups % d == 0)
     out = pl.pallas_call(
-        functools.partial(attend_kernel, score_scale, chunks, blocks),
+        functools.partial(attend_kernel, score_scale, steps, blocks),
         out_shape=[
             pltpu.VMEM((requests + 1, heads_here, latent_size), jnp.bfloat16)
             for _ in range(blocks)
         ]
         + [pltpu.VMEM(output_weight.shape, output_weight.dtype)],
-        in_specs=[SMEM_SPEC, VMEM_SPEC, any_spec, any_spec],
+        in_specs=[SMEM_SPEC, pl.BlockSpec(memory_space=pl.ANY)]
+        + [VMEM_SPEC] * (CACHE_PARTS + blocks),
         out_specs=[VMEM_SPEC] * (blocks + 1),
         scratch_shapes=[
-            pltpu.VMEM(latent_cache.shape, latent_cache.dtype),
+            pltpu.VMEM((requests, heads, entry_size), jnp.bfloat16),
             pltpu.VMEM((pages // 2, heads, pair_len), jnp.float32),
             pltpu.VMEM((requests + 1, heads, pair_len), jnp.float32),
             pltpu.VMEM((requests + 1, heads, pair_len), jnp.float32),
             pltpu.VMEM((requests + 1, heads, latent_size), jnp.float32),
-            pltpu.SemaphoreType.DMA((chunks,)),
             pltpu.SemaphoreType.DMA,
         ],
-        compiler_params=pltpu.CompilerParams(vmem_limit_bytes=34 * MIB),
+        compiler_params=pltpu.CompilerParams(vmem_limit_bytes=16 * MIB),
         cost_estimate=pl.CostEstimate(
             flops=2 * pages * page_len * heads * (entry_size + latent_size) * 4,
             bytes_accessed=pages * page_len * entry_size * 2,
             transcendentals=pages * page_len * heads,
         ),
         name="attend",
-    )(page_owner, in_vmem(query_full), latent_cache, output_weight)
-    return out[:-1], out[-1]
+    )(page_owner, output_weight, *map(in_vmem, [*cache_parts, *query_blocks]))
+    return list(out[:-1]), out[-1]
 
 
 def shares(levels):
@@ -308,40 +340,33 @@
     query_latent = jnp.einsum(
         "rhn,hnl->rhl", query_nope, key_absorb, preferred_element_type=jnp.float32
     ).astype(jnp.bfloat16)
-    own = jnp.concatenate(
-        [query_latent, query_rope.reshape(-1, heads_here, latent_size)], axis=0
+    ropes_row = latent_size // rope_size
+    rope = query_rope.reshape(-1, ropes_row, heads_here, rope_size).transpose(0, 2, 1, 3)
+    own = jnp.concatenate([query_latent, rope.reshape(-1, heads_here, latent_size)], axis=0)
+    own, here = lax.optimization_barrier((own, here))
+
+    bits = [1 << b for b in range(count.bit_length() - 1)]
+    block_at = {0: own}
+    for bit in reversed(bits):
+        for distance in list(block_at):
+            block_at[distance ^ bit] = exchange(block_at[distance], bit)
+
+    cache_parts = [
+        load(latent_cache, i, CACHE_PARTS, block) for i, block in enumerate([own, block_at[bits[-1]]])
+    ]
+    message_to, weight = attend(
+        [block_at[d] for d in range(count)],
+        cache_parts, page_owner, output_weight, score_scale, latent_size,
     )
-    own, here = lax.optimization_barrier((own, here))
-
-    even = [*range(4, count, 2), 2] if count > 2 else []
-    block_at = {0: own}
-    for distance in even:
-        block_at[distance] = exchange(own, distance)
-    for distance in [0, *even]:
-        block_at[distance ^ 1] = exchange(block_at[distance], 1)
-    query_full = jnp.concatenate(
-        [
-            jnp.concatenate(
-                [
-                    block_at[d][:requests],
-                    block_at[d][requests:].reshape(requests, heads_here, rope_size),
-                ],
-                axis=2,
-            )
-            for d in range(count)
-        ],
-        axis=1,
-    )
-
-    message_to, weight = attend(
-        query_full, latent_cache, page_owner, output_weight, score_scale, latent_size, count
-    )
-
-    across = {distance: exchange(message_to[distance ^ 1], 1) for distance in [*even, 0]}
-    arrived = [
-        exchange(merge(message_to[distance], across[distance]), distance) for distance in even
-    ]
-    messages = [message_to[0], across[0], *arrived]
+
+    messages = [message_to[0]]
+    for bit in bits:
+        for distance in range(count - bit, 0, -2 * bit):
+            got = exchange(message_to[distance], bit)
+            if distance == bit:
+                messages.append(got)
+            else:
+                message_to[distance ^ bit] = merge(message_to[distance ^ bit], got)
 
     owners = lax.axis_size(axes)
     radices = []

time: 80.6 us -> 81.4 us (level)
  starting transfers between devices: 22.2 us -> 28.4 us
  waiting for transfers between devices: 31.7 us -> 25.6 us
  Pallas kernels: 18.7 us -> 24 us
  local copies, waits for them, and re-layouts: 4.02 us -> 1.37 us
  other arithmetic: 2.35 us -> 0.67 us
    ppermute x14, waiting for transfers between devices: 24.7 us -> 17.2 us  [exchange(): return lax.ppermute(x, 'ctx', [(i, i ^ distance) for i in range(count)])]
    ppermute x14, starting transfers between devices: 16.5 us -> 22.5 us  [exchange(): return lax.ppermute(x, 'ctx', [(i, i ^ distance) for i in range(count)])]
    pallas_call x1 -> x3, Pallas kernels: 14.9 us -> 20.1 us  [the longest x1 12.9 us: attend(): pl.pallas_call(functools.partial(attend_kernel, score_scale, steps, block...]
    unnamed x7 -> x0, other arithmetic: 1.66 us -> none
    reshape x8 -> x3, local copies, waits for them, and re-layouts: 2.54 us -> 1.01 us  [the longest x2 0.91 us: body(): query_rope.reshape(-1, ropes_row, heads_here, rope_size)]
    ppermute x6, waiting for transfers between devices: 6.97 us -> 8.4 us  [body(): lax.ppermute(pieces[k * share:(k + 1) * share], axes, [(i, i ^ k * unit)...]
    unnamed x10 -> x8, local copies, waits for them, and re-layouts: 1.24 us -> 0.24 us
  transfers between devices with their start and end apart: 20 -> 20, of which waited for: 15 -> 12; matrix products, arithmetic and copies ran while one was open for 4% -> 0% of each run, Pallas kernels for 1% -> 10%
where the time goes in v5:
time: 81.4 us; the launch traced here: 81.2 us
  starting transfers between devices  28.4 us (35%)
  waiting for transfers between devices  25.6 us (31%)
  Pallas kernels  24 us (29%)
  local copies, waits for them, and re-layouts  1.37 us (2%)
  matrix products  0.99 us (1%)
    ppermute x14, starting transfers between devices, exchange(): return lax.ppermute(x, 'ctx', [(i, i ^ distance) for i in range(count)])  22.5 us
    ppermute x14, waiting for transfers between devices, exchange(): return lax.ppermute(x, 'ctx', [(i, i ^ distance) for i in range(count)])  17.2 us
    pallas_call x1, Pallas kernels, attend(): pl.pallas_call(functools.partial(attend_kernel, score_scale, steps, block...  12.9 us
    ppermute x6, waiting for transfers between devices, body(): lax.ppermute(pieces[k * share:(k + 1) * share], axes, [(i, i ^ k * unit)...  8.4 us
    pallas_call x2, Pallas kernels, load(): pl.pallas_call(functools.partial(load_kernel, part * pages), out_shape=pl...  7.23 us
    ppermute x6, starting transfers between devices, body(): lax.ppermute(pieces[k * share:(k + 1) * share], axes, [(i, i ^ k * unit)...  5.89 us
    pallas_call x1, Pallas kernels, finish(): pl.pallas_call(functools.partial(finish_kernel, block_columns, radices),...  3.33 us
  transfers between devices with their start and end apart: 20, of which 12 were waited for; matrix products, arithmetic and copies ran while one was open for 0% of the time, Pallas kernels for 10%

profile of v5, /device:TPU:0, one launch (start us, length us, event | category | flops | bytes accessed | tf_op | source)
XLA Modules:
  0.0 81.2 jit_solution(8474221878063937879)
XLA Ops:
  2.4 4.1 %collective-permute-start = (bf16[18,8,512]{2,1,0:T(8,128)(2,1)S(1)}, bf16[18,8,512]{2,1,0:T(8,128)(2,1)S(1)}, u32[]{:S(2)}, u32[]{:S(2)}) collective-permute-start(bf16[18,8,512]{2,1,0:T(8,128)(2,1)S(1)} %pad_maximum_fusion.after_ref.refs_2_), channel_id=1, source_target_pairs={{0,8},{2,10},{4,12},{6,14},{8,0},{10,2},{12,4},{14,6},{1,9},{3,11}... | collective-permute-start | bytes 442376 | tf_op jit(solution)/shard_map/ppermute | solution.py:338
  6.5 1.6 %collective-permute-start.2 = (bf16[18,8,512]{2,1,0:T(8,128)(2,1)S(1)}, bf16[18,8,512]{2,1,0:T(8,128)(2,1)S(1)}, u32[]{:S(2)}, u32[]{:S(2)}) collective-permute-start(bf16[18,8,512]{2,1,0:T(8,128)(2,1)S(1)} %pad_maximum_fusion.after_ref.refs_2_), channel_id=1, source_target_pairs={{0,4},{2,6},{4,0},{6,2},{8,12},{10,14},{12,8},{14,10},{1,5},{3,7},... | collective-permute-start | bytes 442376 | tf_op jit(solution)/shard_map/ppermute | solution.py:338
  8.0 5.5 %collective-permute-done.after_ref.refs_6_ = bf16[18,8,512]{2,1,0:T(8,128)(2,1)S(1)} collective-permute-done((bf16[18,8,512]{2,1,0:T(8,128)(2,1)S(1)}, bf16[18,8,512]{2,1,0:T(8,128)(2,1)S(1)}, u32[]{:S(2)}, u32[]{:S(2)}) %collective-permute-start) | collective-permute-done | bytes 147488 | tf_op jit(solution)/shard_map/ppermute | solution.py:338
  14.2 1.5 %collective-permute-start.1 = (bf16[18,8,512]{2,1,0:T(8,128)(2,1)S(1)}, bf16[18,8,512]{2,1,0:T(8,128)(2,1)S(1)}, u32[]{:S(2)}, u32[]{:S(2)}) collective-permute-start(bf16[18,8,512]{2,1,0:T(8,128)(2,1)S(1)} %pad_maximum_fusion.after_ref.refs_2_), channel_id=1, source_target_pairs={{0,2},{2,0},{4,6},{6,4},{8,10},{10,8},{12,14},{14,12},{1,3},{3,1},... | collective-permute-start | bytes 442376 | tf_op jit(solution)/shard_map/ppermute | solution.py:338
  16.2 1.5 %collective-permute-start.3 = (bf16[18,8,512]{2,1,0:T(8,128)(2,1)S(1)}, bf16[18,8,512]{2,1,0:T(8,128)(2,1)S(1)}, u32[]{:S(2)}, u32[]{:S(2)}) collective-permute-start(bf16[18,8,512]{2,1,0:T(8,128)(2,1)S(1)} %collective-permute-done.2.refs_4_), channel_id=1, source_target_pairs={{0,2},{2,0},{4,6},{6,4},{8,10},{10,8},{12,14},{14,12},{1,3},{3,1},... | collective-permute-start | bytes 442376 | tf_op jit(solution)/shard_map/ppermute | solution.py:338
  18.7 1.6 %collective-permute-start.6 = (bf16[18,8,512]{2,1,0:T(8,128)(2,1)S(1)}, bf16[18,8,512]{2,1,0:T(8,128)(2,1)S(1)}, u32[]{:S(2)}, u32[]{:S(2)}) collective-permute-start(bf16[18,8,512]{2,1,0:T(8,128)(2,1)S(1)} %collective-permute-done.5.refs_8_), channel_id=1, source_target_pairs={{0,2},{2,0},{4,6},{6,4},{8,10},{10,8},{12,14},{14,12},{1,3},{3,1},... | collective-permute-start | bytes 442376 | tf_op jit(solution)/shard_map/ppermute | solution.py:338
  20.3 3.6 %load.2.refs_0_ = bf16[112,64,576]{2,1,0:T(8,128)(2,1)S(1)} custom-call(bf16[224,64,576]{2,1,0:T(8,128)(2,1)} %cache_ref.3, bf16[18,8,512]{2,1,0:T(8,128)(2,1)S(1)} %pad_maximum_fusion.after_ref.refs_2_), custom_call_target="tpu_custom_call" | custom-call | bytes 8257536 | tf_op jit(solution)/shard_map/load/pallas_call | solution.py:52
  23.9 3.6 %load.3.refs_1_ = bf16[112,64,576]{2,1,0:T(8,128)(2,1)S(1)} custom-call(bf16[224,64,576]{2,1,0:T(8,128)(2,1)} %cache_ref.3, bf16[18,8,512]{2,1,0:T(8,128)(2,1)S(1)} %collective-permute-done.after_ref.refs_6_), custom_call_target="tpu_custom_call" | custom-call | bytes 8257536 | tf_op jit(solution)/shard_map/load/pallas_call | solution.py:52
  27.6 1.6 %collective-permute-done.6.refs_9_ = bf16[18,8,512]{2,1,0:T(8,128)(2,1)S(1)} collective-permute-done((bf16[18,8,512]{2,1,0:T(8,128)(2,1)S(1)}, bf16[18,8,512]{2,1,0:T(8,128)(2,1)S(1)}, u32[]{:S(2)}, u32[]{:S(2)}) %collective-permute-start.6) | collective-permute-done | bytes 147488 | tf_op jit(solution)/shard_map/ppermute | solution.py:338
  29.2 12.9 %attend.1 = (bf16[17,8,512]{2,1,0:T(8,128)(2,1)S(1)}, bf16[17,8,512]{2,1,0:T(8,128)(2,1)S(1)}, bf16[17,8,512]{2,1,0:T(8,128)(2,1)S(1)}, bf16[17,8,512]{2,1,0:T(8...) custom-call(s32[224]{0:T(256)S(1)} %copy-done.3, ...), custom_call_target="tpu_custom_call" | custom-call | flops 7985954816 | bytes 16515072 | tf_op jit(solution)/shard_map/attend/pallas_call | solution.py:202
  42.0 1.7 %collective-permute-start.11 = (bf16[17,8,512]{2,1,0:T(8,128)(2,1)S(1)}, bf16[17,8,512]{2,1,0:T(8,128)(2,1)S(1)}, u32[]{:S(2)}, u32[]{:S(2)}) collective-permute-start(bf16[17,8,512]{2,1,0:T(8,128)(2,1)S(1)} %get-tuple-element.26), channel_id=1, source_target_pairs={{0,2},{2,0},{4,6},{6,4},{8,10},{10,8},{12,14},{14,12},{1,3},{3,1},... | collective-permute-start | bytes 417800 | tf_op jit(solution)/shard_map/ppermute | solution.py:338
  44.1 1.6 %collective-permute-start.10 = (bf16[17,8,512]{2,1,0:T(8,128)(2,1)S(1)}, bf16[17,8,512]{2,1,0:T(8,128)(2,1)S(1)}, u32[]{:S(2)}, u32[]{:S(2)}) collective-permute-start(bf16[17,8,512]{2,1,0:T(8,128)(2,1)S(1)} %get-tuple-element.24), channel_id=1, source_target_pairs={{0,2},{2,0},{4,6},{6,4},{8,10},{10,8},{12,14},{14,12},{1,3},{3,1},... | collective-permute-start | bytes 417800 | tf_op jit(solution)/shard_map/ppermute | solution.py:338
  45.7 3.0 %collective-permute-done.11.got_ref = bf16[17,8,512]{2,1,0:T(8,128)(2,1)S(1)} collective-permute-done((bf16[17,8,512]{2,1,0:T(8,128)(2,1)S(1)}, bf16[17,8,512]{2,1,0:T(8,128)(2,1)S(1)}, u32[]{:S(2)}, u32[]{:S(2)}) %collective-permute-start.11) | collective-permute-done | bytes 139296 | tf_op jit(solution)/shard_map/ppermute | solution.py:338
  49.4 1.2 %collective-permute-start.7 = (bf16[17,8,512]{2,1,0:T(8,128)(2,1)S(1)}, bf16[17,8,512]{2,1,0:T(8,128)(2,1)S(1)}, u32[]{:S(2)}, u32[]{:S(2)}) collective-permute-start(bf16[17,8,512]{2,1,0:T(8,128)(2,1)S(1)} %get-tuple-element.20), channel_id=1, source_target_pairs={{0,2},{2,0},{4,6},{6,4},{8,10},{10,8},{12,14},{14,12},{1,3},{3,1},... | collective-permute-start | bytes 417800 | tf_op jit(solution)/shard_map/ppermute | solution.py:338
  52.8 1.2 %collective-permute-done.10.got_ref = bf16[17,8,512]{2,1,0:T(8,128)(2,1)S(1)} collective-permute-done((bf16[17,8,512]{2,1,0:T(8,128)(2,1)S(1)}, bf16[17,8,512]{2,1,0:T(8,128)(2,1)S(1)}, u32[]{:S(2)}, u32[]{:S(2)}) %collective-permute-start.10) | collective-permute-done | bytes 139296 | tf_op jit(solution)/shard_map/ppermute | solution.py:338
  54.3 4.8 %collective-permute-start.13 = (bf16[17,8,512]{2,1,0:T(8,128)(2,1)S(1)}, bf16[17,8,512]{2,1,0:T(8,128)(2,1)S(1)}, u32[]{:S(2)}, u32[]{:S(2)}) collective-permute-start(bf16[17,8,512]{2,1,0:T(8,128)(2,1)S(1)} %merge.7), channel_id=1, source_target_pairs={{0,8},{2,10},{4,12},{6,14},{8,0},{10,2},{12,4},{14,6},{1,9},{3,11}... | collective-permute-start | bytes 417800 | tf_op jit(solution)/shard_map/ppermute | solution.py:338
  59.1 3.8 %collective-permute-done.13.refs_3_ = bf16[17,8,512]{2,1,0:T(8,128)(2,1)S(1)} collective-permute-done((bf16[17,8,512]{2,1,0:T(8,128)(2,1)S(1)}, bf16[17,8,512]{2,1,0:T(8,128)(2,1)S(1)}, u32[]{:S(2)}, u32[]{:S(2)}) %collective-permute-start.13) | collective-permute-done | bytes 139296 | tf_op jit(solution)/shard_map/ppermute | solution.py:338
  62.9 3.3 %finish.1 = bf16[16,16,448]{2,1,0:T(8,128)(2,1)S(1)} custom-call(s32[1]{0:T(128)} %bitcast.2.here_ref, bf16[8,512,128]{2,1,0:T(8,128)(2,1)S(1)} %copy-done.2, bf16[1024,7168]{1,0:T(8,128)(2,1)S(1)} %get-tuple-element.18.weight_ref, bf16[17,8,512]{2,1,0:T(8,128)(2,1)S(1)} %get-tuple-element.19.refs_0_, ...), custom_call_target="tpu_custom_call" | custom-call | flops 3758096384 | tf_op jit(solution)/shard_map/finish/pallas_call | solution.py:309
  66.3 1.6 %collective-permute-start.16 = (bf16[4,16,448]{2,1,0:T(8,128)(2,1)S(1)}, bf16[4,16,448]{2,1,0:T(8,128)(2,1)S(1)}, u32[]{:S(2)}, u32[]{:S(2)}) collective-permute-start(bf16[4,16,448]{2,1,0:T(8,128)(2,1)S(1)} %get-tuple-element.28), channel_id=1, source_target_pairs={{0,3},{1,2},{2,1},{3,0},{4,7},{5,6},{6,5},{7,4},{8,11},{9,10},{10,... | collective-permute-start | bytes 172040 | tf_op jit(solution)/shard_map/ppermute | solution.py:381
  68.4 1.9 %collective-permute-done.16 = bf16[4,16,448]{2,1,0:T(8,128)(2,1)S(1)} collective-permute-done((bf16[4,16,448]{2,1,0:T(8,128)(2,1)S(1)}, bf16[4,16,448]{2,1,0:T(8,128)(2,1)S(1)}, u32[]{:S(2)}, u32[]{:S(2)}) %collective-permute-start.16) | collective-permute-done | bytes 57376 | tf_op jit(solution)/shard_map/ppermute | solution.py:381
  70.4 1.8 %collective-permute-done.15 = bf16[4,16,448]{2,1,0:T(8,128)(2,1)S(1)} collective-permute-done((bf16[4,16,448]{2,1,0:T(8,128)(2,1)S(1)}, bf16[4,16,448]{2,1,0:T(8,128)(2,1)S(1)}, u32[]{:S(2)}, u32[]{:S(2)}) %collective-permute-start.15) | collective-permute-done | bytes 57376 | tf_op jit(solution)/shard_map/ppermute | solution.py:381
  72.3 3.6 %collective-permute-start.19 = (bf16[1,16,448]{2,1,0:T(8,128)(2,1)S(1)}, bf16[1,16,448]{2,1,0:T(8,128)(2,1)S(1)}, u32[]{:S(2)}, u32[]{:S(2)}) collective-permute-start(bf16[1,16,448]{2,1,0:T(8,128)(2,1)S(1)} %get-tuple-element.31), channel_id=1, source_target_pairs={{0,12},{1,13},{2,14},{3,15},{4,8},{5,9},{6,10},{7,11},{8,4},{9,5},... | collective-permute-start | bytes 43016 | tf_op jit(solution)/shard_map/ppermute | solution.py:381
  76.2 1.7 %collective-permute-done.19 = bf16[1,16,448]{2,1,0:T(8,128)(2,1)S(1)} collective-permute-done((bf16[1,16,448]{2,1,0:T(8,128)(2,1)S(1)}, bf16[1,16,448]{2,1,0:T(8,128)(2,1)S(1)}, u32[]{:S(2)}, u32[]{:S(2)}) %collective-permute-start.19) | collective-permute-done | bytes 14368 | tf_op jit(solution)/shard_map/ppermute | solution.py:381
  77.9 2.6 %collective-permute-done.18 = bf16[1,16,448]{2,1,0:T(8,128)(2,1)S(1)} collective-permute-done((bf16[1,16,448]{2,1,0:T(8,128)(2,1)S(1)}, bf16[1,16,448]{2,1,0:T(8,128)(2,1)S(1)}, u32[]{:S(2)}, u32[]{:S(2)}) %collective-permute-start.18) | collective-permute-done | bytes 14368 | tf_op jit(solution)/shard_map/ppermute | solution.py:381
  (42 shorter events, 9.6 us)
Async XLA Ops:
  0.0 1.2 %copy-start = (bf16[8,128,512]{2,1,0:T(8,128)(2,1)S(1)}, bf16[8,128,512]{2,1,0:T(8,128)(2,1)}, u32[]{:S(2)}) copy-start(bf16[8,128,512]{2,1,0:T(8,128)(2,1)} %param.9) | copy-start | bytes 3145732
  2.4 11.2 %collective-permute-start = (bf16[18,8,512]{2,1,0:T(8,128)(2,1)S(1)}, bf16[18,8,512]{2,1,0:T(8,128)(2,1)S(1)}, u32[]{:S(2)}, u32[]{:S(2)}) collective-permute-start(bf16[18,8,512]{2,1,0:T(8,128)(2,1)S(1)} %pad_maximum_fusion.after_ref.refs_2_), channel_id=1, source_target_pairs={{0,8},{2,10},{4,12},{6,14},{8,0},{10,2},{12,4},{14,6},{1,9},{3,11}... | collective-permute-start | bytes 442376 | tf_op jit(solution)/shard_map/ppermute | solution.py:338
  6.5 9.8 %collective-permute-start.2 = (bf16[18,8,512]{2,1,0:T(8,128)(2,1)S(1)}, bf16[18,8,512]{2,1,0:T(8,128)(2,1)S(1)}, u32[]{:S(2)}, u32[]{:S(2)}) collective-permute-start(bf16[18,8,512]{2,1,0:T(8,128)(2,1)S(1)} %pad_maximum_fusion.after_ref.refs_2_), channel_id=1, source_target_pairs={{0,4},{2,6},{4,0},{6,2},{8,12},{10,14},{12,8},{14,10},{1,5},{3,7},... | collective-permute-start | bytes 442376 | tf_op jit(solution)/shard_map/ppermute | solution.py:338
  13.6 5.1 %collective-permute-start.5 = (bf16[18,8,512]{2,1,0:T(8,128)(2,1)S(1)}, bf16[18,8,512]{2,1,0:T(8,128)(2,1)S(1)}, u32[]{:S(2)}, u32[]{:S(2)}) collective-permute-start(bf16[18,8,512]{2,1,0:T(8,128)(2,1)S(1)} %collective-permute-done.after_ref.refs_6_), channel_id=1, source_target_pairs={{0,4},{2,6},{4,0},{6,2},{8,12},{10,14},{12,8},{14,10},{1,5},{3,7},... | collective-permute-start | bytes 442376 | tf_op jit(solution)/shard_map/ppermute | solution.py:338
  14.2 13.4 %collective-permute-start.1 = (bf16[18,8,512]{2,1,0:T(8,128)(2,1)S(1)}, bf16[18,8,512]{2,1,0:T(8,128)(2,1)S(1)}, u32[]{:S(2)}, u32[]{:S(2)}) collective-permute-start(bf16[18,8,512]{2,1,0:T(8,128)(2,1)S(1)} %pad_maximum_fusion.after_ref.refs_2_), channel_id=1, source_target_pairs={{0,2},{2,0},{4,6},{6,4},{8,10},{10,8},{12,14},{14,12},{1,3},{3,1},... | collective-permute-start | bytes 442376 | tf_op jit(solution)/shard_map/ppermute | solution.py:338
  15.7 11.9 %collective-permute-start.4 = (bf16[18,8,512]{2,1,0:T(8,128)(2,1)S(1)}, bf16[18,8,512]{2,1,0:T(8,128)(2,1)S(1)}, u32[]{:S(2)}, u32[]{:S(2)}) collective-permute-start(bf16[18,8,512]{2,1,0:T(8,128)(2,1)S(1)} %collective-permute-done.after_ref.refs_6_), channel_id=1, source_target_pairs={{0,2},{2,0},{4,6},{6,4},{8,10},{10,8},{12,14},{14,12},{1,3},{3,1},... | collective-permute-start | bytes 442376 | tf_op jit(solution)/shard_map/ppermute | solution.py:338
  16.2 11.4 %collective-permute-start.3 = (bf16[18,8,512]{2,1,0:T(8,128)(2,1)S(1)}, bf16[18,8,512]{2,1,0:T(8,128)(2,1)S(1)}, u32[]{:S(2)}, u32[]{:S(2)}) collective-permute-start(bf16[18,8,512]{2,1,0:T(8,128)(2,1)S(1)} %collective-permute-done.2.refs_4_), channel_id=1, source_target_pairs={{0,2},{2,0},{4,6},{6,4},{8,10},{10,8},{12,14},{14,12},{1,3},{3,1},... | collective-permute-start | bytes 442376 | tf_op jit(solution)/shard_map/ppermute | solution.py:338
  18.7 10.4 %collective-permute-start.6 = (bf16[18,8,512]{2,1,0:T(8,128)(2,1)S(1)}, bf16[18,8,512]{2,1,0:T(8,128)(2,1)S(1)}, u32[]{:S(2)}, u32[]{:S(2)}) collective-permute-start(bf16[18,8,512]{2,1,0:T(8,128)(2,1)S(1)} %collective-permute-done.5.refs_8_), channel_id=1, source_target_pairs={{0,2},{2,0},{4,6},{6,4},{8,10},{10,8},{12,14},{14,12},{1,3},{3,1},... | collective-permute-start | bytes 442376 | tf_op jit(solution)/shard_map/ppermute | solution.py:338
  23.9 5.3 %copy-start.3 = (s32[224]{0:T(256)S(1)}, s32[224]{0:T(256)}, u32[]{:S(2)}) copy-start(s32[224]{0:T(256)} %owner_ref.1) | copy-start | bytes 2692
  27.6 35.3 %copy-start.2 = (bf16[8,512,128]{2,1,0:T(8,128)(2,1)S(1)}, bf16[8,512,128]{2,1,0:T(8,128)(2,1)}, u32[]{:S(2)}) copy-start(bf16[8,512,128]{2,1,0:T(8,128)(2,1)} %value_ref.1) | copy-start | bytes 3145732
  29.2 52.0 %copy-start.1 = (bf16[8,128,512]{2,1,0:T(8,128)(2,1)S(1)}, bf16[8,128,512]{2,1,0:T(8,128)(2,1)}, u32[]{:S(2)}) copy-start(bf16[8,128,512]{2,1,0:T(8,128)(2,1)} %param.9) | copy-start | bytes 3145732
  42.0 6.7 %collective-permute-start.11 = (bf16[17,8,512]{2,1,0:T(8,128)(2,1)S(1)}, bf16[17,8,512]{2,1,0:T(8,128)(2,1)S(1)}, u32[]{:S(2)}, u32[]{:S(2)}) collective-permute-start(bf16[17,8,512]{2,1,0:T(8,128)(2,1)S(1)} %get-tuple-element.26), channel_id=1, source_target_pairs={{0,2},{2,0},{4,6},{6,4},{8,10},{10,8},{12,14},{14,12},{1,3},{3,1},... | collective-permute-start | bytes 417800 | tf_op jit(solution)/shard_map/ppermute | solution.py:338
  43.7 8.0 %collective-permute-start.8 = (bf16[17,8,512]{2,1,0:T(8,128)(2,1)S(1)}, bf16[17,8,512]{2,1,0:T(8,128)(2,1)S(1)}, u32[]{:S(2)}, u32[]{:S(2)}) collective-permute-start(bf16[17,8,512]{2,1,0:T(8,128)(2,1)S(1)} %get-tuple-element.22), channel_id=1, source_target_pairs={{0,2},{2,0},{4,6},{6,4},{8,10},{10,8},{12,14},{14,12},{1,3},{3,1},... | collective-permute-start | bytes 417800 | tf_op jit(solution)/shard_map/ppermute | solution.py:338
  44.1 9.9 %collective-permute-start.10 = (bf16[17,8,512]{2,1,0:T(8,128)(2,1)S(1)}, bf16[17,8,512]{2,1,0:T(8,128)(2,1)S(1)}, u32[]{:S(2)}, u32[]{:S(2)}) collective-permute-start(bf16[17,8,512]{2,1,0:T(8,128)(2,1)S(1)} %get-tuple-element.24), channel_id=1, source_target_pairs={{0,2},{2,0},{4,6},{6,4},{8,10},{10,8},{12,14},{14,12},{1,3},{3,1},... | collective-permute-start | bytes 417800 | tf_op jit(solution)/shard_map/ppermute | solution.py:338
  48.9 5.3 %collective-permute-start.12 = (bf16[17,8,512]{2,1,0:T(8,128)(2,1)S(1)}, bf16[17,8,512]{2,1,0:T(8,128)(2,1)S(1)}, u32[]{:S(2)}, u32[]{:S(2)}) collective-permute-start(bf16[17,8,512]{2,1,0:T(8,128)(2,1)S(1)} %merge.6), channel_id=1, source_target_pairs={{0,4},{2,6},{4,0},{6,2},{8,12},{10,14},{12,8},{14,10},{1,5},{3,7},... | collective-permute-start | bytes 417800 | tf_op jit(solution)/shard_map/ppermute | solution.py:338
  49.4 9.7 %collective-permute-start.7 = (bf16[17,8,512]{2,1,0:T(8,128)(2,1)S(1)}, bf16[17,8,512]{2,1,0:T(8,128)(2,1)S(1)}, u32[]{:S(2)}, u32[]{:S(2)}) collective-permute-start(bf16[17,8,512]{2,1,0:T(8,128)(2,1)S(1)} %get-tuple-element.20), channel_id=1, source_target_pairs={{0,2},{2,0},{4,6},{6,4},{8,10},{10,8},{12,14},{14,12},{1,3},{3,1},... | collective-permute-start | bytes 417800 | tf_op jit(solution)/shard_map/ppermute | solution.py:338
  51.8 7.2 %collective-permute-start.9 = (bf16[17,8,512]{2,1,0:T(8,128)(2,1)S(1)}, bf16[17,8,512]{2,1,0:T(8,128)(2,1)S(1)}, u32[]{:S(2)}, u32[]{:S(2)}) collective-permute-start(bf16[17,8,512]{2,1,0:T(8,128)(2,1)S(1)} %merge.4), channel_id=1, source_target_pairs={{0,4},{2,6},{4,0},{6,2},{8,12},{10,14},{12,8},{14,10},{1,5},{3,7},... | collective-permute-start | bytes 417800 | tf_op jit(solution)/shard_map/ppermute | solution.py:338
  54.3 8.6 %collective-permute-start.13 = (bf16[17,8,512]{2,1,0:T(8,128)(2,1)S(1)}, bf16[17,8,512]{2,1,0:T(8,128)(2,1)S(1)}, u32[]{:S(2)}, u32[]{:S(2)}) collective-permute-start(bf16[17,8,512]{2,1,0:T(8,128)(2,1)S(1)} %merge.7), channel_id=1, source_target_pairs={{0,8},{2,10},{4,12},{6,14},{8,0},{10,2},{12,4},{14,6},{1,9},{3,11}... | collective-permute-start | bytes 417800 | tf_op jit(solution)/shard_map/ppermute | solution.py:338
  66.2 2.2 %collective-permute-start.14 = (bf16[4,16,448]{2,1,0:T(8,128)(2,1)S(1)}, bf16[4,16,448]{2,1,0:T(8,128)(2,1)S(1)}, u32[]{:S(2)}, u32[]{:S(2)}) collective-permute-start(bf16[4,16,448]{2,1,0:T(8,128)(2,1)S(1)} %get-tuple-element.27), channel_id=1, source_target_pairs={{0,1},{1,0},{2,3},{3,2},{4,5},{5,4},{6,7},{7,6},{8,9},{9,8},{10,11... | collective-permute-start | bytes 172040 | tf_op jit(solution)/shard_map/ppermute | solution.py:381
  66.3 4.1 %collective-permute-start.16 = (bf16[4,16,448]{2,1,0:T(8,128)(2,1)S(1)}, bf16[4,16,448]{2,1,0:T(8,128)(2,1)S(1)}, u32[]{:S(2)}, u32[]{:S(2)}) collective-permute-start(bf16[4,16,448]{2,1,0:T(8,128)(2,1)S(1)} %get-tuple-element.28), channel_id=1, source_target_pairs={{0,3},{1,2},{2,1},{3,0},{4,7},{5,6},{6,5},{7,4},{8,11},{9,10},{10,... | collective-permute-start | bytes 172040 | tf_op jit(solution)/shard_map/ppermute | solution.py:381
  67.9 4.3 %collective-permute-start.15 = (bf16[4,16,448]{2,1,0:T(8,128)(2,1)S(1)}, bf16[4,16,448]{2,1,0:T(8,128)(2,1)S(1)}, u32[]{:S(2)}, u32[]{:S(2)}) collective-permute-start(bf16[4,16,448]{2,1,0:T(8,128)(2,1)S(1)} %get-tuple-element.29), channel_id=1, source_target_pairs={{0,2},{1,3},{2,0},{3,1},{4,6},{5,7},{6,4},{7,5},{8,10},{9,11},{10,... | collective-permute-start | bytes 172040 | tf_op jit(solution)/shard_map/ppermute | solution.py:381
  72.3 4.0 %collective-permute-start.17 = (bf16[1,16,448]{2,1,0:T(8,128)(2,1)S(1)}, bf16[1,16,448]{2,1,0:T(8,128)(2,1)S(1)}, u32[]{:S(2)}, u32[]{:S(2)}) collective-permute-start(bf16[1,16,448]{2,1,0:T(8,128)(2,1)S(1)} %get-tuple-element.30), channel_id=1, source_target_pairs={{0,4},{1,5},{2,6},{3,7},{4,0},{5,1},{6,2},{7,3},{8,12},{9,13},{10,... | collective-permute-start | bytes 43016 | tf_op jit(solution)/shard_map/ppermute | solution.py:381
  72.3 5.6 %collective-permute-start.19 = (bf16[1,16,448]{2,1,0:T(8,128)(2,1)S(1)}, bf16[1,16,448]{2,1,0:T(8,128)(2,1)S(1)}, u32[]{:S(2)}, u32[]{:S(2)}) collective-permute-start(bf16[1,16,448]{2,1,0:T(8,128)(2,1)S(1)} %get-tuple-element.31), channel_id=1, source_target_pairs={{0,12},{1,13},{2,14},{3,15},{4,8},{5,9},{6,10},{7,11},{8,4},{9,5},... | collective-permute-start | bytes 43016 | tf_op jit(solution)/shard_map/ppermute | solution.py:381
  75.9 4.6 %collective-permute-start.18 = (bf16[1,16,448]{2,1,0:T(8,128)(2,1)S(1)}, bf16[1,16,448]{2,1,0:T(8,128)(2,1)S(1)}, u32[]{:S(2)}, u32[]{:S(2)}) collective-permute-start(bf16[1,16,448]{2,1,0:T(8,128)(2,1)S(1)} %get-tuple-element.32), channel_id=1, source_target_pairs={{0,8},{1,9},{2,10},{3,11},{4,12},{5,13},{6,14},{7,15},{8,0},{9,1},... | collective-permute-start | bytes 43016 | tf_op jit(solution)/shard_map/ppermute | solution.py:381

commit v6 on v5

--- a/solution.py
+++ b/solution.py
@@ -61,6 +61,28 @@
         ),
         name="load",
     )(pltpu.with_memory_space_constraint(cache, pltpu.HBM), after)
+
+
+def pass_kernel(others, here_ref, *refs):
+    refs[others][0] = here_ref[0]
+
+
+def gate(here, blocks, after):
+    any_spec = pl.BlockSpec(memory_space=pl.ANY)
+    out = pl.pallas_call(
+        functools.partial(pass_kernel, len(blocks) + 1),
+        out_shape=[
+            jax.ShapeDtypeStruct(here.shape, here.dtype),
+            *[jax.ShapeDtypeStruct(x.shape, x.dtype) for x in blocks],
+        ],
+        in_specs=[SMEM_SPEC] + [any_spec] * (len(blocks) + 1),
+        out_specs=[SMEM_SPEC] + [any_spec] * len(blocks),
+        input_output_aliases={i + 1: i + 1 for i in range(len(blocks))},
+        compiler_params=pltpu.CompilerParams(vmem_limit_bytes=MIB),
+        cost_estimate=pl.CostEstimate(flops=0, bytes_accessed=0, transcendentals=0),
+        name="gate",
+    )(here, *blocks, after)
+    return out[0], list(out[1:])
 
 
 def attend_kernel(score_scale, steps, blocks, owner_ref, weight_ref, *refs):
@@ -343,36 +365,33 @@
     ropes_row = latent_size // rope_size
     rope = query_rope.reshape(-1, ropes_row, heads_here, rope_size).transpose(0, 2, 1, 3)
     own = jnp.concatenate([query_latent, rope.reshape(-1, heads_here, latent_size)], axis=0)
-    own, here = lax.optimization_barrier((own, here))
-
-    bits = [1 << b for b in range(count.bit_length() - 1)]
-    block_at = {0: own}
-    for bit in reversed(bits):
-        for distance in list(block_at):
-            block_at[distance ^ bit] = exchange(block_at[distance], bit)
-
-    cache_parts = [
-        load(latent_cache, i, CACHE_PARTS, block) for i, block in enumerate([own, block_at[bits[-1]]])
-    ]
+
+    bits = [1 << b for b in reversed(range(count.bit_length() - 1))]
+    block_at = {bit: exchange(own, bit) for bit in bits}
+    cache_parts = [load(latent_cache, 0, CACHE_PARTS, own)]
+    here, passed = gate(here, list(block_at.values()), cache_parts[0])
+    block_at = {0: own, **dict(zip(bits, passed))}
+    for distance in sorted(range(count), key=lambda d: (d.bit_count(), -d)):
+        if distance.bit_count() > 1:
+            bit = distance & -distance
+            block_at[distance] = exchange(block_at[distance ^ bit], bit)
+    for part in range(1, CACHE_PARTS):
+        cache_parts.append(load(latent_cache, part, CACHE_PARTS, block_at[bits[0]]))
+
     message_to, weight = attend(
         [block_at[d] for d in range(count)],
         cache_parts, page_owner, output_weight, score_scale, latent_size,
     )
 
-    messages = [message_to[0]]
-    for bit in bits:
-        for distance in range(count - bit, 0, -2 * bit):
-            got = exchange(message_to[distance], bit)
-            if distance == bit:
-                messages.append(got)
-            else:
-                message_to[distance ^ bit] = merge(message_to[distance ^ bit], got)
+    even = [*range(4, count, 2), *range(2, min(4, count), 2)]
+    across = {distance: exchange(message_to[distance ^ 1], 1) for distance in [*even, 0]}
+    arrived = [
+        exchange(merge(message_to[distance], across[distance]), distance) for distance in even
+    ]
+    messages = [message_to[0], across[0], *arrived]
 
     owners = lax.axis_size(axes)
-    radices = []
-    while functools.reduce(lambda a, b: a * b, radices, 1) < owners:
-        left = owners // functools.reduce(lambda a, b: a * b, radices, 1)
-        radices.append(4 if left % 4 == 0 else 2)
+    radices = [owners // count, count]
     pieces = finish(here, messages, value_absorb, weight, radices)
     unit = 1
     for radix in radices:

time: 81.4 us -> 82.5 us (1.014)
  waiting for transfers between devices: 25.6 us -> 17 us
  local copies, waits for them, and re-layouts: 1.37 us -> 8.55 us
  starting transfers between devices: 28.4 us -> 29.7 us
  Pallas kernels: 24 us -> 25.1 us
    unnamed x8 -> x18, local copies, waits for them, and re-layouts: 0.24 us -> 7.42 us
    ppermute x6 -> x8, starting transfers between devices: 5.89 us -> 11.3 us  [body(): lax.ppermute(pieces[k * share:(k + 1) * share], axes, [(i, i ^ k * unit)...]
    ppermute x6 -> x8, waiting for transfers between devices: 8.4 us -> 3.22 us  [body(): lax.ppermute(pieces[k * share:(k + 1) * share], axes, [(i, i ^ k * unit)...]
    ppermute x14, starting transfers between devices: 22.5 us -> 18.4 us  [exchange(): return lax.ppermute(x, 'ctx', [(i, i ^ distance) for i in range(count)])]
    ppermute x14, waiting for transfers between devices: 17.2 us -> 13.8 us  [exchange(): return lax.ppermute(x, 'ctx', [(i, i ^ distance) for i in range(count)])]
  transfers between devices with their start and end apart: 20 -> 22, of which waited for: 12 -> 11; matrix products, arithmetic and copies ran while one was open for 0% -> 0% of each run, Pallas kernels for 10% -> 9%
where the time goes in v6:
time: 82.5 us; the launch traced here: 82.2 us
  starting transfers between devices  29.7 us (36%)
  Pallas kernels  25.1 us (30%)
  waiting for transfers between devices  17 us (21%)
  local copies, waits for them, and re-layouts  8.55 us (10%)
  matrix products  0.99 us (1%)
    ppermute x14, starting transfers between devices, exchange(): return lax.ppermute(x, 'ctx', [(i, i ^ distance) for i in range(count)])  18.4 us
    ppermute x14, waiting for transfers between devices, exchange(): return lax.ppermute(x, 'ctx', [(i, i ^ distance) for i in range(count)])  13.8 us
    pallas_call x1, Pallas kernels, attend(): pl.pallas_call(functools.partial(attend_kernel, score_scale, steps, block...  13 us
    ppermute x8, starting transfers between devices, body(): lax.ppermute(pieces[k * share:(k + 1) * share], axes, [(i, i ^ k * unit)...  11.3 us
    unnamed x18, local copies, waits for them, and re-layouts  7.42 us
    pallas_call x2, Pallas kernels, load(): pl.pallas_call(functools.partial(load_kernel, part * pages), out_shape=pl...  7.23 us
    pallas_call x1, Pallas kernels, finish(): pl.pallas_call(functools.partial(finish_kernel, block_columns, radices),...  3.94 us
    ppermute x8, waiting for transfers between devices, body(): lax.ppermute(pieces[k * share:(k + 1) * share], axes, [(i, i ^ k * unit)...  3.22 us
  transfers between devices with their start and end apart: 22, of which 11 were waited for; matrix products, arithmetic and copies ran while one was open for 0% of the time, Pallas kernels for 9%

profile of v6, /device:TPU:0, one launch (start us, length us, event | category | flops | bytes accessed | tf_op | source)
XLA Modules:
  0.0 82.2 jit_solution(15051073750115369621)
XLA Ops:
  2.4 3.0 %collective-permute-start.2 = (bf16[18,8,512]{2,1,0:T(8,128)(2,1)S(1)}, bf16[18,8,512]{2,1,0:T(8,128)(2,1)S(1)}, u32[]{:S(2)}, u32[]{:S(2)}) collective-permute-start(bf16[18,8,512]{2,1,0:T(8,128)(2,1)S(1)} %pad_maximum_fusion.after_ref.refs_2_), channel_id=1, source_target_pairs={{0,2},{2,0},{4,6},{6,4},{8,10},{10,8},{12,14},{14,12},{1,3},{3,1},... | collective-permute-start | bytes 442376 | tf_op jit(solution)/shard_map/ppermute | solution.py:360
  5.4 1.6 %collective-permute-start.1 = (bf16[18,8,512]{2,1,0:T(8,128)(2,1)S(1)}, bf16[18,8,512]{2,1,0:T(8,128)(2,1)S(1)}, u32[]{:S(2)}, u32[]{:S(2)}) collective-permute-start(bf16[18,8,512]{2,1,0:T(8,128)(2,1)S(1)} %pad_maximum_fusion.after_ref.refs_2_), channel_id=1, source_target_pairs={{0,4},{2,6},{4,0},{6,2},{8,12},{10,14},{12,8},{14,10},{1,5},{3,7},... | collective-permute-start | bytes 442376 | tf_op jit(solution)/shard_map/ppermute | solution.py:360
  7.0 2.6 %collective-permute-start = (bf16[18,8,512]{2,1,0:T(8,128)(2,1)S(1)}, bf16[18,8,512]{2,1,0:T(8,128)(2,1)S(1)}, u32[]{:S(2)}, u32[]{:S(2)}) collective-permute-start(bf16[18,8,512]{2,1,0:T(8,128)(2,1)S(1)} %pad_maximum_fusion.after_ref.refs_2_), channel_id=1, source_target_pairs={{0,8},{2,10},{4,12},{6,14},{8,0},{10,2},{12,4},{14,6},{1,9},{3,11}... | collective-permute-start | bytes 442376 | tf_op jit(solution)/shard_map/ppermute | solution.py:360
  9.6 3.6 %load.2.refs_3_.refs_0_ = bf16[112,64,576]{2,1,0:T(8,128)(2,1)S(1)} custom-call(bf16[224,64,576]{2,1,0:T(8,128)(2,1)} %cache_ref.3, bf16[18,8,512]{2,1,0:T(8,128)(2,1)S(1)} %pad_maximum_fusion.after_ref.refs_2_), custom_call_target="tpu_custom_call" | custom-call | bytes 8257536 | tf_op jit(solution)/shard_map/load/pallas_call | solution.py:52
  13.2 3.6 %copy-done.2 = bf16[112,64,576]{2,1,0:T(8,128)(2,1)} copy-done((bf16[112,64,576]{2,1,0:T(8,128)(2,1)}, bf16[112,64,576]{2,1,0:T(8,128)(2,1)S(1)}, u32[]{:S(2)}) %copy-start.2) | copy-done | bytes 8257560
  16.8 3.6 %copy-done.3 = bf16[112,64,576]{2,1,0:T(8,128)(2,1)S(1)} copy-done((bf16[112,64,576]{2,1,0:T(8,128)(2,1)S(1)}, bf16[112,64,576]{2,1,0:T(8,128)(2,1)}, u32[]{:S(2)}) %copy-start.3) | copy-done | bytes 8257560
  21.9 1.5 %collective-permute-start.3 = (bf16[18,8,512]{2,1,0:T(8,128)(2,1)S(1)}, bf16[18,8,512]{2,1,0:T(8,128)(2,1)S(1)}, u32[]{:S(2)}, u32[]{:S(2)}) collective-permute-start(bf16[18,8,512]{2,1,0:T(8,128)(2,1)S(1)} %get-tuple-element.21.refs_4_), channel_id=1, source_target_pairs={{0,2},{2,0},{4,6},{6,4},{8,10},{10,8},{12,14},{14,12},{1,3},{3,1},... | collective-permute-start | bytes 442376 | tf_op jit(solution)/shard_map/ppermute | solution.py:360
  23.5 2.7 %collective-permute-done.5.refs_8_ = bf16[18,8,512]{2,1,0:T(8,128)(2,1)S(1)} collective-permute-done((bf16[18,8,512]{2,1,0:T(8,128)(2,1)S(1)}, bf16[18,8,512]{2,1,0:T(8,128)(2,1)S(1)}, u32[]{:S(2)}, u32[]{:S(2)}) %collective-permute-start.5) | collective-permute-done | bytes 147488 | tf_op jit(solution)/shard_map/ppermute | solution.py:360
  26.6 3.6 %load.3.refs_1_ = bf16[112,64,576]{2,1,0:T(8,128)(2,1)S(1)} custom-call(bf16[224,64,576]{2,1,0:T(8,128)(2,1)} %cache_ref.3, bf16[18,8,512]{2,1,0:T(8,128)(2,1)S(1)} %get-tuple-element.19.after_ref.refs_6_), custom_call_target="tpu_custom_call" | custom-call | bytes 8257536 | tf_op jit(solution)/shard_map/load/pallas_call | solution.py:52
  30.6 1.6 %collective-permute-done.6.refs_9_ = bf16[18,8,512]{2,1,0:T(8,128)(2,1)S(1)} collective-permute-done((bf16[18,8,512]{2,1,0:T(8,128)(2,1)S(1)}, bf16[18,8,512]{2,1,0:T(8,128)(2,1)S(1)}, u32[]{:S(2)}, u32[]{:S(2)}) %collective-permute-start.6) | collective-permute-done | bytes 147488 | tf_op jit(solution)/shard_map/ppermute | solution.py:360
  32.3 13.0 %attend.1 = (bf16[17,8,512]{2,1,0:T(8,128)(2,1)S(1)}, bf16[17,8,512]{2,1,0:T(8,128)(2,1)S(1)}, bf16[17,8,512]{2,1,0:T(8,128)(2,1)S(1)}, bf16[17,8,512]{2,1,0:T(8...) custom-call(s32[224]{0:T(256)S(1)} %copy-done.5, ...), custom_call_target="tpu_custom_call" | custom-call | flops 7985954816 | bytes 16515072 | tf_op jit(solution)/shard_map/attend/pallas_call | solution.py:224
  45.7 1.6 %collective-permute-start.10 = (bf16[17,8,512]{2,1,0:T(8,128)(2,1)S(1)}, bf16[17,8,512]{2,1,0:T(8,128)(2,1)S(1)}, u32[]{:S(2)}, u32[]{:S(2)}) collective-permute-start(bf16[17,8,512]{2,1,0:T(8,128)(2,1)S(1)} %get-tuple-element.28), channel_id=1, source_target_pairs={{0,2},{2,0},{4,6},{6,4},{8,10},{10,8},{12,14},{14,12},{1,3},{3,1},... | collective-permute-start | bytes 417800 | tf_op jit(solution)/shard_map/ppermute | solution.py:360
  47.7 1.6 %collective-permute-start.7 = (bf16[17,8,512]{2,1,0:T(8,128)(2,1)S(1)}, bf16[17,8,512]{2,1,0:T(8,128)(2,1)S(1)}, u32[]{:S(2)}, u32[]{:S(2)}) collective-permute-start(bf16[17,8,512]{2,1,0:T(8,128)(2,1)S(1)} %get-tuple-element.24), channel_id=1, source_target_pairs={{0,2},{2,0},{4,6},{6,4},{8,10},{10,8},{12,14},{14,12},{1,3},{3,1},... | collective-permute-start | bytes 417800 | tf_op jit(solution)/shard_map/ppermute | solution.py:360
  49.4 2.6 %collective-permute-done.8.got_ref = bf16[17,8,512]{2,1,0:T(8,128)(2,1)S(1)} collective-permute-done((bf16[17,8,512]{2,1,0:T(8,128)(2,1)S(1)}, bf16[17,8,512]{2,1,0:T(8,128)(2,1)S(1)}, u32[]{:S(2)}, u32[]{:S(2)}) %collective-permute-start.8) | collective-permute-done | bytes 139296 | tf_op jit(solution)/shard_map/ppermute | solution.py:360
  53.1 1.5 %collective-permute-done.10.got_ref = bf16[17,8,512]{2,1,0:T(8,128)(2,1)S(1)} collective-permute-done((bf16[17,8,512]{2,1,0:T(8,128)(2,1)S(1)}, bf16[17,8,512]{2,1,0:T(8,128)(2,1)S(1)}, u32[]{:S(2)}, u32[]{:S(2)}) %collective-permute-start.10) | collective-permute-done | bytes 139296 | tf_op jit(solution)/shard_map/ppermute | solution.py:360
  56.4 1.5 %collective-permute-start.13 = (bf16[17,8,512]{2,1,0:T(8,128)(2,1)S(1)}, bf16[17,8,512]{2,1,0:T(8,128)(2,1)S(1)}, u32[]{:S(2)}, u32[]{:S(2)}) collective-permute-start(bf16[17,8,512]{2,1,0:T(8,128)(2,1)S(1)} %merge.5), channel_id=1, source_target_pairs={{0,4},{2,6},{4,0},{6,2},{8,12},{10,14},{12,8},{14,10},{1,5},{3,7},... | collective-permute-start | bytes 417800 | tf_op jit(solution)/shard_map/ppermute | solution.py:360
  57.9 1.7 %collective-permute-done.9.refs_2_ = bf16[17,8,512]{2,1,0:T(8,128)(2,1)S(1)} collective-permute-done((bf16[17,8,512]{2,1,0:T(8,128)(2,1)S(1)}, bf16[17,8,512]{2,1,0:T(8,128)(2,1)S(1)}, u32[]{:S(2)}, u32[]{:S(2)}) %collective-permute-start.9) | collective-permute-done | bytes 139296 | tf_op jit(solution)/shard_map/ppermute | solution.py:360
  59.7 2.2 %collective-permute-done.11.refs_3_ = bf16[17,8,512]{2,1,0:T(8,128)(2,1)S(1)} collective-permute-done((bf16[17,8,512]{2,1,0:T(8,128)(2,1)S(1)}, bf16[17,8,512]{2,1,0:T(8,128)(2,1)S(1)}, u32[]{:S(2)}, u32[]{:S(2)}) %collective-permute-start.11) | collective-permute-done | bytes 139296 | tf_op jit(solution)/shard_map/ppermute | solution.py:360
  63.0 3.9 %finish.1 = bf16[16,16,448]{2,1,0:T(8,128)(2,1)S(1)} custom-call(s32[1]{0:T(128)} %get-tuple-element.18.here_ref, bf16[8,512,128]{2,1,0:T(8,128)(2,1)S(1)} %copy-done.4, bf16[1024,7168]{1,0:T(8,128)(2,1)S(1)} %get-tuple-element.22.weight_ref, bf16[17,8,512]{2,1,0:T(8,128)(2,1)S(1)} %get-tuple-element.23.refs_0_, ...), custom_call_target="tpu_custom_call" | custom-call | flops 3758096384 | tf_op jit(solution)/shard_map/finish/pallas_call | solution.py:331
  69.0 2.7 %collective-permute-start.21 = (bf16[1,16,448]{2,1,0:T(8,128)(2,1)S(1)}, bf16[1,16,448]{2,1,0:T(8,128)(2,1)S(1)}, u32[]{:S(2)}, u32[]{:S(2)}) collective-permute-start(bf16[1,16,448]{2,1,0:T(8,128)(2,1)S(1)} %get-tuple-element.32), channel_id=1, source_target_pairs={{0,14},{1,15},{2,12},{3,13},{4,10},{5,11},{6,8},{7,9},{8,6},{9,7},... | collective-permute-start | bytes 43016 | tf_op jit(solution)/shard_map/ppermute | solution.py:400
  71.7 2.1 %collective-permute-start.20 = (bf16[1,16,448]{2,1,0:T(8,128)(2,1)S(1)}, bf16[1,16,448]{2,1,0:T(8,128)(2,1)S(1)}, u32[]{:S(2)}, u32[]{:S(2)}) collective-permute-start(bf16[1,16,448]{2,1,0:T(8,128)(2,1)S(1)} %get-tuple-element.33), channel_id=1, source_target_pairs={{0,12},{1,13},{2,14},{3,15},{4,8},{5,9},{6,10},{7,11},{8,4},{9,5},... | collective-permute-start | bytes 43016 | tf_op jit(solution)/shard_map/ppermute | solution.py:400
  73.8 2.8 %collective-permute-start.18 = (bf16[1,16,448]{2,1,0:T(8,128)(2,1)S(1)}, bf16[1,16,448]{2,1,0:T(8,128)(2,1)S(1)}, u32[]{:S(2)}, u32[]{:S(2)}) collective-permute-start(bf16[1,16,448]{2,1,0:T(8,128)(2,1)S(1)} %get-tuple-element.35), channel_id=1, source_target_pairs={{0,8},{1,9},{2,10},{3,11},{4,12},{5,13},{6,14},{7,15},{8,0},{9,1},... | collective-permute-start | bytes 43016 | tf_op jit(solution)/shard_map/ppermute | solution.py:400
  77.0 2.7 %collective-permute-start.16 = (bf16[1,16,448]{2,1,0:T(8,128)(2,1)S(1)}, bf16[1,16,448]{2,1,0:T(8,128)(2,1)S(1)}, u32[]{:S(2)}, u32[]{:S(2)}) collective-permute-start(bf16[1,16,448]{2,1,0:T(8,128)(2,1)S(1)} %get-tuple-element.37), channel_id=1, source_target_pairs={{0,4},{1,5},{2,6},{3,7},{4,0},{5,1},{6,2},{7,3},{8,12},{9,13},{10,... | collective-permute-start | bytes 43016 | tf_op jit(solution)/shard_map/ppermute | solution.py:400
  79.7 1.6 %collective-permute-done.17 = bf16[1,16,448]{2,1,0:T(8,128)(2,1)S(1)} collective-permute-done((bf16[1,16,448]{2,1,0:T(8,128)(2,1)S(1)}, bf16[1,16,448]{2,1,0:T(8,128)(2,1)S(1)}, u32[]{:S(2)}, u32[]{:S(2)}) %collective-permute-start.17) | collective-permute-done | bytes 14368 | tf_op jit(solution)/shard_map/ppermute | solution.py:400
  (57 shorter events, 13.0 us)
Async XLA Ops:
  2.4 14.4 %collective-permute-start.2 = (bf16[18,8,512]{2,1,0:T(8,128)(2,1)S(1)}, bf16[18,8,512]{2,1,0:T(8,128)(2,1)S(1)}, u32[]{:S(2)}, u32[]{:S(2)}) collective-permute-start(bf16[18,8,512]{2,1,0:T(8,128)(2,1)S(1)} %pad_maximum_fusion.after_ref.refs_2_), channel_id=1, source_target_pairs={{0,2},{2,0},{4,6},{6,4},{8,10},{10,8},{12,14},{14,12},{1,3},{3,1},... | collective-permute-start | bytes 442376 | tf_op jit(solution)/shard_map/ppermute | solution.py:360
  5.4 11.4 %collective-permute-start.1 = (bf16[18,8,512]{2,1,0:T(8,128)(2,1)S(1)}, bf16[18,8,512]{2,1,0:T(8,128)(2,1)S(1)}, u32[]{:S(2)}, u32[]{:S(2)}) collective-permute-start(bf16[18,8,512]{2,1,0:T(8,128)(2,1)S(1)} %pad_maximum_fusion.after_ref.refs_2_), channel_id=1, source_target_pairs={{0,4},{2,6},{4,0},{6,2},{8,12},{10,14},{12,8},{14,10},{1,5},{3,7},... | collective-permute-start | bytes 442376 | tf_op jit(solution)/shard_map/ppermute | solution.py:360
  7.0 9.8 %collective-permute-start = (bf16[18,8,512]{2,1,0:T(8,128)(2,1)S(1)}, bf16[18,8,512]{2,1,0:T(8,128)(2,1)S(1)}, u32[]{:S(2)}, u32[]{:S(2)}) collective-permute-start(bf16[18,8,512]{2,1,0:T(8,128)(2,1)S(1)} %pad_maximum_fusion.after_ref.refs_2_), channel_id=1, source_target_pairs={{0,8},{2,10},{4,12},{6,14},{8,0},{10,2},{12,4},{14,6},{1,9},{3,11}... | collective-permute-start | bytes 442376 | tf_op jit(solution)/shard_map/ppermute | solution.py:360
  20.9 5.2 %collective-permute-start.5 = (bf16[18,8,512]{2,1,0:T(8,128)(2,1)S(1)}, bf16[18,8,512]{2,1,0:T(8,128)(2,1)S(1)}, u32[]{:S(2)}, u32[]{:S(2)}) collective-permute-start(bf16[18,8,512]{2,1,0:T(8,128)(2,1)S(1)} %get-tuple-element.19.after_ref.refs_6_), channel_id=1, source_target_pairs={{0,4},{2,6},{4,0},{6,2},{8,12},{10,14},{12,8},{14,10},{1,5},{3,7},... | collective-permute-start | bytes 442376 | tf_op jit(solution)/shard_map/ppermute | solution.py:360
  21.4 9.2 %collective-permute-start.4 = (bf16[18,8,512]{2,1,0:T(8,128)(2,1)S(1)}, bf16[18,8,512]{2,1,0:T(8,128)(2,1)S(1)}, u32[]{:S(2)}, u32[]{:S(2)}) collective-permute-start(bf16[18,8,512]{2,1,0:T(8,128)(2,1)S(1)} %get-tuple-element.19.after_ref.refs_6_), channel_id=1, source_target_pairs={{0,2},{2,0},{4,6},{6,4},{8,10},{10,8},{12,14},{14,12},{1,3},{3,1},... | collective-permute-start | bytes 442376 | tf_op jit(solution)/shard_map/ppermute | solution.py:360
  21.9 8.7 %collective-permute-start.3 = (bf16[18,8,512]{2,1,0:T(8,128)(2,1)S(1)}, bf16[18,8,512]{2,1,0:T(8,128)(2,1)S(1)}, u32[]{:S(2)}, u32[]{:S(2)}) collective-permute-start(bf16[18,8,512]{2,1,0:T(8,128)(2,1)S(1)} %get-tuple-element.21.refs_4_), channel_id=1, source_target_pairs={{0,2},{2,0},{4,6},{6,4},{8,10},{10,8},{12,14},{14,12},{1,3},{3,1},... | collective-permute-start | bytes 442376 | tf_op jit(solution)/shard_map/ppermute | solution.py:360
  26.1 6.1 %collective-permute-start.6 = (bf16[18,8,512]{2,1,0:T(8,128)(2,1)S(1)}, bf16[18,8,512]{2,1,0:T(8,128)(2,1)S(1)}, u32[]{:S(2)}, u32[]{:S(2)}) collective-permute-start(bf16[18,8,512]{2,1,0:T(8,128)(2,1)S(1)} %collective-permute-done.5.refs_8_), channel_id=1, source_target_pairs={{0,2},{2,0},{4,6},{6,4},{8,10},{10,8},{12,14},{14,12},{1,3},{3,1},... | collective-permute-start | bytes 442376 | tf_op jit(solution)/shard_map/ppermute | solution.py:360
  32.2 30.8 %copy-start.4 = (bf16[8,512,128]{2,1,0:T(8,128)(2,1)S(1)}, bf16[8,512,128]{2,1,0:T(8,128)(2,1)}, u32[]{:S(2)}) copy-start(bf16[8,512,128]{2,1,0:T(8,128)(2,1)} %value_ref.1) | copy-start | bytes 3145732
  32.3 49.9 %copy-start.1 = (bf16[8,128,512]{2,1,0:T(8,128)(2,1)S(1)}, bf16[8,128,512]{2,1,0:T(8,128)(2,1)}, u32[]{:S(2)}) copy-start(bf16[8,128,512]{2,1,0:T(8,128)(2,1)} %param.9) | copy-start | bytes 3145732
  45.2 6.7 %collective-permute-start.8 = (bf16[17,8,512]{2,1,0:T(8,128)(2,1)S(1)}, bf16[17,8,512]{2,1,0:T(8,128)(2,1)S(1)}, u32[]{:S(2)}, u32[]{:S(2)}) collective-permute-start(bf16[17,8,512]{2,1,0:T(8,128)(2,1)S(1)} %get-tuple-element.26), channel_id=1, source_target_pairs={{0,2},{2,0},{4,6},{6,4},{8,10},{10,8},{12,14},{14,12},{1,3},{3,1},... | collective-permute-start | bytes 417800 | tf_op jit(solution)/shard_map/ppermute | solution.py:360
  45.7 9.0 %collective-permute-start.10 = (bf16[17,8,512]{2,1,0:T(8,128)(2,1)S(1)}, bf16[17,8,512]{2,1,0:T(8,128)(2,1)S(1)}, u32[]{:S(2)}, u32[]{:S(2)}) collective-permute-start(bf16[17,8,512]{2,1,0:T(8,128)(2,1)S(1)} %get-tuple-element.28), channel_id=1, source_target_pairs={{0,2},{2,0},{4,6},{6,4},{8,10},{10,8},{12,14},{14,12},{1,3},{3,1},... | collective-permute-start | bytes 417800 | tf_op jit(solution)/shard_map/ppermute | solution.py:360
  47.3 8.9 %collective-permute-start.12 = (bf16[17,8,512]{2,1,0:T(8,128)(2,1)S(1)}, bf16[17,8,512]{2,1,0:T(8,128)(2,1)S(1)}, u32[]{:S(2)}, u32[]{:S(2)}) collective-permute-start(bf16[17,8,512]{2,1,0:T(8,128)(2,1)S(1)} %get-tuple-element.30), channel_id=1, source_target_pairs={{0,2},{2,0},{4,6},{6,4},{8,10},{10,8},{12,14},{14,12},{1,3},{3,1},... | collective-permute-start | bytes 417800 | tf_op jit(solution)/shard_map/ppermute | solution.py:360
  47.7 10.2 %collective-permute-start.7 = (bf16[17,8,512]{2,1,0:T(8,128)(2,1)S(1)}, bf16[17,8,512]{2,1,0:T(8,128)(2,1)S(1)}, u32[]{:S(2)}, u32[]{:S(2)}) collective-permute-start(bf16[17,8,512]{2,1,0:T(8,128)(2,1)S(1)} %get-tuple-element.24), channel_id=1, source_target_pairs={{0,2},{2,0},{4,6},{6,4},{8,10},{10,8},{12,14},{14,12},{1,3},{3,1},... | collective-permute-start | bytes 417800 | tf_op jit(solution)/shard_map/ppermute | solution.py:360
  52.1 7.6 %collective-permute-start.9 = (bf16[17,8,512]{2,1,0:T(8,128)(2,1)S(1)}, bf16[17,8,512]{2,1,0:T(8,128)(2,1)S(1)}, u32[]{:S(2)}, u32[]{:S(2)}) collective-permute-start(bf16[17,8,512]{2,1,0:T(8,128)(2,1)S(1)} %merge.3), channel_id=1, source_target_pairs={{0,8},{2,10},{4,12},{6,14},{8,0},{10,2},{12,4},{14,6},{1,9},{3,11}... | collective-permute-start | bytes 417800 | tf_op jit(solution)/shard_map/ppermute | solution.py:360
  54.8 7.1 %collective-permute-start.11 = (bf16[17,8,512]{2,1,0:T(8,128)(2,1)S(1)}, bf16[17,8,512]{2,1,0:T(8,128)(2,1)S(1)}, u32[]{:S(2)}, u32[]{:S(2)}) collective-permute-start(bf16[17,8,512]{2,1,0:T(8,128)(2,1)S(1)} %merge.4), channel_id=1, source_target_pairs={{0,12},{2,14},{4,8},{6,10},{8,4},{10,6},{12,0},{14,2},{1,13},{3,15... | collective-permute-start | bytes 417800 | tf_op jit(solution)/shard_map/ppermute | solution.py:360
  56.4 6.6 %collective-permute-start.13 = (bf16[17,8,512]{2,1,0:T(8,128)(2,1)S(1)}, bf16[17,8,512]{2,1,0:T(8,128)(2,1)S(1)}, u32[]{:S(2)}, u32[]{:S(2)}) collective-permute-start(bf16[17,8,512]{2,1,0:T(8,128)(2,1)S(1)} %merge.5), channel_id=1, source_target_pairs={{0,4},{2,6},{4,0},{6,2},{8,12},{10,14},{12,8},{14,10},{1,5},{3,7},... | collective-permute-start | bytes 417800 | tf_op jit(solution)/shard_map/ppermute | solution.py:360
  67.0 1.4 %collective-permute-start.14 = (bf16[8,16,448]{2,1,0:T(8,128)(2,1)S(1)}, bf16[8,16,448]{2,1,0:T(8,128)(2,1)S(1)}, u32[]{:S(2)}, u32[]{:S(2)}) collective-permute-start(bf16[8,16,448]{2,1,0:T(8,128)(2,1)S(1)} %slice.41), channel_id=1, source_target_pairs={{0,1},{1,0},{2,3},{3,2},{4,5},{5,4},{6,7},{7,6},{8,9},{9,8},{10,11... | collective-permute-start | bytes 344072 | tf_op jit(solution)/shard_map/ppermute | solution.py:400
  68.5 8.2 %collective-permute-start.15 = (bf16[1,16,448]{2,1,0:T(8,128)(2,1)S(1)}, bf16[1,16,448]{2,1,0:T(8,128)(2,1)S(1)}, u32[]{:S(2)}, u32[]{:S(2)}) collective-permute-start(bf16[1,16,448]{2,1,0:T(8,128)(2,1)S(1)} %get-tuple-element.31), channel_id=1, source_target_pairs={{0,2},{1,3},{2,0},{3,1},{4,6},{5,7},{6,4},{7,5},{8,10},{9,11},{10,... | collective-permute-start | bytes 43016 | tf_op jit(solution)/shard_map/ppermute | solution.py:400
  69.0 8.0 %collective-permute-start.21 = (bf16[1,16,448]{2,1,0:T(8,128)(2,1)S(1)}, bf16[1,16,448]{2,1,0:T(8,128)(2,1)S(1)}, u32[]{:S(2)}, u32[]{:S(2)}) collective-permute-start(bf16[1,16,448]{2,1,0:T(8,128)(2,1)S(1)} %get-tuple-element.32), channel_id=1, source_target_pairs={{0,14},{1,15},{2,12},{3,13},{4,10},{5,11},{6,8},{7,9},{8,6},{9,7},... | collective-permute-start | bytes 43016 | tf_op jit(solution)/shard_map/ppermute | solution.py:400
  71.7 8.0 %collective-permute-start.20 = (bf16[1,16,448]{2,1,0:T(8,128)(2,1)S(1)}, bf16[1,16,448]{2,1,0:T(8,128)(2,1)S(1)}, u32[]{:S(2)}, u32[]{:S(2)}) collective-permute-start(bf16[1,16,448]{2,1,0:T(8,128)(2,1)S(1)} %get-tuple-element.33), channel_id=1, source_target_pairs={{0,12},{1,13},{2,14},{3,15},{4,8},{5,9},{6,10},{7,11},{8,4},{9,5},... | collective-permute-start | bytes 43016 | tf_op jit(solution)/shard_map/ppermute | solution.py:400
  73.8 5.9 %collective-permute-start.19 = (bf16[1,16,448]{2,1,0:T(8,128)(2,1)S(1)}, bf16[1,16,448]{2,1,0:T(8,128)(2,1)S(1)}, u32[]{:S(2)}, u32[]{:S(2)}) collective-permute-start(bf16[1,16,448]{2,1,0:T(8,128)(2,1)S(1)} %get-tuple-element.34), channel_id=1, source_target_pairs={{0,10},{1,11},{2,8},{3,9},{4,14},{5,15},{6,12},{7,13},{8,2},{9,3},... | collective-permute-start | bytes 43016 | tf_op jit(solution)/shard_map/ppermute | solution.py:400
  73.8 5.9 %collective-permute-start.18 = (bf16[1,16,448]{2,1,0:T(8,128)(2,1)S(1)}, bf16[1,16,448]{2,1,0:T(8,128)(2,1)S(1)}, u32[]{:S(2)}, u32[]{:S(2)}) collective-permute-start(bf16[1,16,448]{2,1,0:T(8,128)(2,1)S(1)} %get-tuple-element.35), channel_id=1, source_target_pairs={{0,8},{1,9},{2,10},{3,11},{4,12},{5,13},{6,14},{7,15},{8,0},{9,1},... | collective-permute-start | bytes 43016 | tf_op jit(solution)/shard_map/ppermute | solution.py:400
  76.7 4.6 %collective-permute-start.17 = (bf16[1,16,448]{2,1,0:T(8,128)(2,1)S(1)}, bf16[1,16,448]{2,1,0:T(8,128)(2,1)S(1)}, u32[]{:S(2)}, u32[]{:S(2)}) collective-permute-start(bf16[1,16,448]{2,1,0:T(8,128)(2,1)S(1)} %get-tuple-element.36), channel_id=1, source_target_pairs={{0,6},{1,7},{2,4},{3,5},{4,2},{5,3},{6,0},{7,1},{8,14},{9,15},{10,... | collective-permute-start | bytes 43016 | tf_op jit(solution)/shard_map/ppermute | solution.py:400
  77.0 4.6 %collective-permute-start.16 = (bf16[1,16,448]{2,1,0:T(8,128)(2,1)S(1)}, bf16[1,16,448]{2,1,0:T(8,128)(2,1)S(1)}, u32[]{:S(2)}, u32[]{:S(2)}) collective-permute-start(bf16[1,16,448]{2,1,0:T(8,128)(2,1)S(1)} %get-tuple-element.37), channel_id=1, source_target_pairs={{0,4},{1,5},{2,6},{3,7},{4,0},{5,1},{6,2},{7,3},{8,12},{9,13},{10,... | collective-permute-start | bytes 43016 | tf_op jit(solution)/shard_map/ppermute | solution.py:400
  (7 other events, 51.6 us)

commit v7 on v6

--- a/solution.py
+++ b/solution.py
@@ -41,18 +41,22 @@
     return (parts[0] + parts[1]) + parts[2]
 
 
-def load_kernel(first, cache_ref, after_ref, out_ref, sem):
+def load_kernel(first, here_ref, cache_ref, after_ref, out_ref, sem):
     copy = pltpu.make_async_copy(cache_ref.at[pl.ds(first, out_ref.shape[0])], out_ref, sem)
     copy.start()
     copy.wait()
 
 
-def load(cache, part, parts, after):
+def load(here, cache, part, parts, after):
     pages = cache.shape[0] // parts
     return pl.pallas_call(
         functools.partial(load_kernel, part * pages),
         out_shape=pltpu.VMEM((pages, *cache.shape[1:]), cache.dtype),
-        in_specs=[pl.BlockSpec(memory_space=pltpu.HBM), pl.BlockSpec(memory_space=pl.ANY)],
+        in_specs=[
+            SMEM_SPEC,
+            pl.BlockSpec(memory_space=pltpu.HBM),
+            pl.BlockSpec(memory_space=pl.ANY),
+        ],
         out_specs=VMEM_SPEC,
         scratch_shapes=[pltpu.SemaphoreType.DMA],
         compiler_params=pltpu.CompilerParams(vmem_limit_bytes=MIB),
@@ -60,7 +64,7 @@
             flops=0, bytes_accessed=2 * cache.size // parts, transcendentals=0
         ),
         name="load",
-    )(pltpu.with_memory_space_constraint(cache, pltpu.HBM), after)
+    )(here, pltpu.with_memory_space_constraint(cache, pltpu.HBM), after)
 
 
 def pass_kernel(others, here_ref, *refs):
@@ -366,24 +370,23 @@
     rope = query_rope.reshape(-1, ropes_row, heads_here, rope_size).transpose(0, 2, 1, 3)
     own = jnp.concatenate([query_latent, rope.reshape(-1, heads_here, latent_size)], axis=0)
 
-    bits = [1 << b for b in reversed(range(count.bit_length() - 1))]
-    block_at = {bit: exchange(own, bit) for bit in bits}
-    cache_parts = [load(latent_cache, 0, CACHE_PARTS, own)]
-    here, passed = gate(here, list(block_at.values()), cache_parts[0])
-    block_at = {0: own, **dict(zip(bits, passed))}
-    for distance in sorted(range(count), key=lambda d: (d.bit_count(), -d)):
-        if distance.bit_count() > 1:
-            bit = distance & -distance
-            block_at[distance] = exchange(block_at[distance ^ bit], bit)
+    even = [*range(4, count, 2), *range(2, min(4, count), 2)]
+    block_at = {distance: exchange(own, distance) for distance in [*even, 1]}
+    cache_parts = [load(here, latent_cache, 0, CACHE_PARTS, own)]
+    here, (block_at[2], block_at[1]) = gate(here, [block_at[2], block_at[1]], cache_parts[0])
     for part in range(1, CACHE_PARTS):
-        cache_parts.append(load(latent_cache, part, CACHE_PARTS, block_at[bits[0]]))
+        cache_parts.append(load(here, latent_cache, part, CACHE_PARTS, block_at[2]))
+    block_at[3] = exchange(block_at[2], 1)
+    for distance in even[:-1]:
+        _, (block_at[distance],) = gate(here, [block_at[distance]], cache_parts[-1])
+        block_at[distance ^ 1] = exchange(block_at[distance], 1)
+    block_at[0] = own
 
     message_to, weight = attend(
         [block_at[d] for d in range(count)],
         cache_parts, page_owner, output_weight, score_scale, latent_size,
     )
 
-    even = [*range(4, count, 2), *range(2, min(4, count), 2)]
     across = {distance: exchange(message_to[distance ^ 1], 1) for distance in [*even, 0]}
     arrived = [
         exchange(merge(message_to[distance], across[distance]), distance) for distance in even
@@ -391,7 +394,7 @@
     messages = [message_to[0], across[0], *arrived]
 
     owners = lax.axis_size(axes)
-    radices = [owners // count, count]
+    radices = [4] * ((owners.bit_length() - 1) // 2) + [2] * ((owners.bit_length() - 1) % 2)
     pieces = finish(here, messages, value_absorb, weight, radices)
     unit = 1
     for radix in radices:

time: 82.5 us -> 78.6 us (0.953)
  local copies, waits for them, and re-layouts: 8.55 us -> 1.37 us
  waiting for transfers between devices: 17 us -> 20.9 us
  starting transfers between devices: 29.7 us -> 25.9 us
  Pallas kernels: 25.1 us -> 28.3 us
    unnamed x18 -> x8, local copies, waits for them, and re-layouts: 7.42 us -> 0.24 us
    ppermute x8 -> x6, starting transfers between devices: 11.3 us -> 5.77 us  [body(): lax.ppermute(pieces[k * share:(k + 1) * share], axes, [(i, i ^ k * unit)...]
    ppermute x8 -> x6, waiting for transfers between devices: 3.22 us -> 7.88 us  [body(): lax.ppermute(pieces[k * share:(k + 1) * share], axes, [(i, i ^ k * unit)...]
    pallas_call x1 -> x3, Pallas kernels: 0.52 us -> 2.82 us  [gate(): pl.pallas_call(functools.partial(pass_kernel, len(blocks) + 1), out_shape...]
    ppermute x14, starting transfers between devices: 18.4 us -> 20.1 us  [exchange(): return lax.ppermute(x, 'ctx', [(i, i ^ distance) for i in range(count)])]
  transfers between devices with their start and end apart: 22 -> 20, of which waited for: 11 -> 12; matrix products, arithmetic and copies ran while one was open for 0% -> 0% of each run, Pallas kernels for 9% -> 14%
where the time goes in v7:
time: 78.6 us; the launch traced here: 78.2 us
  Pallas kernels  28.3 us (36%)
  starting transfers between devices  25.9 us (33%)
  waiting for transfers between devices  20.9 us (27%)
  local copies, waits for them, and re-layouts  1.37 us (2%)
  matrix products  0.99 us (1%)
    ppermute x14, starting transfers between devices, exchange(): return lax.ppermute(x, 'ctx', [(i, i ^ distance) for i in range(count)])  20.1 us
    pallas_call x1, Pallas kernels, attend(): pl.pallas_call(functools.partial(attend_kernel, score_scale, steps, block...  13.2 us
    ppermute x14, waiting for transfers between devices, exchange(): return lax.ppermute(x, 'ctx', [(i, i ^ distance) for i in range(count)])  13 us
    ppermute x6, waiting for transfers between devices, body(): lax.ppermute(pieces[k * share:(k + 1) * share], axes, [(i, i ^ k * unit)...  7.88 us
    pallas_call x2, Pallas kernels, load(): pl.pallas_call(functools.partial(load_kernel, part * pages), out_shape=pl...  7.86 us
    ppermute x6, starting transfers between devices, body(): lax.ppermute(pieces[k * share:(k + 1) * share], axes, [(i, i ^ k * unit)...  5.77 us
    pallas_call x1, Pallas kernels, finish(): pl.pallas_call(functools.partial(finish_kernel, block_columns, radices),...  4 us
    pallas_call x3, Pallas kernels, gate(): pl.pallas_call(functools.partial(pass_kernel, len(blocks) + 1), out_shape...  2.82 us
  transfers between devices with their start and end apart: 20, of which 12 were waited for; matrix products, arithmetic and copies ran while one was open for 0% of the time, Pallas kernels for 14%

profile of v7, /device:TPU:0, one launch (start us, length us, event | category | flops | bytes accessed | tf_op | source)
XLA Modules:
  0.0 78.2 jit_solution(6633485495780563274)
XLA Ops:
  2.4 3.0 %collective-permute-start.1 = (bf16[18,8,512]{2,1,0:T(8,128)(2,1)S(1)}, bf16[18,8,512]{2,1,0:T(8,128)(2,1)S(1)}, u32[]{:S(2)}, u32[]{:S(2)}) collective-permute-start(bf16[18,8,512]{2,1,0:T(8,128)(2,1)S(1)} %pad_maximum_fusion.after_ref.refs_2_), channel_id=1, source_target_pairs={{0,2},{2,0},{4,6},{6,4},{8,10},{10,8},{12,14},{14,12},{1,3},{3,1},... | collective-permute-start | bytes 442376 | tf_op jit(solution)/shard_map/ppermute | solution.py:364
  5.4 1.6 %collective-permute-start = (bf16[18,8,512]{2,1,0:T(8,128)(2,1)S(1)}, bf16[18,8,512]{2,1,0:T(8,128)(2,1)S(1)}, u32[]{:S(2)}, u32[]{:S(2)}) collective-permute-start(bf16[18,8,512]{2,1,0:T(8,128)(2,1)S(1)} %pad_maximum_fusion.after_ref.refs_2_), channel_id=1, source_target_pairs={{0,4},{2,6},{4,0},{6,2},{8,12},{10,14},{12,8},{14,10},{1,5},{3,7},... | collective-permute-start | bytes 442376 | tf_op jit(solution)/shard_map/ppermute | solution.py:364
  7.0 2.6 %collective-permute-start.3 = (bf16[18,8,512]{2,1,0:T(8,128)(2,1)S(1)}, bf16[18,8,512]{2,1,0:T(8,128)(2,1)S(1)}, u32[]{:S(2)}, u32[]{:S(2)}) collective-permute-start(bf16[18,8,512]{2,1,0:T(8,128)(2,1)S(1)} %pad_maximum_fusion.after_ref.refs_2_), channel_id=1, source_target_pairs={{0,8},{2,10},{4,12},{6,14},{8,0},{10,2},{12,4},{14,6},{1,9},{3,11}... | collective-permute-start | bytes 442376 | tf_op jit(solution)/shard_map/ppermute | solution.py:364
  9.8 3.6 %load.2.refs_2_.refs_0_ = bf16[112,64,576]{2,1,0:T(8,128)(2,1)S(1)} custom-call(s32[1]{0:T(128)} %bitcast.here_ref, bf16[224,64,576]{2,1,0:T(8,128)(2,1)} %cache_ref.3, bf16[18,8,512]{2,1,0:T(8,128)(2,1)S(1)} %pad_maximum_fusion.after_ref.refs_2_), custom_call_target="tpu_custom_call" | custom-call | bytes 8257536 | tf_op jit(solution)/shard_map/load/pallas_call | solution.py:52
  14.3 4.2 %load.3.refs_1_ = bf16[112,64,576]{2,1,0:T(8,128)(2,1)S(1)} custom-call(s32[1]{0:T(128)} %get-tuple-element.19.here_ref, bf16[224,64,576]{2,1,0:T(8,128)(2,1)} %cache_ref.3, bf16[18,8,512]{2,1,0:T(8,128)(2,1)S(1)} %get-tuple-element.20.after_ref.refs_4_), custom_call_target="tpu_custom_call" | custom-call | bytes 8257536 | tf_op jit(solution)/shard_map/load/pallas_call | solution.py:52
  18.6 2.3 %collective-permute-done.3.refs_0_ = bf16[18,8,512]{2,1,0:T(8,128)(2,1)S(1)} collective-permute-done((bf16[18,8,512]{2,1,0:T(8,128)(2,1)S(1)}, bf16[18,8,512]{2,1,0:T(8,128)(2,1)S(1)}, u32[]{:S(2)}, u32[]{:S(2)}) %collective-permute-start.3) | collective-permute-done | bytes 147488 | tf_op jit(solution)/shard_map/ppermute | solution.py:364
  23.7 1.6 %collective-permute-start.6 = (bf16[18,8,512]{2,1,0:T(8,128)(2,1)S(1)}, bf16[18,8,512]{2,1,0:T(8,128)(2,1)S(1)}, u32[]{:S(2)}, u32[]{:S(2)}) collective-permute-start(bf16[18,8,512]{2,1,0:T(8,128)(2,1)S(1)} %get-tuple-element.23.refs_8_), channel_id=1, source_target_pairs={{0,2},{2,0},{4,6},{6,4},{8,10},{10,8},{12,14},{14,12},{1,3},{3,1},... | collective-permute-start | bytes 442376 | tf_op jit(solution)/shard_map/ppermute | solution.py:364
  25.3 1.9 %collective-permute-done.4.refs_7_ = bf16[18,8,512]{2,1,0:T(8,128)(2,1)S(1)} collective-permute-done((bf16[18,8,512]{2,1,0:T(8,128)(2,1)S(1)}, bf16[18,8,512]{2,1,0:T(8,128)(2,1)S(1)}, u32[]{:S(2)}, u32[]{:S(2)}) %collective-permute-start.4) | collective-permute-done | bytes 147488 | tf_op jit(solution)/shard_map/ppermute | solution.py:364
  27.2 1.7 %collective-permute-done.6.refs_9_ = bf16[18,8,512]{2,1,0:T(8,128)(2,1)S(1)} collective-permute-done((bf16[18,8,512]{2,1,0:T(8,128)(2,1)S(1)}, bf16[18,8,512]{2,1,0:T(8,128)(2,1)S(1)}, u32[]{:S(2)}, u32[]{:S(2)}) %collective-permute-start.6) | collective-permute-done | bytes 147488 | tf_op jit(solution)/shard_map/ppermute | solution.py:364
  28.9 13.2 %attend.1 = (bf16[17,8,512]{2,1,0:T(8,128)(2,1)S(1)}, bf16[17,8,512]{2,1,0:T(8,128)(2,1)S(1)}, bf16[17,8,512]{2,1,0:T(8,128)(2,1)S(1)}, bf16[17,8,512]{2,1,0:T(8...) custom-call(s32[224]{0:T(256)S(1)} %copy-done.3, ...), custom_call_target="tpu_custom_call" | custom-call | flops 7985954816 | bytes 16515072 | tf_op jit(solution)/shard_map/attend/pallas_call | solution.py:228
  42.2 1.6 %collective-permute-start.8 = (bf16[17,8,512]{2,1,0:T(8,128)(2,1)S(1)}, bf16[17,8,512]{2,1,0:T(8,128)(2,1)S(1)}, u32[]{:S(2)}, u32[]{:S(2)}) collective-permute-start(bf16[17,8,512]{2,1,0:T(8,128)(2,1)S(1)} %get-tuple-element.28), channel_id=1, source_target_pairs={{0,2},{2,0},{4,6},{6,4},{8,10},{10,8},{12,14},{14,12},{1,3},{3,1},... | collective-permute-start | bytes 417800 | tf_op jit(solution)/shard_map/ppermute | solution.py:364
  44.3 1.6 %collective-permute-start.12 = (bf16[17,8,512]{2,1,0:T(8,128)(2,1)S(1)}, bf16[17,8,512]{2,1,0:T(8,128)(2,1)S(1)}, u32[]{:S(2)}, u32[]{:S(2)}) collective-permute-start(bf16[17,8,512]{2,1,0:T(8,128)(2,1)S(1)} %get-tuple-element.32), channel_id=1, source_target_pairs={{0,2},{2,0},{4,6},{6,4},{8,10},{10,8},{12,14},{14,12},{1,3},{3,1},... | collective-permute-start | bytes 417800 | tf_op jit(solution)/shard_map/ppermute | solution.py:364
  46.3 2.0 %collective-permute-done.8.got_ref = bf16[17,8,512]{2,1,0:T(8,128)(2,1)S(1)} collective-permute-done((bf16[17,8,512]{2,1,0:T(8,128)(2,1)S(1)}, bf16[17,8,512]{2,1,0:T(8,128)(2,1)S(1)}, u32[]{:S(2)}, u32[]{:S(2)}) %collective-permute-start.8) | collective-permute-done | bytes 139296 | tf_op jit(solution)/shard_map/ppermute | solution.py:364
  48.5 2.0 %collective-permute-start.9 = (bf16[17,8,512]{2,1,0:T(8,128)(2,1)S(1)}, bf16[17,8,512]{2,1,0:T(8,128)(2,1)S(1)}, u32[]{:S(2)}, u32[]{:S(2)}) collective-permute-start(bf16[17,8,512]{2,1,0:T(8,128)(2,1)S(1)} %merge.3), channel_id=1, source_target_pairs={{0,8},{2,10},{4,12},{6,14},{8,0},{10,2},{12,4},{14,6},{1,9},{3,11}... | collective-permute-start | bytes 417800 | tf_op jit(solution)/shard_map/ppermute | solution.py:364
  50.7 3.9 %collective-permute-start.11 = (bf16[17,8,512]{2,1,0:T(8,128)(2,1)S(1)}, bf16[17,8,512]{2,1,0:T(8,128)(2,1)S(1)}, u32[]{:S(2)}, u32[]{:S(2)}) collective-permute-start(bf16[17,8,512]{2,1,0:T(8,128)(2,1)S(1)} %merge.4), channel_id=1, source_target_pairs={{0,12},{2,14},{4,8},{6,10},{8,4},{10,6},{12,0},{14,2},{1,13},{3,15... | collective-permute-start | bytes 417800 | tf_op jit(solution)/shard_map/ppermute | solution.py:364
  56.0 1.7 %collective-permute-done.11.refs_3_ = bf16[17,8,512]{2,1,0:T(8,128)(2,1)S(1)} collective-permute-done((bf16[17,8,512]{2,1,0:T(8,128)(2,1)S(1)}, bf16[17,8,512]{2,1,0:T(8,128)(2,1)S(1)}, u32[]{:S(2)}, u32[]{:S(2)}) %collective-permute-start.11) | collective-permute-done | bytes 139296 | tf_op jit(solution)/shard_map/ppermute | solution.py:364
  57.7 2.2 %collective-permute-done.13.refs_4_ = bf16[17,8,512]{2,1,0:T(8,128)(2,1)S(1)} collective-permute-done((bf16[17,8,512]{2,1,0:T(8,128)(2,1)S(1)}, bf16[17,8,512]{2,1,0:T(8,128)(2,1)S(1)}, u32[]{:S(2)}, u32[]{:S(2)}) %collective-permute-start.13) | collective-permute-done | bytes 139296 | tf_op jit(solution)/shard_map/ppermute | solution.py:364
  59.9 4.0 %finish.1 = bf16[16,16,448]{2,1,0:T(8,128)(2,1)S(1)} custom-call(s32[1]{0:T(128)} %get-tuple-element.19.here_ref, bf16[8,512,128]{2,1,0:T(8,128)(2,1)S(1)} %copy-done.2, bf16[1024,7168]{1,0:T(8,128)(2,1)S(1)} %get-tuple-element.24.weight_ref, bf16[17,8,512]{2,1,0:T(8,128)(2,1)S(1)} %get-tuple-element.25.refs_0_, ...), custom_call_target="tpu_custom_call" | custom-call | flops 3758096384 | tf_op jit(solution)/shard_map/finish/pallas_call | solution.py:335
  64.7 1.4 %collective-permute-start.15 = (bf16[4,16,448]{2,1,0:T(8,128)(2,1)S(1)}, bf16[4,16,448]{2,1,0:T(8,128)(2,1)S(1)}, u32[]{:S(2)}, u32[]{:S(2)}) collective-permute-start(bf16[4,16,448]{2,1,0:T(8,128)(2,1)S(1)} %get-tuple-element.35), channel_id=1, source_target_pairs={{0,2},{1,3},{2,0},{3,1},{4,6},{5,7},{6,4},{7,5},{8,10},{9,11},{10,... | collective-permute-start | bytes 172040 | tf_op jit(solution)/shard_map/ppermute | solution.py:403
  66.1 1.7 %collective-permute-done.16 = bf16[4,16,448]{2,1,0:T(8,128)(2,1)S(1)} collective-permute-done((bf16[4,16,448]{2,1,0:T(8,128)(2,1)S(1)}, bf16[4,16,448]{2,1,0:T(8,128)(2,1)S(1)}, u32[]{:S(2)}, u32[]{:S(2)}) %collective-permute-start.16) | collective-permute-done | bytes 57376 | tf_op jit(solution)/shard_map/ppermute | solution.py:403
  67.9 2.0 %collective-permute-done.15 = bf16[4,16,448]{2,1,0:T(8,128)(2,1)S(1)} collective-permute-done((bf16[4,16,448]{2,1,0:T(8,128)(2,1)S(1)}, bf16[4,16,448]{2,1,0:T(8,128)(2,1)S(1)}, u32[]{:S(2)}, u32[]{:S(2)}) %collective-permute-start.15) | collective-permute-done | bytes 57376 | tf_op jit(solution)/shard_map/ppermute | solution.py:403
  69.9 1.4 %collective-permute-start.17 = (bf16[1,16,448]{2,1,0:T(8,128)(2,1)S(1)}, bf16[1,16,448]{2,1,0:T(8,128)(2,1)S(1)}, u32[]{:S(2)}, u32[]{:S(2)}) collective-permute-start(bf16[1,16,448]{2,1,0:T(8,128)(2,1)S(1)} %get-tuple-element.36), channel_id=1, source_target_pairs={{0,4},{1,5},{2,6},{3,7},{4,0},{5,1},{6,2},{7,3},{8,12},{9,13},{10,... | collective-permute-start | bytes 43016 | tf_op jit(solution)/shard_map/ppermute | solution.py:403
  71.3 1.7 %collective-permute-start.19 = (bf16[1,16,448]{2,1,0:T(8,128)(2,1)S(1)}, bf16[1,16,448]{2,1,0:T(8,128)(2,1)S(1)}, u32[]{:S(2)}, u32[]{:S(2)}) collective-permute-start(bf16[1,16,448]{2,1,0:T(8,128)(2,1)S(1)} %get-tuple-element.37), channel_id=1, source_target_pairs={{0,12},{1,13},{2,14},{3,15},{4,8},{5,9},{6,10},{7,11},{8,4},{9,5},... | collective-permute-start | bytes 43016 | tf_op jit(solution)/shard_map/ppermute | solution.py:403
  73.7 3.1 %collective-permute-done.19 = bf16[1,16,448]{2,1,0:T(8,128)(2,1)S(1)} collective-permute-done((bf16[1,16,448]{2,1,0:T(8,128)(2,1)S(1)}, bf16[1,16,448]{2,1,0:T(8,128)(2,1)S(1)}, u32[]{:S(2)}, u32[]{:S(2)}) %collective-permute-start.19) | collective-permute-done | bytes 14368 | tf_op jit(solution)/shard_map/ppermute | solution.py:403
  (44 shorter events, 11.9 us)
Async XLA Ops:
  0.0 1.2 %copy-start = (bf16[8,128,512]{2,1,0:T(8,128)(2,1)S(1)}, bf16[8,128,512]{2,1,0:T(8,128)(2,1)}, u32[]{:S(2)}) copy-start(bf16[8,128,512]{2,1,0:T(8,128)(2,1)} %param.9) | copy-start | bytes 3145732
  2.4 11.0 %collective-permute-start.1 = (bf16[18,8,512]{2,1,0:T(8,128)(2,1)S(1)}, bf16[18,8,512]{2,1,0:T(8,128)(2,1)S(1)}, u32[]{:S(2)}, u32[]{:S(2)}) collective-permute-start(bf16[18,8,512]{2,1,0:T(8,128)(2,1)S(1)} %pad_maximum_fusion.after_ref.refs_2_), channel_id=1, source_target_pairs={{0,2},{2,0},{4,6},{6,4},{8,10},{10,8},{12,14},{14,12},{1,3},{3,1},... | collective-permute-start | bytes 442376 | tf_op jit(solution)/shard_map/ppermute | solution.py:364
  5.4 8.0 %collective-permute-start = (bf16[18,8,512]{2,1,0:T(8,128)(2,1)S(1)}, bf16[18,8,512]{2,1,0:T(8,128)(2,1)S(1)}, u32[]{:S(2)}, u32[]{:S(2)}) collective-permute-start(bf16[18,8,512]{2,1,0:T(8,128)(2,1)S(1)} %pad_maximum_fusion.after_ref.refs_2_), channel_id=1, source_target_pairs={{0,4},{2,6},{4,0},{6,2},{8,12},{10,14},{12,8},{14,10},{1,5},{3,7},... | collective-permute-start | bytes 442376 | tf_op jit(solution)/shard_map/ppermute | solution.py:364
  7.0 13.9 %collective-permute-start.3 = (bf16[18,8,512]{2,1,0:T(8,128)(2,1)S(1)}, bf16[18,8,512]{2,1,0:T(8,128)(2,1)S(1)}, u32[]{:S(2)}, u32[]{:S(2)}) collective-permute-start(bf16[18,8,512]{2,1,0:T(8,128)(2,1)S(1)} %pad_maximum_fusion.after_ref.refs_2_), channel_id=1, source_target_pairs={{0,8},{2,10},{4,12},{6,14},{8,0},{10,2},{12,4},{14,6},{1,9},{3,11}... | collective-permute-start | bytes 442376 | tf_op jit(solution)/shard_map/ppermute | solution.py:364
  9.6 13.0 %collective-permute-start.5 = (bf16[18,8,512]{2,1,0:T(8,128)(2,1)S(1)}, bf16[18,8,512]{2,1,0:T(8,128)(2,1)S(1)}, u32[]{:S(2)}, u32[]{:S(2)}) collective-permute-start(bf16[18,8,512]{2,1,0:T(8,128)(2,1)S(1)} %pad_maximum_fusion.after_ref.refs_2_), channel_id=1, source_target_pairs={{0,12},{2,14},{4,8},{6,10},{8,4},{10,6},{12,0},{14,2},{1,13},{3,15... | collective-permute-start | bytes 442376 | tf_op jit(solution)/shard_map/ppermute | solution.py:364
  13.9 11.4 %collective-permute-start.2 = (bf16[18,8,512]{2,1,0:T(8,128)(2,1)S(1)}, bf16[18,8,512]{2,1,0:T(8,128)(2,1)S(1)}, u32[]{:S(2)}, u32[]{:S(2)}) collective-permute-start(bf16[18,8,512]{2,1,0:T(8,128)(2,1)S(1)} %get-tuple-element.20.after_ref.refs_4_), channel_id=1, source_target_pairs={{0,2},{2,0},{4,6},{6,4},{8,10},{10,8},{12,14},{14,12},{1,3},{3,1},... | collective-permute-start | bytes 442376 | tf_op jit(solution)/shard_map/ppermute | solution.py:364
  18.6 10.4 %copy-start.3 = (s32[224]{0:T(256)S(1)}, s32[224]{0:T(256)}, u32[]{:S(2)}) copy-start(s32[224]{0:T(256)} %owner_ref.1) | copy-start | bytes 2692
  22.0 5.2 %collective-permute-start.4 = (bf16[18,8,512]{2,1,0:T(8,128)(2,1)S(1)}, bf16[18,8,512]{2,1,0:T(8,128)(2,1)S(1)}, u32[]{:S(2)}, u32[]{:S(2)}) collective-permute-start(bf16[18,8,512]{2,1,0:T(8,128)(2,1)S(1)} %get-tuple-element.22.refs_6_), channel_id=1, source_target_pairs={{0,2},{2,0},{4,6},{6,4},{8,10},{10,8},{12,14},{14,12},{1,3},{3,1},... | collective-permute-start | bytes 442376 | tf_op jit(solution)/shard_map/ppermute | solution.py:364
  23.7 5.2 %collective-permute-start.6 = (bf16[18,8,512]{2,1,0:T(8,128)(2,1)S(1)}, bf16[18,8,512]{2,1,0:T(8,128)(2,1)S(1)}, u32[]{:S(2)}, u32[]{:S(2)}) collective-permute-start(bf16[18,8,512]{2,1,0:T(8,128)(2,1)S(1)} %get-tuple-element.23.refs_8_), channel_id=1, source_target_pairs={{0,2},{2,0},{4,6},{6,4},{8,10},{10,8},{12,14},{14,12},{1,3},{3,1},... | collective-permute-start | bytes 442376 | tf_op jit(solution)/shard_map/ppermute | solution.py:364
  28.9 30.9 %copy-start.2 = (bf16[8,512,128]{2,1,0:T(8,128)(2,1)S(1)}, bf16[8,512,128]{2,1,0:T(8,128)(2,1)}, u32[]{:S(2)}) copy-start(bf16[8,512,128]{2,1,0:T(8,128)(2,1)} %value_ref.1) | copy-start | bytes 3145732
  28.9 49.3 %copy-start.1 = (bf16[8,128,512]{2,1,0:T(8,128)(2,1)S(1)}, bf16[8,128,512]{2,1,0:T(8,128)(2,1)}, u32[]{:S(2)}) copy-start(bf16[8,128,512]{2,1,0:T(8,128)(2,1)} %param.9) | copy-start | bytes 3145732
  42.2 6.2 %collective-permute-start.8 = (bf16[17,8,512]{2,1,0:T(8,128)(2,1)S(1)}, bf16[17,8,512]{2,1,0:T(8,128)(2,1)S(1)}, u32[]{:S(2)}, u32[]{:S(2)}) collective-permute-start(bf16[17,8,512]{2,1,0:T(8,128)(2,1)S(1)} %get-tuple-element.28), channel_id=1, source_target_pairs={{0,2},{2,0},{4,6},{6,4},{8,10},{10,8},{12,14},{14,12},{1,3},{3,1},... | collective-permute-start | bytes 417800 | tf_op jit(solution)/shard_map/ppermute | solution.py:364
  43.8 6.7 %collective-permute-start.10 = (bf16[17,8,512]{2,1,0:T(8,128)(2,1)S(1)}, bf16[17,8,512]{2,1,0:T(8,128)(2,1)S(1)}, u32[]{:S(2)}, u32[]{:S(2)}) collective-permute-start(bf16[17,8,512]{2,1,0:T(8,128)(2,1)S(1)} %get-tuple-element.30), channel_id=1, source_target_pairs={{0,2},{2,0},{4,6},{6,4},{8,10},{10,8},{12,14},{14,12},{1,3},{3,1},... | collective-permute-start | bytes 417800 | tf_op jit(solution)/shard_map/ppermute | solution.py:364
  44.3 10.3 %collective-permute-start.12 = (bf16[17,8,512]{2,1,0:T(8,128)(2,1)S(1)}, bf16[17,8,512]{2,1,0:T(8,128)(2,1)S(1)}, u32[]{:S(2)}, u32[]{:S(2)}) collective-permute-start(bf16[17,8,512]{2,1,0:T(8,128)(2,1)S(1)} %get-tuple-element.32), channel_id=1, source_target_pairs={{0,2},{2,0},{4,6},{6,4},{8,10},{10,8},{12,14},{14,12},{1,3},{3,1},... | collective-permute-start | bytes 417800 | tf_op jit(solution)/shard_map/ppermute | solution.py:364
  45.8 9.0 %collective-permute-start.7 = (bf16[17,8,512]{2,1,0:T(8,128)(2,1)S(1)}, bf16[17,8,512]{2,1,0:T(8,128)(2,1)S(1)}, u32[]{:S(2)}, u32[]{:S(2)}) collective-permute-start(bf16[17,8,512]{2,1,0:T(8,128)(2,1)S(1)} %get-tuple-element.26), channel_id=1, source_target_pairs={{0,2},{2,0},{4,6},{6,4},{8,10},{10,8},{12,14},{14,12},{1,3},{3,1},... | collective-permute-start | bytes 417800 | tf_op jit(solution)/shard_map/ppermute | solution.py:364
  48.5 7.5 %collective-permute-start.9 = (bf16[17,8,512]{2,1,0:T(8,128)(2,1)S(1)}, bf16[17,8,512]{2,1,0:T(8,128)(2,1)S(1)}, u32[]{:S(2)}, u32[]{:S(2)}) collective-permute-start(bf16[17,8,512]{2,1,0:T(8,128)(2,1)S(1)} %merge.3), channel_id=1, source_target_pairs={{0,8},{2,10},{4,12},{6,14},{8,0},{10,2},{12,4},{14,6},{1,9},{3,11}... | collective-permute-start | bytes 417800 | tf_op jit(solution)/shard_map/ppermute | solution.py:364
  50.7 7.0 %collective-permute-start.11 = (bf16[17,8,512]{2,1,0:T(8,128)(2,1)S(1)}, bf16[17,8,512]{2,1,0:T(8,128)(2,1)S(1)}, u32[]{:S(2)}, u32[]{:S(2)}) collective-permute-start(bf16[17,8,512]{2,1,0:T(8,128)(2,1)S(1)} %merge.4), channel_id=1, source_target_pairs={{0,12},{2,14},{4,8},{6,10},{8,4},{10,6},{12,0},{14,2},{1,13},{3,15... | collective-permute-start | bytes 417800 | tf_op jit(solution)/shard_map/ppermute | solution.py:364
  54.8 5.1 %collective-permute-start.13 = (bf16[17,8,512]{2,1,0:T(8,128)(2,1)S(1)}, bf16[17,8,512]{2,1,0:T(8,128)(2,1)S(1)}, u32[]{:S(2)}, u32[]{:S(2)}) collective-permute-start(bf16[17,8,512]{2,1,0:T(8,128)(2,1)S(1)} %merge.5), channel_id=1, source_target_pairs={{0,4},{2,6},{4,0},{6,2},{8,12},{10,14},{12,8},{14,10},{1,5},{3,7},... | collective-permute-start | bytes 417800 | tf_op jit(solution)/shard_map/ppermute | solution.py:364
  63.9 2.2 %collective-permute-start.14 = (bf16[4,16,448]{2,1,0:T(8,128)(2,1)S(1)}, bf16[4,16,448]{2,1,0:T(8,128)(2,1)S(1)}, u32[]{:S(2)}, u32[]{:S(2)}) collective-permute-start(bf16[4,16,448]{2,1,0:T(8,128)(2,1)S(1)} %get-tuple-element.33), channel_id=1, source_target_pairs={{0,1},{1,0},{2,3},{3,2},{4,5},{5,4},{6,7},{7,6},{8,9},{9,8},{10,11... | collective-permute-start | bytes 172040 | tf_op jit(solution)/shard_map/ppermute | solution.py:403
  64.0 3.9 %collective-permute-start.16 = (bf16[4,16,448]{2,1,0:T(8,128)(2,1)S(1)}, bf16[4,16,448]{2,1,0:T(8,128)(2,1)S(1)}, u32[]{:S(2)}, u32[]{:S(2)}) collective-permute-start(bf16[4,16,448]{2,1,0:T(8,128)(2,1)S(1)} %get-tuple-element.34), channel_id=1, source_target_pairs={{0,3},{1,2},{2,1},{3,0},{4,7},{5,6},{6,5},{7,4},{8,11},{9,10},{10,... | collective-permute-start | bytes 172040 | tf_op jit(solution)/shard_map/ppermute | solution.py:403
  64.7 5.1 %collective-permute-start.15 = (bf16[4,16,448]{2,1,0:T(8,128)(2,1)S(1)}, bf16[4,16,448]{2,1,0:T(8,128)(2,1)S(1)}, u32[]{:S(2)}, u32[]{:S(2)}) collective-permute-start(bf16[4,16,448]{2,1,0:T(8,128)(2,1)S(1)} %get-tuple-element.35), channel_id=1, source_target_pairs={{0,2},{1,3},{2,0},{3,1},{4,6},{5,7},{6,4},{7,5},{8,10},{9,11},{10,... | collective-permute-start | bytes 172040 | tf_op jit(solution)/shard_map/ppermute | solution.py:403
  69.9 3.8 %collective-permute-start.17 = (bf16[1,16,448]{2,1,0:T(8,128)(2,1)S(1)}, bf16[1,16,448]{2,1,0:T(8,128)(2,1)S(1)}, u32[]{:S(2)}, u32[]{:S(2)}) collective-permute-start(bf16[1,16,448]{2,1,0:T(8,128)(2,1)S(1)} %get-tuple-element.36), channel_id=1, source_target_pairs={{0,4},{1,5},{2,6},{3,7},{4,0},{5,1},{6,2},{7,3},{8,12},{9,13},{10,... | collective-permute-start | bytes 43016 | tf_op jit(solution)/shard_map/ppermute | solution.py:403
  71.3 5.5 %collective-permute-start.19 = (bf16[1,16,448]{2,1,0:T(8,128)(2,1)S(1)}, bf16[1,16,448]{2,1,0:T(8,128)(2,1)S(1)}, u32[]{:S(2)}, u32[]{:S(2)}) collective-permute-start(bf16[1,16,448]{2,1,0:T(8,128)(2,1)S(1)} %get-tuple-element.37), channel_id=1, source_target_pairs={{0,12},{1,13},{2,14},{3,15},{4,8},{5,9},{6,10},{7,11},{8,4},{9,5},... | collective-permute-start | bytes 43016 | tf_op jit(solution)/shard_map/ppermute | solution.py:403
  73.0 4.6 %collective-permute-start.18 = (bf16[1,16,448]{2,1,0:T(8,128)(2,1)S(1)}, bf16[1,16,448]{2,1,0:T(8,128)(2,1)S(1)}, u32[]{:S(2)}, u32[]{:S(2)}) collective-permute-start(bf16[1,16,448]{2,1,0:T(8,128)(2,1)S(1)} %get-tuple-element.38), channel_id=1, source_target_pairs={{0,8},{1,9},{2,10},{3,11},{4,12},{5,13},{6,14},{7,15},{8,0},{9,1},... | collective-permute-start | bytes 43016 | tf_op jit(solution)/shard_map/ppermute | solution.py:403

commit v8 on v7

--- a/solution.py
+++ b/solution.py
@@ -67,26 +67,21 @@
     )(here, pltpu.with_memory_space_constraint(cache, pltpu.HBM), after)
 
 
-def pass_kernel(others, here_ref, *refs):
-    refs[others][0] = here_ref[0]
-
-
-def gate(here, blocks, after):
-    any_spec = pl.BlockSpec(memory_space=pl.ANY)
-    out = pl.pallas_call(
-        functools.partial(pass_kernel, len(blocks) + 1),
-        out_shape=[
-            jax.ShapeDtypeStruct(here.shape, here.dtype),
-            *[jax.ShapeDtypeStruct(x.shape, x.dtype) for x in blocks],
-        ],
-        in_specs=[SMEM_SPEC] + [any_spec] * (len(blocks) + 1),
-        out_specs=[SMEM_SPEC] + [any_spec] * len(blocks),
-        input_output_aliases={i + 1: i + 1 for i in range(len(blocks))},
+def gate_kernel(block_ref, after_ref, out_ref):
+    pass
+
+
+def gate(block, after):
+    return pl.pallas_call(
+        gate_kernel,
+        out_shape=jax.ShapeDtypeStruct(block.shape, block.dtype),
+        in_specs=[pl.BlockSpec(memory_space=pl.ANY)] * 2,
+        out_specs=pl.BlockSpec(memory_space=pl.ANY),
+        input_output_aliases={0: 0},
         compiler_params=pltpu.CompilerParams(vmem_limit_bytes=MIB),
         cost_estimate=pl.CostEstimate(flops=0, bytes_accessed=0, transcendentals=0),
         name="gate",
-    )(here, *blocks, after)
-    return out[0], list(out[1:])
+    )(block, after)
 
 
 def attend_kernel(score_scale, steps, blocks, owner_ref, weight_ref, *refs):
@@ -286,7 +281,7 @@
 
 
 def finish_kernel(
-    block_columns, radices, here_ref, value_ref, weight_ref, *refs
+    block_columns, count, here_ref, value_ref, weight_ref, *refs
 ):
     messages, (out_ref, attended_scr, head_scr) = refs[:-3], refs[-3:]
     requests, heads_here = messages[0].shape[0] - 1, messages[0].shape[1]
@@ -315,25 +310,21 @@
             preferred_element_type=jnp.float32,
         ).astype(jnp.bfloat16)
         for i in range(per_block):
-            distance = here_ref[0] ^ (j * per_block + i)
-            place = 0
-            for radix in radices:
-                place = place * radix + (distance & (radix - 1))
-                distance = distance >> (radix.bit_length() - 1)
+            ctx, head = divmod(j * per_block + i, owners // count)
+            place = (here_ref[0] ^ head) * count + ctx
             out_ref[place] = product[:, i * width : (i + 1) * width]
 
 
-def finish(here, messages, value_absorb, weight, radices):
+def finish(here, messages, value_absorb, weight, count, owners):
     requests, heads_here = messages[0].shape[0] - 1, messages[0].shape[1]
     latent_size, value_size = value_absorb.shape[1:]
     depth, columns = weight.shape
-    owners = functools.reduce(lambda a, b: a * b, radices)
     width = columns // owners
     block_columns = width
     while block_columns % LANES:
         block_columns *= 2
     return pl.pallas_call(
-        functools.partial(finish_kernel, block_columns, radices),
+        functools.partial(finish_kernel, block_columns, count),
         out_shape=pltpu.VMEM((owners, requests, width), jnp.bfloat16),
         in_specs=[SMEM_SPEC] + [VMEM_SPEC] * (2 + len(messages)),
         out_specs=VMEM_SPEC,
@@ -357,8 +348,8 @@
     rope_size = query_rope.shape[1] // heads_here
     score_scale = (nope_size + rope_size) ** (-0.5)
     count = lax.axis_size("ctx")
-    axes = ("ctx", "head")
-    here = lax.axis_index(axes).astype(jnp.int32).reshape(1)
+    cores = lax.axis_size("head")
+    here = lax.axis_index("head").astype(jnp.int32).reshape(1)
 
     def exchange(x, distance):
         return lax.ppermute(x, "ctx", [(i, i ^ distance) for i in range(count)])
@@ -371,16 +362,15 @@
     own = jnp.concatenate([query_latent, rope.reshape(-1, heads_here, latent_size)], axis=0)
 
     even = [*range(4, count, 2), *range(2, min(4, count), 2)]
-    block_at = {distance: exchange(own, distance) for distance in [*even, 1]}
-    cache_parts = [load(here, latent_cache, 0, CACHE_PARTS, own)]
-    here, (block_at[2], block_at[1]) = gate(here, [block_at[2], block_at[1]], cache_parts[0])
-    for part in range(1, CACHE_PARTS):
-        cache_parts.append(load(here, latent_cache, part, CACHE_PARTS, block_at[2]))
-    block_at[3] = exchange(block_at[2], 1)
+    block_at = {distance: exchange(own, distance) for distance in [*even, 3, 1]}
+    block_at[0] = own
+    cache_parts, last = [], own
+    for part in range(CACHE_PARTS):
+        last = load(here, latent_cache, part, CACHE_PARTS, last)
+        cache_parts.append(last)
     for distance in even[:-1]:
-        _, (block_at[distance],) = gate(here, [block_at[distance]], cache_parts[-1])
+        block_at[distance] = gate(block_at[distance], last)
         block_at[distance ^ 1] = exchange(block_at[distance], 1)
-    block_at[0] = own
 
     message_to, weight = attend(
         [block_at[d] for d in range(count)],
@@ -393,23 +383,19 @@
     ]
     messages = [message_to[0], across[0], *arrived]
 
-    owners = lax.axis_size(axes)
-    radices = [4] * ((owners.bit_length() - 1) // 2) + [2] * ((owners.bit_length() - 1) % 2)
-    pieces = finish(here, messages, value_absorb, weight, radices)
-    unit = 1
-    for radix in radices:
-        share = pieces.shape[0] // radix
-        got = [
-            lax.ppermute(
-                pieces[k * share : (k + 1) * share],
-                axes,
-                [(i, i ^ (k * unit)) for i in range(owners)],
-            )
-            for k in range(1, radix)
-        ]
-        pieces = sum(x.astype(jnp.float32) for x in [pieces[:share], *got]).astype(jnp.bfloat16)
-        unit *= radix
-    return pieces[0]
+    pieces = finish(here, messages, value_absorb, weight, count, count * cores)
+    total = pieces[:count].astype(jnp.float32)
+    for distance in range(1, cores):
+        got = lax.ppermute(
+            pieces[distance * count : (distance + 1) * count],
+            "head",
+            [(i, i ^ distance) for i in range(cores)],
+        )
+        total = total + got.astype(jnp.float32)
+    pieces = lax.all_to_all(
+        total.astype(jnp.bfloat16), "ctx", split_axis=0, concat_axis=0, tiled=True
+    )
+    return jnp.sum(pieces.astype(jnp.float32), axis=0).astype(jnp.bfloat16)
 
 
 def solution(mesh):

time: 78.6 us -> 76 us (0.967)
  blocking collectives: 0 us -> 11.5 us
  waiting for transfers between devices: 20.9 us -> 15.5 us
  starting transfers between devices: 25.9 us -> 21.1 us
  Pallas kernels: 28.3 us -> 24.3 us
    all_to_all x0 -> x1, blocking collectives: none -> 11.5 us  [body(): lax.all_to_all(total.astype(jnp.bfloat16), 'ctx', split_axis=0, concat_ax...]
    ppermute x6 -> x1, waiting for transfers between devices: 7.88 us -> 1.33 us  [body(): lax.ppermute(pieces[distance * count:(distance + 1) * count], 'head', [(i...]
    ppermute x6 -> x1, starting transfers between devices: 5.77 us -> 0.07 us  [body(): lax.ppermute(pieces[distance * count:(distance + 1) * count], 'head', [(i...]
    pallas_call x4 -> x3, Pallas kernels: 6.81 us -> 3.37 us  [the longest x1 3.37 us: finish(): pl.pallas_call(functools.partial(finish_kernel, block_columns, count), ou...]
    ppermute x14, waiting for transfers between devices: 13 us -> 14.2 us  [exchange(): return lax.ppermute(x, 'ctx', [(i, i ^ distance) for i in range(count)])]
    ppermute x14, starting transfers between devices: 20.1 us -> 21.1 us  [exchange(): return lax.ppermute(x, 'ctx', [(i, i ^ distance) for i in range(count)])]
  transfers between devices with their start and end apart: 20 -> 15, of which waited for: 12 -> 8; matrix products, arithmetic and copies ran while one was open for 0% -> 0% of each run, Pallas kernels for 14% -> 10%
where the time goes in v8:
time: 76 us; the launch traced here: 75.6 us
  Pallas kernels  24.3 us (32%)
  starting transfers between devices  21.1 us (28%)
  waiting for transfers between devices  15.5 us (20%)
  blocking collectives  11.5 us (15%)
  local copies, waits for them, and re-layouts  1.36 us (2%)
  matrix products  0.99 us (1%)
    ppermute x14, starting transfers between devices, exchange(): return lax.ppermute(x, 'ctx', [(i, i ^ distance) for i in range(count)])  21.1 us
    ppermute x14, waiting for transfers between devices, exchange(): return lax.ppermute(x, 'ctx', [(i, i ^ distance) for i in range(count)])  14.2 us
    pallas_call x1, Pallas kernels, attend(): pl.pallas_call(functools.partial(attend_kernel, score_scale, steps, block...  13.3 us
    all_to_all x1, blocking collectives, body(): lax.all_to_all(total.astype(jnp.bfloat16), 'ctx', split_axis=0, concat_ax...  11.5 us
    pallas_call x2, Pallas kernels, load(): pl.pallas_call(functools.partial(load_kernel, part * pages), out_shape=pl...  7.23 us
    pallas_call x1, Pallas kernels, finish(): pl.pallas_call(functools.partial(finish_kernel, block_columns, count), ou...  3.37 us
  transfers between devices with their start and end apart: 15, of which 8 were waited for; matrix products, arithmetic and copies ran while one was open for 0% of the time, Pallas kernels for 10%

profile of v8, /device:TPU:0, one launch (start us, length us, event | category | flops | bytes accessed | tf_op | source)
XLA Modules:
  0.0 75.6 jit_solution(3404744567221683996)
XLA Ops:
  0.0 0.9 %reshape.10 = bf16[2,8,8,64]{3,2,1,0:T(8,128)(2,1)S(1)} reshape(bf16[16,512]{1,0:T(8,128)(2,1)} %param.8) | data formatting | bytes 32768 | tf_op jit(solution)/shard_map/reshape | solution.py:361
  1.2 1.0 %fusion.1 = bf16[8,512,16]{1,2,0:T(8,128)(2,1)S(1)} fusion(bf16[8,128,512]{2,1,0:T(8,128)(2,1)S(1)} %copy-done, bf16[16,8,128]{2,1,0:T(8,128)(2,1)} %param.7), kind=kOutput, calls=%fused_computation.5 | convolution fusion | flops 16777216 | bytes 1212416 | tf_op jit(solution)/shard_map/rhn,hnl->rhl/dot_general | solution.py:357
  2.4 4.1 %collective-permute-start.3 = (bf16[18,8,512]{2,1,0:T(8,128)(2,1)S(1)}, bf16[18,8,512]{2,1,0:T(8,128)(2,1)S(1)}, u32[]{:S(2)}, u32[]{:S(2)}) collective-permute-start(bf16[18,8,512]{2,1,0:T(8,128)(2,1)S(1)} %pad_maximum_fusion.after_ref.refs_2_), channel_id=1, source_target_pairs={{0,8},{2,10},{4,12},{6,14},{8,0},{10,2},{12,4},{14,6},{1,9},{3,11}... | collective-permute-start | bytes 442376 | tf_op jit(solution)/shard_map/ppermute | solution.py:355
  6.5 1.3 %collective-permute-start.5 = (bf16[18,8,512]{2,1,0:T(8,128)(2,1)S(1)}, bf16[18,8,512]{2,1,0:T(8,128)(2,1)S(1)}, u32[]{:S(2)}, u32[]{:S(2)}) collective-permute-start(bf16[18,8,512]{2,1,0:T(8,128)(2,1)S(1)} %pad_maximum_fusion.after_ref.refs_2_), channel_id=1, source_target_pairs={{0,12},{2,14},{4,8},{6,10},{8,4},{10,6},{12,0},{14,2},{1,13},{3,15... | collective-permute-start | bytes 442376 | tf_op jit(solution)/shard_map/ppermute | solution.py:355
  7.8 1.2 %collective-permute-start.2 = (bf16[18,8,512]{2,1,0:T(8,128)(2,1)S(1)}, bf16[18,8,512]{2,1,0:T(8,128)(2,1)S(1)}, u32[]{:S(2)}, u32[]{:S(2)}) collective-permute-start(bf16[18,8,512]{2,1,0:T(8,128)(2,1)S(1)} %pad_maximum_fusion.after_ref.refs_2_), channel_id=1, source_target_pairs={{0,6},{2,4},{4,2},{6,0},{8,14},{10,12},{12,10},{14,8},{1,7},{3,5},... | collective-permute-start | bytes 442376 | tf_op jit(solution)/shard_map/ppermute | solution.py:355
  9.0 1.8 %collective-permute-start.1 = (bf16[18,8,512]{2,1,0:T(8,128)(2,1)S(1)}, bf16[18,8,512]{2,1,0:T(8,128)(2,1)S(1)}, u32[]{:S(2)}, u32[]{:S(2)}) collective-permute-start(bf16[18,8,512]{2,1,0:T(8,128)(2,1)S(1)} %pad_maximum_fusion.after_ref.refs_2_), channel_id=1, source_target_pairs={{0,4},{2,6},{4,0},{6,2},{8,12},{10,14},{12,8},{14,10},{1,5},{3,7},... | collective-permute-start | bytes 442376 | tf_op jit(solution)/shard_map/ppermute | solution.py:355
  11.3 3.6 %load.2.after_ref.refs_0_ = bf16[112,64,576]{2,1,0:T(8,128)(2,1)S(1)} custom-call(s32[1]{0:T(128)} %bitcast.here_ref, bf16[224,64,576]{2,1,0:T(8,128)(2,1)} %cache_ref.3, bf16[18,8,512]{2,1,0:T(8,128)(2,1)S(1)} %pad_maximum_fusion.after_ref.refs_2_), custom_call_target="tpu_custom_call" | custom-call | bytes 8257536 | tf_op jit(solution)/shard_map/load/pallas_call | solution.py:52
  14.9 3.6 %load.3.after_ref.refs_1_ = bf16[112,64,576]{2,1,0:T(8,128)(2,1)S(1)} custom-call(s32[1]{0:T(128)} %bitcast.here_ref, bf16[224,64,576]{2,1,0:T(8,128)(2,1)} %cache_ref.3, bf16[112,64,576]{2,1,0:T(8,128)(2,1)S(1)} %load.2.after_ref.refs_0_), custom_call_target="tpu_custom_call" | custom-call | bytes 8257536 | tf_op jit(solution)/shard_map/load/pallas_call | solution.py:52
  18.6 1.6 %collective-permute-start.4 = (bf16[18,8,512]{2,1,0:T(8,128)(2,1)S(1)}, bf16[18,8,512]{2,1,0:T(8,128)(2,1)S(1)}, u32[]{:S(2)}, u32[]{:S(2)}) collective-permute-start(bf16[18,8,512]{2,1,0:T(8,128)(2,1)S(1)} %gate.2.refs_6_), channel_id=1, source_target_pairs={{0,2},{2,0},{4,6},{6,4},{8,10},{10,8},{12,14},{14,12},{1,3},{3,1},... | collective-permute-start | bytes 442376 | tf_op jit(solution)/shard_map/ppermute | solution.py:355
  20.7 1.4 %collective-permute-done.1.refs_4_ = bf16[18,8,512]{2,1,0:T(8,128)(2,1)S(1)} collective-permute-done((bf16[18,8,512]{2,1,0:T(8,128)(2,1)S(1)}, bf16[18,8,512]{2,1,0:T(8,128)(2,1)S(1)}, u32[]{:S(2)}, u32[]{:S(2)}) %collective-permute-start.1) | collective-permute-done | bytes 147488 | tf_op jit(solution)/shard_map/ppermute | solution.py:355
  22.0 2.7 %collective-permute-done.4.refs_7_ = bf16[18,8,512]{2,1,0:T(8,128)(2,1)S(1)} collective-permute-done((bf16[18,8,512]{2,1,0:T(8,128)(2,1)S(1)}, bf16[18,8,512]{2,1,0:T(8,128)(2,1)S(1)}, u32[]{:S(2)}, u32[]{:S(2)}) %collective-permute-start.4) | collective-permute-done | bytes 147488 | tf_op jit(solution)/shard_map/ppermute | solution.py:355
  24.7 1.6 %collective-permute-done.6.refs_9_ = bf16[18,8,512]{2,1,0:T(8,128)(2,1)S(1)} collective-permute-done((bf16[18,8,512]{2,1,0:T(8,128)(2,1)S(1)}, bf16[18,8,512]{2,1,0:T(8,128)(2,1)S(1)}, u32[]{:S(2)}, u32[]{:S(2)}) %collective-permute-start.6) | collective-permute-done | bytes 147488 | tf_op jit(solution)/shard_map/ppermute | solution.py:355
  26.3 13.3 %attend.1 = (bf16[17,8,512]{2,1,0:T(8,128)(2,1)S(1)}, bf16[17,8,512]{2,1,0:T(8,128)(2,1)S(1)}, bf16[17,8,512]{2,1,0:T(8,128)(2,1)S(1)}, bf16[17,8,512]{2,1,0:T(8...) custom-call(s32[224]{0:T(256)S(1)} %copy-done.3, ...), custom_call_target="tpu_custom_call" | custom-call | flops 7985954816 | bytes 16515072 | tf_op jit(solution)/shard_map/attend/pallas_call | solution.py:223
  39.6 1.3 %collective-permute-start.8 = (bf16[17,8,512]{2,1,0:T(8,128)(2,1)S(1)}, bf16[17,8,512]{2,1,0:T(8,128)(2,1)S(1)}, u32[]{:S(2)}, u32[]{:S(2)}) collective-permute-start(bf16[17,8,512]{2,1,0:T(8,128)(2,1)S(1)} %get-tuple-element.18), channel_id=1, source_target_pairs={{0,2},{2,0},{4,6},{6,4},{8,10},{10,8},{12,14},{14,12},{1,3},{3,1},... | collective-permute-start | bytes 417800 | tf_op jit(solution)/shard_map/ppermute | solution.py:355
  40.9 0.8 %collective-permute-start.10 = (bf16[17,8,512]{2,1,0:T(8,128)(2,1)S(1)}, bf16[17,8,512]{2,1,0:T(8,128)(2,1)S(1)}, u32[]{:S(2)}, u32[]{:S(2)}) collective-permute-start(bf16[17,8,512]{2,1,0:T(8,128)(2,1)S(1)} %get-tuple-element.20), channel_id=1, source_target_pairs={{0,2},{2,0},{4,6},{6,4},{8,10},{10,8},{12,14},{14,12},{1,3},{3,1},... | collective-permute-start | bytes 417800 | tf_op jit(solution)/shard_map/ppermute | solution.py:355
  41.7 1.2 %collective-permute-start.12 = (bf16[17,8,512]{2,1,0:T(8,128)(2,1)S(1)}, bf16[17,8,512]{2,1,0:T(8,128)(2,1)S(1)}, u32[]{:S(2)}, u32[]{:S(2)}) collective-permute-start(bf16[17,8,512]{2,1,0:T(8,128)(2,1)S(1)} %get-tuple-element.22), channel_id=1, source_target_pairs={{0,2},{2,0},{4,6},{6,4},{8,10},{10,8},{12,14},{14,12},{1,3},{3,1},... | collective-permute-start | bytes 417800 | tf_op jit(solution)/shard_map/ppermute | solution.py:355
  43.7 2.6 %collective-permute-done.8.got_ref = bf16[17,8,512]{2,1,0:T(8,128)(2,1)S(1)} collective-permute-done((bf16[17,8,512]{2,1,0:T(8,128)(2,1)S(1)}, bf16[17,8,512]{2,1,0:T(8,128)(2,1)S(1)}, u32[]{:S(2)}, u32[]{:S(2)}) %collective-permute-start.8) | collective-permute-done | bytes 139296 | tf_op jit(solution)/shard_map/ppermute | solution.py:355
  46.4 2.3 %collective-permute-start.9 = (bf16[17,8,512]{2,1,0:T(8,128)(2,1)S(1)}, bf16[17,8,512]{2,1,0:T(8,128)(2,1)S(1)}, u32[]{:S(2)}, u32[]{:S(2)}) collective-permute-start(bf16[17,8,512]{2,1,0:T(8,128)(2,1)S(1)} %merge.3), channel_id=1, source_target_pairs={{0,8},{2,10},{4,12},{6,14},{8,0},{10,2},{12,4},{14,6},{1,9},{3,11}... | collective-permute-start | bytes 417800 | tf_op jit(solution)/shard_map/ppermute | solution.py:355
  49.2 3.5 %collective-permute-start.11 = (bf16[17,8,512]{2,1,0:T(8,128)(2,1)S(1)}, bf16[17,8,512]{2,1,0:T(8,128)(2,1)S(1)}, u32[]{:S(2)}, u32[]{:S(2)}) collective-permute-start(bf16[17,8,512]{2,1,0:T(8,128)(2,1)S(1)} %merge.4), channel_id=1, source_target_pairs={{0,12},{2,14},{4,8},{6,10},{8,4},{10,6},{12,0},{14,2},{1,13},{3,15... | collective-permute-start | bytes 417800 | tf_op jit(solution)/shard_map/ppermute | solution.py:355
  53.0 4.2 %collective-permute-done.9.refs_2_ = bf16[17,8,512]{2,1,0:T(8,128)(2,1)S(1)} collective-permute-done((bf16[17,8,512]{2,1,0:T(8,128)(2,1)S(1)}, bf16[17,8,512]{2,1,0:T(8,128)(2,1)S(1)}, u32[]{:S(2)}, u32[]{:S(2)}) %collective-permute-start.9) | collective-permute-done | bytes 139296 | tf_op jit(solution)/shard_map/ppermute | solution.py:355
  57.2 1.4 %collective-permute-done.13.refs_4_ = bf16[17,8,512]{2,1,0:T(8,128)(2,1)S(1)} collective-permute-done((bf16[17,8,512]{2,1,0:T(8,128)(2,1)S(1)}, bf16[17,8,512]{2,1,0:T(8,128)(2,1)S(1)}, u32[]{:S(2)}, u32[]{:S(2)}) %collective-permute-start.13) | collective-permute-done | bytes 139296 | tf_op jit(solution)/shard_map/ppermute | solution.py:355
  58.7 3.4 %finish.1 = bf16[16,16,448]{2,1,0:T(8,128)(2,1)S(1)} custom-call(s32[1]{0:T(128)} %bitcast.here_ref, bf16[8,512,128]{2,1,0:T(8,128)(2,1)S(1)} %copy-done.2, bf16[1024,7168]{1,0:T(8,128)(2,1)S(1)} %get-tuple-element.14.weight_ref, bf16[17,8,512]{2,1,0:T(8,128)(2,1)S(1)} %get-tuple-element.15.refs_0_, bf16[17,8,512]{2,1,0:T(8,128)(2,1)S(1)} %collective-permute-done.7.refs_1_, ...), custom_call_target="tpu_custom_call" | custom-call | flops 3758096384 | tf_op jit(solution)/shard_map/finish/pallas_call | solution.py:326
  62.1 1.3 %collective-permute-done.14 = bf16[8,16,448]{2,1,0:T(8,128)(2,1)S(1)} collective-permute-done((bf16[8,16,448]{2,1,0:T(8,128)(2,1)S(1)}, bf16[8,16,448]{2,1,0:T(8,128)(2,1)S(1)}, u32[]{:S(2)}, u32[]{:S(2)}) %collective-permute-start.14) | collective-permute-done | bytes 114720 | tf_op jit(solution)/shard_map/ppermute | solution.py:389
  63.5 11.5 %all_to_all.5 = bf16[8,16,448]{2,1,0:T(8,128)(2,1)S(1)} all-to-all(bf16[8,16,448]{2,1,0:T(8,128)(2,1)S(1)} %add_convert_fusion), channel_id=1, replica_groups=mesh['groups'=2,'ctx'=8,'head'=2] {'ctx'}, dimensions={0} | all-to-all | bytes 229376 | tf_op jit(solution)/shard_map/all_to_all | solution.py:395
  (33 shorter events, 4.0 us)
Async XLA Ops:
  0.0 1.2 %copy-start = (bf16[8,128,512]{2,1,0:T(8,128)(2,1)S(1)}, bf16[8,128,512]{2,1,0:T(8,128)(2,1)}, u32[]{:S(2)}) copy-start(bf16[8,128,512]{2,1,0:T(8,128)(2,1)} %param.9) | copy-start | bytes 3145732
  2.4 16.2 %collective-permute-start.3 = (bf16[18,8,512]{2,1,0:T(8,128)(2,1)S(1)}, bf16[18,8,512]{2,1,0:T(8,128)(2,1)S(1)}, u32[]{:S(2)}, u32[]{:S(2)}) collective-permute-start(bf16[18,8,512]{2,1,0:T(8,128)(2,1)S(1)} %pad_maximum_fusion.after_ref.refs_2_), channel_id=1, source_target_pairs={{0,8},{2,10},{4,12},{6,14},{8,0},{10,2},{12,4},{14,6},{1,9},{3,11}... | collective-permute-start | bytes 442376 | tf_op jit(solution)/shard_map/ppermute | solution.py:355
  6.5 13.7 %collective-permute-start.5 = (bf16[18,8,512]{2,1,0:T(8,128)(2,1)S(1)}, bf16[18,8,512]{2,1,0:T(8,128)(2,1)S(1)}, u32[]{:S(2)}, u32[]{:S(2)}) collective-permute-start(bf16[18,8,512]{2,1,0:T(8,128)(2,1)S(1)} %pad_maximum_fusion.after_ref.refs_2_), channel_id=1, source_target_pairs={{0,12},{2,14},{4,8},{6,10},{8,4},{10,6},{12,0},{14,2},{1,13},{3,15... | collective-permute-start | bytes 442376 | tf_op jit(solution)/shard_map/ppermute | solution.py:355
  7.8 12.9 %collective-permute-start.2 = (bf16[18,8,512]{2,1,0:T(8,128)(2,1)S(1)}, bf16[18,8,512]{2,1,0:T(8,128)(2,1)S(1)}, u32[]{:S(2)}, u32[]{:S(2)}) collective-permute-start(bf16[18,8,512]{2,1,0:T(8,128)(2,1)S(1)} %pad_maximum_fusion.after_ref.refs_2_), channel_id=1, source_target_pairs={{0,6},{2,4},{4,2},{6,0},{8,14},{10,12},{12,10},{14,8},{1,7},{3,5},... | collective-permute-start | bytes 442376 | tf_op jit(solution)/shard_map/ppermute | solution.py:355
  9.0 13.0 %collective-permute-start.1 = (bf16[18,8,512]{2,1,0:T(8,128)(2,1)S(1)}, bf16[18,8,512]{2,1,0:T(8,128)(2,1)S(1)}, u32[]{:S(2)}, u32[]{:S(2)}) collective-permute-start(bf16[18,8,512]{2,1,0:T(8,128)(2,1)S(1)} %pad_maximum_fusion.after_ref.refs_2_), channel_id=1, source_target_pairs={{0,4},{2,6},{4,0},{6,2},{8,12},{10,14},{12,8},{14,10},{1,5},{3,7},... | collective-permute-start | bytes 442376 | tf_op jit(solution)/shard_map/ppermute | solution.py:355
  10.8 11.3 %collective-permute-start = (bf16[18,8,512]{2,1,0:T(8,128)(2,1)S(1)}, bf16[18,8,512]{2,1,0:T(8,128)(2,1)S(1)}, u32[]{:S(2)}, u32[]{:S(2)}) collective-permute-start(bf16[18,8,512]{2,1,0:T(8,128)(2,1)S(1)} %pad_maximum_fusion.after_ref.refs_2_), channel_id=1, source_target_pairs={{0,2},{2,0},{4,6},{6,4},{8,10},{10,8},{12,14},{14,12},{1,3},{3,1},... | collective-permute-start | bytes 442376 | tf_op jit(solution)/shard_map/ppermute | solution.py:355
  18.5 7.8 %copy-start.3 = (s32[224]{0:T(256)S(1)}, s32[224]{0:T(256)}, u32[]{:S(2)}) copy-start(s32[224]{0:T(256)} %owner_ref.1) | copy-start | bytes 2692
  18.6 6.1 %collective-permute-start.4 = (bf16[18,8,512]{2,1,0:T(8,128)(2,1)S(1)}, bf16[18,8,512]{2,1,0:T(8,128)(2,1)S(1)}, u32[]{:S(2)}, u32[]{:S(2)}) collective-permute-start(bf16[18,8,512]{2,1,0:T(8,128)(2,1)S(1)} %gate.2.refs_6_), channel_id=1, source_target_pairs={{0,2},{2,0},{4,6},{6,4},{8,10},{10,8},{12,14},{14,12},{1,3},{3,1},... | collective-permute-start | bytes 442376 | tf_op jit(solution)/shard_map/ppermute | solution.py:355
  20.2 38.5 %copy-start.2 = (bf16[8,512,128]{2,1,0:T(8,128)(2,1)S(1)}, bf16[8,512,128]{2,1,0:T(8,128)(2,1)}, u32[]{:S(2)}) copy-start(bf16[8,512,128]{2,1,0:T(8,128)(2,1)} %value_ref.1) | copy-start | bytes 3145732
  20.2 6.1 %collective-permute-start.6 = (bf16[18,8,512]{2,1,0:T(8,128)(2,1)S(1)}, bf16[18,8,512]{2,1,0:T(8,128)(2,1)S(1)}, u32[]{:S(2)}, u32[]{:S(2)}) collective-permute-start(bf16[18,8,512]{2,1,0:T(8,128)(2,1)S(1)} %gate.3.refs_8_), channel_id=1, source_target_pairs={{0,2},{2,0},{4,6},{6,4},{8,10},{10,8},{12,14},{14,12},{1,3},{3,1},... | collective-permute-start | bytes 442376 | tf_op jit(solution)/shard_map/ppermute | solution.py:355
  26.3 49.3 %copy-start.1 = (bf16[8,128,512]{2,1,0:T(8,128)(2,1)S(1)}, bf16[8,128,512]{2,1,0:T(8,128)(2,1)}, u32[]{:S(2)}) copy-start(bf16[8,128,512]{2,1,0:T(8,128)(2,1)} %param.9) | copy-start | bytes 3145732
  39.6 6.7 %collective-permute-start.8 = (bf16[17,8,512]{2,1,0:T(8,128)(2,1)S(1)}, bf16[17,8,512]{2,1,0:T(8,128)(2,1)S(1)}, u32[]{:S(2)}, u32[]{:S(2)}) collective-permute-start(bf16[17,8,512]{2,1,0:T(8,128)(2,1)S(1)} %get-tuple-element.18), channel_id=1, source_target_pairs={{0,2},{2,0},{4,6},{6,4},{8,10},{10,8},{12,14},{14,12},{1,3},{3,1},... | collective-permute-start | bytes 417800 | tf_op jit(solution)/shard_map/ppermute | solution.py:355
  40.9 8.2 %collective-permute-start.10 = (bf16[17,8,512]{2,1,0:T(8,128)(2,1)S(1)}, bf16[17,8,512]{2,1,0:T(8,128)(2,1)S(1)}, u32[]{:S(2)}, u32[]{:S(2)}) collective-permute-start(bf16[17,8,512]{2,1,0:T(8,128)(2,1)S(1)} %get-tuple-element.20), channel_id=1, source_target_pairs={{0,2},{2,0},{4,6},{6,4},{8,10},{10,8},{12,14},{14,12},{1,3},{3,1},... | collective-permute-start | bytes 417800 | tf_op jit(solution)/shard_map/ppermute | solution.py:355
  41.7 11.0 %collective-permute-start.12 = (bf16[17,8,512]{2,1,0:T(8,128)(2,1)S(1)}, bf16[17,8,512]{2,1,0:T(8,128)(2,1)S(1)}, u32[]{:S(2)}, u32[]{:S(2)}) collective-permute-start(bf16[17,8,512]{2,1,0:T(8,128)(2,1)S(1)} %get-tuple-element.22), channel_id=1, source_target_pairs={{0,2},{2,0},{4,6},{6,4},{8,10},{10,8},{12,14},{14,12},{1,3},{3,1},... | collective-permute-start | bytes 417800 | tf_op jit(solution)/shard_map/ppermute | solution.py:355
  42.9 10.1 %collective-permute-start.7 = (bf16[17,8,512]{2,1,0:T(8,128)(2,1)S(1)}, bf16[17,8,512]{2,1,0:T(8,128)(2,1)S(1)}, u32[]{:S(2)}, u32[]{:S(2)}) collective-permute-start(bf16[17,8,512]{2,1,0:T(8,128)(2,1)S(1)} %get-tuple-element.16), channel_id=1, source_target_pairs={{0,2},{2,0},{4,6},{6,4},{8,10},{10,8},{12,14},{14,12},{1,3},{3,1},... | collective-permute-start | bytes 417800 | tf_op jit(solution)/shard_map/ppermute | solution.py:355
  46.4 10.8 %collective-permute-start.9 = (bf16[17,8,512]{2,1,0:T(8,128)(2,1)S(1)}, bf16[17,8,512]{2,1,0:T(8,128)(2,1)S(1)}, u32[]{:S(2)}, u32[]{:S(2)}) collective-permute-start(bf16[17,8,512]{2,1,0:T(8,128)(2,1)S(1)} %merge.3), channel_id=1, source_target_pairs={{0,8},{2,10},{4,12},{6,14},{8,0},{10,2},{12,4},{14,6},{1,9},{3,11}... | collective-permute-start | bytes 417800 | tf_op jit(solution)/shard_map/ppermute | solution.py:355
  49.2 8.0 %collective-permute-start.11 = (bf16[17,8,512]{2,1,0:T(8,128)(2,1)S(1)}, bf16[17,8,512]{2,1,0:T(8,128)(2,1)S(1)}, u32[]{:S(2)}, u32[]{:S(2)}) collective-permute-start(bf16[17,8,512]{2,1,0:T(8,128)(2,1)S(1)} %merge.4), channel_id=1, source_target_pairs={{0,12},{2,14},{4,8},{6,10},{8,4},{10,6},{12,0},{14,2},{1,13},{3,15... | collective-permute-start | bytes 417800 | tf_op jit(solution)/shard_map/ppermute | solution.py:355
  52.9 5.8 %collective-permute-start.13 = (bf16[17,8,512]{2,1,0:T(8,128)(2,1)S(1)}, bf16[17,8,512]{2,1,0:T(8,128)(2,1)S(1)}, u32[]{:S(2)}, u32[]{:S(2)}) collective-permute-start(bf16[17,8,512]{2,1,0:T(8,128)(2,1)S(1)} %merge.5), channel_id=1, source_target_pairs={{0,4},{2,6},{4,0},{6,2},{8,12},{10,14},{12,8},{14,10},{1,5},{3,7},... | collective-permute-start | bytes 417800 | tf_op jit(solution)/shard_map/ppermute | solution.py:355
  62.0 1.4 %collective-permute-start.14 = (bf16[8,16,448]{2,1,0:T(8,128)(2,1)S(1)}, bf16[8,16,448]{2,1,0:T(8,128)(2,1)S(1)}, u32[]{:S(2)}, u32[]{:S(2)}) collective-permute-start(bf16[8,16,448]{2,1,0:T(8,128)(2,1)S(1)} %slice.9), channel_id=1, source_target_pairs={{0,1},{1,0},{2,3},{3,2},{4,5},{5,4},{6,7},{7,6},{8,9},{9,8},{10,11... | collective-permute-start | bytes 344072 | tf_op jit(solution)/shard_map/ppermute | solution.py:389

commit v9 on v8

--- a/solution.py
+++ b/solution.py
@@ -364,13 +364,12 @@
     even = [*range(4, count, 2), *range(2, min(4, count), 2)]
     block_at = {distance: exchange(own, distance) for distance in [*even, 3, 1]}
     block_at[0] = own
-    cache_parts, last = [], own
-    for part in range(CACHE_PARTS):
-        last = load(here, latent_cache, part, CACHE_PARTS, last)
-        cache_parts.append(last)
+    cache_parts = [load(here, latent_cache, 0, CACHE_PARTS, own)]
     for distance in even[:-1]:
-        block_at[distance] = gate(block_at[distance], last)
+        block_at[distance] = gate(block_at[distance], cache_parts[0])
         block_at[distance ^ 1] = exchange(block_at[distance], 1)
+    for part in range(1, CACHE_PARTS):
+        cache_parts.append(load(here, latent_cache, part, CACHE_PARTS, block_at[count - 2]))
 
     message_to, weight = attend(
         [block_at[d] for d in range(count)],

time: 76 us -> 76.4 us (level)
  blocking collectives: 11.5 us -> 12.4 us
  waiting for transfers between devices: 15.5 us -> 14.7 us
    all_to_all x1, blocking collectives: 11.5 us -> 12.4 us  [body(): lax.all_to_all(total.astype(jnp.bfloat16), 'ctx', split_axis=0, concat_ax...]
    ppermute x14, waiting for transfers between devices: 14.2 us -> 13.4 us  [exchange(): return lax.ppermute(x, 'ctx', [(i, i ^ distance) for i in range(count)])]
  transfers between devices with their start and end apart: 15 -> 15, of which waited for: 8 -> 9; matrix products, arithmetic and copies ran while one was open for 0% -> 0% of each run, Pallas kernels for 10% -> 10%
where the time goes in v9:
time: 76.4 us; the launch traced here: 76.2 us
  Pallas kernels  24.3 us (32%)
  starting transfers between devices  21.6 us (28%)
  waiting for transfers between devices  14.7 us (19%)
  blocking collectives  12.4 us (16%)
  local copies, waits for them, and re-layouts  1.36 us (2%)
  matrix products  0.99 us (1%)
    ppermute x14, starting transfers between devices, exchange(): return lax.ppermute(x, 'ctx', [(i, i ^ distance) for i in range(count)])  21.6 us
    ppermute x14, waiting for transfers between devices, exchange(): return lax.ppermute(x, 'ctx', [(i, i ^ distance) for i in range(count)])  13.4 us
    pallas_call x1, Pallas kernels, attend(): pl.pallas_call(functools.partial(attend_kernel, score_scale, steps, block...  13.2 us
    all_to_all x1, blocking collectives, body(): lax.all_to_all(total.astype(jnp.bfloat16), 'ctx', split_axis=0, concat_ax...  12.4 us
    pallas_call x2, Pallas kernels, load(): pl.pallas_call(functools.partial(load_kernel, part * pages), out_shape=pl...  7.23 us
    pallas_call x1, Pallas kernels, finish(): pl.pallas_call(functools.partial(finish_kernel, block_columns, count), ou...  3.36 us
  transfers between devices with their start and end apart: 15, of which 9 were waited for; matrix products, arithmetic and copies ran while one was open for 0% of the time, Pallas kernels for 10%

profile of v9, /device:TPU:0, one launch (start us, length us, event | category | flops | bytes accessed | tf_op | source)
XLA Modules:
  0.0 76.2 jit_solution(2256532544750303339)
XLA Ops:
  0.0 0.9 %reshape.10 = bf16[2,8,8,64]{3,2,1,0:T(8,128)(2,1)S(1)} reshape(bf16[16,512]{1,0:T(8,128)(2,1)} %param.8) | data formatting | bytes 32768 | tf_op jit(solution)/shard_map/reshape | solution.py:361
  1.2 1.0 %fusion.1 = bf16[8,512,16]{1,2,0:T(8,128)(2,1)S(1)} fusion(bf16[8,128,512]{2,1,0:T(8,128)(2,1)S(1)} %copy-done, bf16[16,8,128]{2,1,0:T(8,128)(2,1)} %param.7), kind=kOutput, calls=%fused_computation.5 | convolution fusion | flops 16777216 | bytes 1212416 | tf_op jit(solution)/shard_map/rhn,hnl->rhl/dot_general | solution.py:357
  2.4 4.1 %collective-permute-start.4 = (bf16[18,8,512]{2,1,0:T(8,128)(2,1)S(1)}, bf16[18,8,512]{2,1,0:T(8,128)(2,1)S(1)}, u32[]{:S(2)}, u32[]{:S(2)}) collective-permute-start(bf16[18,8,512]{2,1,0:T(8,128)(2,1)S(1)} %pad_maximum_fusion.after_ref.refs_2_), channel_id=1, source_target_pairs={{0,8},{2,10},{4,12},{6,14},{8,0},{10,2},{12,4},{14,6},{1,9},{3,11}... | collective-permute-start | bytes 442376 | tf_op jit(solution)/shard_map/ppermute | solution.py:355
  6.5 1.3 %collective-permute-start = (bf16[18,8,512]{2,1,0:T(8,128)(2,1)S(1)}, bf16[18,8,512]{2,1,0:T(8,128)(2,1)S(1)}, u32[]{:S(2)}, u32[]{:S(2)}) collective-permute-start(bf16[18,8,512]{2,1,0:T(8,128)(2,1)S(1)} %pad_maximum_fusion.after_ref.refs_2_), channel_id=1, source_target_pairs={{0,12},{2,14},{4,8},{6,10},{8,4},{10,6},{12,0},{14,2},{1,13},{3,15... | collective-permute-start | bytes 442376 | tf_op jit(solution)/shard_map/ppermute | solution.py:355
  7.8 1.2 %collective-permute-start.3 = (bf16[18,8,512]{2,1,0:T(8,128)(2,1)S(1)}, bf16[18,8,512]{2,1,0:T(8,128)(2,1)S(1)}, u32[]{:S(2)}, u32[]{:S(2)}) collective-permute-start(bf16[18,8,512]{2,1,0:T(8,128)(2,1)S(1)} %pad_maximum_fusion.after_ref.refs_2_), channel_id=1, source_target_pairs={{0,6},{2,4},{4,2},{6,0},{8,14},{10,12},{12,10},{14,8},{1,7},{3,5},... | collective-permute-start | bytes 442376 | tf_op jit(solution)/shard_map/ppermute | solution.py:355
  9.0 1.8 %collective-permute-start.2 = (bf16[18,8,512]{2,1,0:T(8,128)(2,1)S(1)}, bf16[18,8,512]{2,1,0:T(8,128)(2,1)S(1)}, u32[]{:S(2)}, u32[]{:S(2)}) collective-permute-start(bf16[18,8,512]{2,1,0:T(8,128)(2,1)S(1)} %pad_maximum_fusion.after_ref.refs_2_), channel_id=1, source_target_pairs={{0,4},{2,6},{4,0},{6,2},{8,12},{10,14},{12,8},{14,10},{1,5},{3,7},... | collective-permute-start | bytes 442376 | tf_op jit(solution)/shard_map/ppermute | solution.py:355
  11.3 3.6 %load.2.after_ref.refs_0_ = bf16[112,64,576]{2,1,0:T(8,128)(2,1)S(1)} custom-call(s32[1]{0:T(128)} %bitcast.here_ref, bf16[224,64,576]{2,1,0:T(8,128)(2,1)} %cache_ref.3, bf16[18,8,512]{2,1,0:T(8,128)(2,1)S(1)} %pad_maximum_fusion.after_ref.refs_2_), custom_call_target="tpu_custom_call" | custom-call | bytes 8257536 | tf_op jit(solution)/shard_map/load/pallas_call | solution.py:52
  14.9 2.6 %collective-permute-done.4.block_ref = bf16[18,8,512]{2,1,0:T(8,128)(2,1)S(1)} collective-permute-done((bf16[18,8,512]{2,1,0:T(8,128)(2,1)S(1)}, bf16[18,8,512]{2,1,0:T(8,128)(2,1)S(1)}, u32[]{:S(2)}, u32[]{:S(2)}) %collective-permute-start.4) | collective-permute-done | bytes 147488 | tf_op jit(solution)/shard_map/ppermute | solution.py:355
  17.5 1.9 %collective-permute-start.5 = (bf16[18,8,512]{2,1,0:T(8,128)(2,1)S(1)}, bf16[18,8,512]{2,1,0:T(8,128)(2,1)S(1)}, u32[]{:S(2)}, u32[]{:S(2)}) collective-permute-start(bf16[18,8,512]{2,1,0:T(8,128)(2,1)S(1)} %gate.3.refs_6_), channel_id=1, source_target_pairs={{0,2},{2,0},{4,6},{6,4},{8,10},{10,8},{12,14},{14,12},{1,3},{3,1},... | collective-permute-start | bytes 442376 | tf_op jit(solution)/shard_map/ppermute | solution.py:355
  19.5 3.6 %load.3.refs_1_ = bf16[112,64,576]{2,1,0:T(8,128)(2,1)S(1)} custom-call(s32[1]{0:T(128)} %bitcast.here_ref, bf16[224,64,576]{2,1,0:T(8,128)(2,1)} %cache_ref.3, bf16[18,8,512]{2,1,0:T(8,128)(2,1)S(1)} %gate.2.after_ref.refs_8_), custom_call_target="tpu_custom_call" | custom-call | bytes 8257536 | tf_op jit(solution)/shard_map/load/pallas_call | solution.py:52
  23.2 0.9 %collective-permute-done.5.refs_7_ = bf16[18,8,512]{2,1,0:T(8,128)(2,1)S(1)} collective-permute-done((bf16[18,8,512]{2,1,0:T(8,128)(2,1)S(1)}, bf16[18,8,512]{2,1,0:T(8,128)(2,1)S(1)}, u32[]{:S(2)}, u32[]{:S(2)}) %collective-permute-start.5) | collective-permute-done | bytes 147488 | tf_op jit(solution)/shard_map/ppermute | solution.py:355
  24.1 1.6 %collective-permute-done.6.refs_9_ = bf16[18,8,512]{2,1,0:T(8,128)(2,1)S(1)} collective-permute-done((bf16[18,8,512]{2,1,0:T(8,128)(2,1)S(1)}, bf16[18,8,512]{2,1,0:T(8,128)(2,1)S(1)}, u32[]{:S(2)}, u32[]{:S(2)}) %collective-permute-start.6) | collective-permute-done | bytes 147488 | tf_op jit(solution)/shard_map/ppermute | solution.py:355
  25.7 13.2 %attend.1 = (bf16[17,8,512]{2,1,0:T(8,128)(2,1)S(1)}, bf16[17,8,512]{2,1,0:T(8,128)(2,1)S(1)}, bf16[17,8,512]{2,1,0:T(8,128)(2,1)S(1)}, bf16[17,8,512]{2,1,0:T(8...) custom-call(s32[224]{0:T(256)S(1)} %copy-done.3, ...), custom_call_target="tpu_custom_call" | custom-call | flops 7985954816 | bytes 16515072 | tf_op jit(solution)/shard_map/attend/pallas_call | solution.py:223
  38.9 1.3 %collective-permute-start.8 = (bf16[17,8,512]{2,1,0:T(8,128)(2,1)S(1)}, bf16[17,8,512]{2,1,0:T(8,128)(2,1)S(1)}, u32[]{:S(2)}, u32[]{:S(2)}) collective-permute-start(bf16[17,8,512]{2,1,0:T(8,128)(2,1)S(1)} %get-tuple-element.18), channel_id=1, source_target_pairs={{0,2},{2,0},{4,6},{6,4},{8,10},{10,8},{12,14},{14,12},{1,3},{3,1},... | collective-permute-start | bytes 417800 | tf_op jit(solution)/shard_map/ppermute | solution.py:355
  41.0 1.2 %collective-permute-start.12 = (bf16[17,8,512]{2,1,0:T(8,128)(2,1)S(1)}, bf16[17,8,512]{2,1,0:T(8,128)(2,1)S(1)}, u32[]{:S(2)}, u32[]{:S(2)}) collective-permute-start(bf16[17,8,512]{2,1,0:T(8,128)(2,1)S(1)} %get-tuple-element.22), channel_id=1, source_target_pairs={{0,2},{2,0},{4,6},{6,4},{8,10},{10,8},{12,14},{14,12},{1,3},{3,1},... | collective-permute-start | bytes 417800 | tf_op jit(solution)/shard_map/ppermute | solution.py:355
  42.2 0.8 %collective-permute-start.7 = (bf16[17,8,512]{2,1,0:T(8,128)(2,1)S(1)}, bf16[17,8,512]{2,1,0:T(8,128)(2,1)S(1)}, u32[]{:S(2)}, u32[]{:S(2)}) collective-permute-start(bf16[17,8,512]{2,1,0:T(8,128)(2,1)S(1)} %get-tuple-element.16), channel_id=1, source_target_pairs={{0,2},{2,0},{4,6},{6,4},{8,10},{10,8},{12,14},{14,12},{1,3},{3,1},... | collective-permute-start | bytes 417800 | tf_op jit(solution)/shard_map/ppermute | solution.py:355
  43.0 2.6 %collective-permute-done.8.got_ref = bf16[17,8,512]{2,1,0:T(8,128)(2,1)S(1)} collective-permute-done((bf16[17,8,512]{2,1,0:T(8,128)(2,1)S(1)}, bf16[17,8,512]{2,1,0:T(8,128)(2,1)S(1)}, u32[]{:S(2)}, u32[]{:S(2)}) %collective-permute-start.8) | collective-permute-done | bytes 139296 | tf_op jit(solution)/shard_map/ppermute | solution.py:355
  45.7 2.5 %collective-permute-start.9 = (bf16[17,8,512]{2,1,0:T(8,128)(2,1)S(1)}, bf16[17,8,512]{2,1,0:T(8,128)(2,1)S(1)}, u32[]{:S(2)}, u32[]{:S(2)}) collective-permute-start(bf16[17,8,512]{2,1,0:T(8,128)(2,1)S(1)} %merge.3), channel_id=1, source_target_pairs={{0,8},{2,10},{4,12},{6,14},{8,0},{10,2},{12,4},{14,6},{1,9},{3,11}... | collective-permute-start | bytes 417800 | tf_op jit(solution)/shard_map/ppermute | solution.py:355
  48.7 3.9 %collective-permute-start.11 = (bf16[17,8,512]{2,1,0:T(8,128)(2,1)S(1)}, bf16[17,8,512]{2,1,0:T(8,128)(2,1)S(1)}, u32[]{:S(2)}, u32[]{:S(2)}) collective-permute-start(bf16[17,8,512]{2,1,0:T(8,128)(2,1)S(1)} %merge.4), channel_id=1, source_target_pairs={{0,12},{2,14},{4,8},{6,10},{8,4},{10,6},{12,0},{14,2},{1,13},{3,15... | collective-permute-start | bytes 417800 | tf_op jit(solution)/shard_map/ppermute | solution.py:355
  52.8 3.0 %collective-permute-done.9.refs_2_ = bf16[17,8,512]{2,1,0:T(8,128)(2,1)S(1)} collective-permute-done((bf16[17,8,512]{2,1,0:T(8,128)(2,1)S(1)}, bf16[17,8,512]{2,1,0:T(8,128)(2,1)S(1)}, u32[]{:S(2)}, u32[]{:S(2)}) %collective-permute-start.9) | collective-permute-done | bytes 139296 | tf_op jit(solution)/shard_map/ppermute | solution.py:355
  56.6 1.8 %collective-permute-done.13.refs_4_ = bf16[17,8,512]{2,1,0:T(8,128)(2,1)S(1)} collective-permute-done((bf16[17,8,512]{2,1,0:T(8,128)(2,1)S(1)}, bf16[17,8,512]{2,1,0:T(8,128)(2,1)S(1)}, u32[]{:S(2)}, u32[]{:S(2)}) %collective-permute-start.13) | collective-permute-done | bytes 139296 | tf_op jit(solution)/shard_map/ppermute | solution.py:355
  58.3 3.4 %finish.1 = bf16[16,16,448]{2,1,0:T(8,128)(2,1)S(1)} custom-call(s32[1]{0:T(128)} %bitcast.here_ref, bf16[8,512,128]{2,1,0:T(8,128)(2,1)S(1)} %copy-done.2, bf16[1024,7168]{1,0:T(8,128)(2,1)S(1)} %get-tuple-element.14.weight_ref, bf16[17,8,512]{2,1,0:T(8,128)(2,1)S(1)} %get-tuple-element.15.refs_0_, bf16[17,8,512]{2,1,0:T(8,128)(2,1)S(1)} %collective-permute-done.7.refs_1_, ...), custom_call_target="tpu_custom_call" | custom-call | flops 3758096384 | tf_op jit(solution)/shard_map/finish/pallas_call | solution.py:326
  61.8 1.3 %collective-permute-done.14 = bf16[8,16,448]{2,1,0:T(8,128)(2,1)S(1)} collective-permute-done((bf16[8,16,448]{2,1,0:T(8,128)(2,1)S(1)}, bf16[8,16,448]{2,1,0:T(8,128)(2,1)S(1)}, u32[]{:S(2)}, u32[]{:S(2)}) %collective-permute-start.14) | collective-permute-done | bytes 114720 | tf_op jit(solution)/shard_map/ppermute | solution.py:388
  63.2 12.4 %all_to_all.5 = bf16[8,16,448]{2,1,0:T(8,128)(2,1)S(1)} all-to-all(bf16[8,16,448]{2,1,0:T(8,128)(2,1)S(1)} %add_convert_fusion), channel_id=1, replica_groups=mesh['groups'=2,'ctx'=8,'head'=2] {'ctx'}, dimensions={0} | all-to-all | bytes 229376 | tf_op jit(solution)/shard_map/all_to_all | solution.py:394
  (33 shorter events, 4.3 us)
Async XLA Ops:
  0.0 1.2 %copy-start = (bf16[8,128,512]{2,1,0:T(8,128)(2,1)S(1)}, bf16[8,128,512]{2,1,0:T(8,128)(2,1)}, u32[]{:S(2)}) copy-start(bf16[8,128,512]{2,1,0:T(8,128)(2,1)} %param.9) | copy-start | bytes 3145732
  2.4 15.1 %collective-permute-start.4 = (bf16[18,8,512]{2,1,0:T(8,128)(2,1)S(1)}, bf16[18,8,512]{2,1,0:T(8,128)(2,1)S(1)}, u32[]{:S(2)}, u32[]{:S(2)}) collective-permute-start(bf16[18,8,512]{2,1,0:T(8,128)(2,1)S(1)} %pad_maximum_fusion.after_ref.refs_2_), channel_id=1, source_target_pairs={{0,8},{2,10},{4,12},{6,14},{8,0},{10,2},{12,4},{14,6},{1,9},{3,11}... | collective-permute-start | bytes 442376 | tf_op jit(solution)/shard_map/ppermute | solution.py:355
  6.5 12.9 %collective-permute-start = (bf16[18,8,512]{2,1,0:T(8,128)(2,1)S(1)}, bf16[18,8,512]{2,1,0:T(8,128)(2,1)S(1)}, u32[]{:S(2)}, u32[]{:S(2)}) collective-permute-start(bf16[18,8,512]{2,1,0:T(8,128)(2,1)S(1)} %pad_maximum_fusion.after_ref.refs_2_), channel_id=1, source_target_pairs={{0,12},{2,14},{4,8},{6,10},{8,4},{10,6},{12,0},{14,2},{1,13},{3,15... | collective-permute-start | bytes 442376 | tf_op jit(solution)/shard_map/ppermute | solution.py:355
  7.8 15.4 %collective-permute-start.3 = (bf16[18,8,512]{2,1,0:T(8,128)(2,1)S(1)}, bf16[18,8,512]{2,1,0:T(8,128)(2,1)S(1)}, u32[]{:S(2)}, u32[]{:S(2)}) collective-permute-start(bf16[18,8,512]{2,1,0:T(8,128)(2,1)S(1)} %pad_maximum_fusion.after_ref.refs_2_), channel_id=1, source_target_pairs={{0,6},{2,4},{4,2},{6,0},{8,14},{10,12},{12,10},{14,8},{1,7},{3,5},... | collective-permute-start | bytes 442376 | tf_op jit(solution)/shard_map/ppermute | solution.py:355
  9.0 14.2 %collective-permute-start.2 = (bf16[18,8,512]{2,1,0:T(8,128)(2,1)S(1)}, bf16[18,8,512]{2,1,0:T(8,128)(2,1)S(1)}, u32[]{:S(2)}, u32[]{:S(2)}) collective-permute-start(bf16[18,8,512]{2,1,0:T(8,128)(2,1)S(1)} %pad_maximum_fusion.after_ref.refs_2_), channel_id=1, source_target_pairs={{0,4},{2,6},{4,0},{6,2},{8,12},{10,14},{12,8},{14,10},{1,5},{3,7},... | collective-permute-start | bytes 442376 | tf_op jit(solution)/shard_map/ppermute | solution.py:355
  10.8 12.4 %collective-permute-start.1 = (bf16[18,8,512]{2,1,0:T(8,128)(2,1)S(1)}, bf16[18,8,512]{2,1,0:T(8,128)(2,1)S(1)}, u32[]{:S(2)}, u32[]{:S(2)}) collective-permute-start(bf16[18,8,512]{2,1,0:T(8,128)(2,1)S(1)} %pad_maximum_fusion.after_ref.refs_2_), channel_id=1, source_target_pairs={{0,2},{2,0},{4,6},{6,4},{8,10},{10,8},{12,14},{14,12},{1,3},{3,1},... | collective-permute-start | bytes 442376 | tf_op jit(solution)/shard_map/ppermute | solution.py:355
  17.5 6.6 %collective-permute-start.5 = (bf16[18,8,512]{2,1,0:T(8,128)(2,1)S(1)}, bf16[18,8,512]{2,1,0:T(8,128)(2,1)S(1)}, u32[]{:S(2)}, u32[]{:S(2)}) collective-permute-start(bf16[18,8,512]{2,1,0:T(8,128)(2,1)S(1)} %gate.3.refs_6_), channel_id=1, source_target_pairs={{0,2},{2,0},{4,6},{6,4},{8,10},{10,8},{12,14},{14,12},{1,3},{3,1},... | collective-permute-start | bytes 442376 | tf_op jit(solution)/shard_map/ppermute | solution.py:355
  19.4 6.3 %copy-start.3 = (s32[224]{0:T(256)S(1)}, s32[224]{0:T(256)}, u32[]{:S(2)}) copy-start(s32[224]{0:T(256)} %owner_ref.1) | copy-start | bytes 2692
  19.4 6.3 %collective-permute-start.6 = (bf16[18,8,512]{2,1,0:T(8,128)(2,1)S(1)}, bf16[18,8,512]{2,1,0:T(8,128)(2,1)S(1)}, u32[]{:S(2)}, u32[]{:S(2)}) collective-permute-start(bf16[18,8,512]{2,1,0:T(8,128)(2,1)S(1)} %gate.2.after_ref.refs_8_), channel_id=1, source_target_pairs={{0,2},{2,0},{4,6},{6,4},{8,10},{10,8},{12,14},{14,12},{1,3},{3,1},... | collective-permute-start | bytes 442376 | tf_op jit(solution)/shard_map/ppermute | solution.py:355
  23.2 35.2 %copy-start.2 = (bf16[8,512,128]{2,1,0:T(8,128)(2,1)S(1)}, bf16[8,512,128]{2,1,0:T(8,128)(2,1)}, u32[]{:S(2)}) copy-start(bf16[8,512,128]{2,1,0:T(8,128)(2,1)} %value_ref.1) | copy-start | bytes 3145732
  25.7 50.6 %copy-start.1 = (bf16[8,128,512]{2,1,0:T(8,128)(2,1)S(1)}, bf16[8,128,512]{2,1,0:T(8,128)(2,1)}, u32[]{:S(2)}) copy-start(bf16[8,128,512]{2,1,0:T(8,128)(2,1)} %param.9) | copy-start | bytes 3145732
  38.9 6.7 %collective-permute-start.8 = (bf16[17,8,512]{2,1,0:T(8,128)(2,1)S(1)}, bf16[17,8,512]{2,1,0:T(8,128)(2,1)S(1)}, u32[]{:S(2)}, u32[]{:S(2)}) collective-permute-start(bf16[17,8,512]{2,1,0:T(8,128)(2,1)S(1)} %get-tuple-element.18), channel_id=1, source_target_pairs={{0,2},{2,0},{4,6},{6,4},{8,10},{10,8},{12,14},{14,12},{1,3},{3,1},... | collective-permute-start | bytes 417800 | tf_op jit(solution)/shard_map/ppermute | solution.py:355
  40.2 8.4 %collective-permute-start.10 = (bf16[17,8,512]{2,1,0:T(8,128)(2,1)S(1)}, bf16[17,8,512]{2,1,0:T(8,128)(2,1)S(1)}, u32[]{:S(2)}, u32[]{:S(2)}) collective-permute-start(bf16[17,8,512]{2,1,0:T(8,128)(2,1)S(1)} %get-tuple-element.20), channel_id=1, source_target_pairs={{0,2},{2,0},{4,6},{6,4},{8,10},{10,8},{12,14},{14,12},{1,3},{3,1},... | collective-permute-start | bytes 417800 | tf_op jit(solution)/shard_map/ppermute | solution.py:355
  41.0 11.6 %collective-permute-start.12 = (bf16[17,8,512]{2,1,0:T(8,128)(2,1)S(1)}, bf16[17,8,512]{2,1,0:T(8,128)(2,1)S(1)}, u32[]{:S(2)}, u32[]{:S(2)}) collective-permute-start(bf16[17,8,512]{2,1,0:T(8,128)(2,1)S(1)} %get-tuple-element.22), channel_id=1, source_target_pairs={{0,2},{2,0},{4,6},{6,4},{8,10},{10,8},{12,14},{14,12},{1,3},{3,1},... | collective-permute-start | bytes 417800 | tf_op jit(solution)/shard_map/ppermute | solution.py:355
  42.2 10.6 %collective-permute-start.7 = (bf16[17,8,512]{2,1,0:T(8,128)(2,1)S(1)}, bf16[17,8,512]{2,1,0:T(8,128)(2,1)S(1)}, u32[]{:S(2)}, u32[]{:S(2)}) collective-permute-start(bf16[17,8,512]{2,1,0:T(8,128)(2,1)S(1)} %get-tuple-element.16), channel_id=1, source_target_pairs={{0,2},{2,0},{4,6},{6,4},{8,10},{10,8},{12,14},{14,12},{1,3},{3,1},... | collective-permute-start | bytes 417800 | tf_op jit(solution)/shard_map/ppermute | solution.py:355
  45.7 10.1 %collective-permute-start.9 = (bf16[17,8,512]{2,1,0:T(8,128)(2,1)S(1)}, bf16[17,8,512]{2,1,0:T(8,128)(2,1)S(1)}, u32[]{:S(2)}, u32[]{:S(2)}) collective-permute-start(bf16[17,8,512]{2,1,0:T(8,128)(2,1)S(1)} %merge.3), channel_id=1, source_target_pairs={{0,8},{2,10},{4,12},{6,14},{8,0},{10,2},{12,4},{14,6},{1,9},{3,11}... | collective-permute-start | bytes 417800 | tf_op jit(solution)/shard_map/ppermute | solution.py:355
  48.7 7.8 %collective-permute-start.11 = (bf16[17,8,512]{2,1,0:T(8,128)(2,1)S(1)}, bf16[17,8,512]{2,1,0:T(8,128)(2,1)S(1)}, u32[]{:S(2)}, u32[]{:S(2)}) collective-permute-start(bf16[17,8,512]{2,1,0:T(8,128)(2,1)S(1)} %merge.4), channel_id=1, source_target_pairs={{0,12},{2,14},{4,8},{6,10},{8,4},{10,6},{12,0},{14,2},{1,13},{3,15... | collective-permute-start | bytes 417800 | tf_op jit(solution)/shard_map/ppermute | solution.py:355
  52.7 5.6 %collective-permute-start.13 = (bf16[17,8,512]{2,1,0:T(8,128)(2,1)S(1)}, bf16[17,8,512]{2,1,0:T(8,128)(2,1)S(1)}, u32[]{:S(2)}, u32[]{:S(2)}) collective-permute-start(bf16[17,8,512]{2,1,0:T(8,128)(2,1)S(1)} %merge.5), channel_id=1, source_target_pairs={{0,4},{2,6},{4,0},{6,2},{8,12},{10,14},{12,8},{14,10},{1,5},{3,7},... | collective-permute-start | bytes 417800 | tf_op jit(solution)/shard_map/ppermute | solution.py:355
  61.7 1.4 %collective-permute-start.14 = (bf16[8,16,448]{2,1,0:T(8,128)(2,1)S(1)}, bf16[8,16,448]{2,1,0:T(8,128)(2,1)S(1)}, u32[]{:S(2)}, u32[]{:S(2)}) collective-permute-start(bf16[8,16,448]{2,1,0:T(8,128)(2,1)S(1)} %slice.9), channel_id=1, source_target_pairs={{0,1},{1,0},{2,3},{3,2},{4,5},{5,4},{6,7},{7,6},{8,9},{9,8},{10,11... | collective-permute-start | bytes 344072 | tf_op jit(solution)/shard_map/ppermute | solution.py:388

commit v10 on v9

--- a/solution.py
+++ b/solution.py
@@ -376,12 +376,13 @@
         cache_parts, page_owner, output_weight, score_scale, latent_size,
     )
 
-    across = {distance: exchange(message_to[distance ^ 1], 1) for distance in [*even, 0]}
+    across = {distance: exchange(message_to[distance ^ 1], 1) for distance in [*even[:-1], 0]}
+    direct = [exchange(message_to[distance], distance) for distance in (3, 2)]
     arrived = [
-        exchange(merge(message_to[distance], across[distance]), distance) for distance in even
+        exchange(merge(message_to[distance], across[distance]), distance)
+        for distance in even[:-1]
     ]
-    messages = [message_to[0], across[0], *arrived]
-
+    messages = [message_to[0], across[0], *direct, *arrived]
     pieces = finish(here, messages, value_absorb, weight, count, count * cores)
     total = pieces[:count].astype(jnp.float32)
     for distance in range(1, cores):

time: 76.4 us -> 77.2 us (1.010)
  starting transfers between devices: 21.6 us -> 24.3 us
  waiting for transfers between devices: 14.7 us -> 12.8 us
    ppermute x14, starting transfers between devices: 21.6 us -> 24.2 us  [exchange(): return lax.ppermute(x, 'ctx', [(i, i ^ distance) for i in range(count)])]
    ppermute x14, waiting for transfers between devices: 13.4 us -> 11.5 us  [exchange(): return lax.ppermute(x, 'ctx', [(i, i ^ distance) for i in range(count)])]
  transfers between devices with their start and end apart: 15 -> 15, of which waited for: 9 -> 7; matrix products, arithmetic and copies ran while one was open for 0% -> 0% of each run, Pallas kernels for 10% -> 10%
where the time goes in v10:
time: 77.2 us; the launch traced here: 76.9 us
  starting transfers between devices  24.3 us (31%)
  Pallas kernels  24.2 us (31%)
  waiting for transfers between devices  12.8 us (17%)
  blocking collectives  12.5 us (16%)
  local copies, waits for them, and re-layouts  1.36 us (2%)
  matrix products  0.99 us (1%)
    ppermute x14, starting transfers between devices, exchange(): return lax.ppermute(x, 'ctx', [(i, i ^ distance) for i in range(count)])  24.2 us
    pallas_call x1, Pallas kernels, attend(): pl.pallas_call(functools.partial(attend_kernel, score_scale, steps, block...  13.2 us
    all_to_all x1, blocking collectives, body(): lax.all_to_all(total.astype(jnp.bfloat16), 'ctx', split_axis=0, concat_ax...  12.5 us
    ppermute x14, waiting for transfers between devices, exchange(): return lax.ppermute(x, 'ctx', [(i, i ^ distance) for i in range(count)])  11.5 us
    pallas_call x2, Pallas kernels, load(): pl.pallas_call(functools.partial(load_kernel, part * pages), out_shape=pl...  7.23 us
    pallas_call x1, Pallas kernels, finish(): pl.pallas_call(functools.partial(finish_kernel, block_columns, count), ou...  3.4 us
  transfers between devices with their start and end apart: 15, of which 7 were waited for; matrix products, arithmetic and copies ran while one was open for 0% of the time, Pallas kernels for 10%

profile of v10, /device:TPU:0, one launch (start us, length us, event | category | flops | bytes accessed | tf_op | source)
XLA Modules:
  0.0 76.9 jit_solution(17966451908957984647)
XLA Ops:
  0.0 0.9 %reshape.10 = bf16[2,8,8,64]{3,2,1,0:T(8,128)(2,1)S(1)} reshape(bf16[16,512]{1,0:T(8,128)(2,1)} %param.8) | data formatting | bytes 32768 | tf_op jit(solution)/shard_map/reshape | solution.py:361
  1.2 1.0 %fusion.1 = bf16[8,512,16]{1,2,0:T(8,128)(2,1)S(1)} fusion(bf16[8,128,512]{2,1,0:T(8,128)(2,1)S(1)} %copy-done, bf16[16,8,128]{2,1,0:T(8,128)(2,1)} %param.7), kind=kOutput, calls=%fused_computation.5 | convolution fusion | flops 16777216 | bytes 1212416 | tf_op jit(solution)/shard_map/rhn,hnl->rhl/dot_general | solution.py:357
  2.4 4.1 %collective-permute-start.4 = (bf16[18,8,512]{2,1,0:T(8,128)(2,1)S(1)}, bf16[18,8,512]{2,1,0:T(8,128)(2,1)S(1)}, u32[]{:S(2)}, u32[]{:S(2)}) collective-permute-start(bf16[18,8,512]{2,1,0:T(8,128)(2,1)S(1)} %pad_maximum_fusion.after_ref.refs_2_), channel_id=1, source_target_pairs={{0,8},{2,10},{4,12},{6,14},{8,0},{10,2},{12,4},{14,6},{1,9},{3,11}... | collective-permute-start | bytes 442376 | tf_op jit(solution)/shard_map/ppermute | solution.py:355
  6.5 1.3 %collective-permute-start = (bf16[18,8,512]{2,1,0:T(8,128)(2,1)S(1)}, bf16[18,8,512]{2,1,0:T(8,128)(2,1)S(1)}, u32[]{:S(2)}, u32[]{:S(2)}) collective-permute-start(bf16[18,8,512]{2,1,0:T(8,128)(2,1)S(1)} %pad_maximum_fusion.after_ref.refs_2_), channel_id=1, source_target_pairs={{0,12},{2,14},{4,8},{6,10},{8,4},{10,6},{12,0},{14,2},{1,13},{3,15... | collective-permute-start | bytes 442376 | tf_op jit(solution)/shard_map/ppermute | solution.py:355
  7.8 1.2 %collective-permute-start.3 = (bf16[18,8,512]{2,1,0:T(8,128)(2,1)S(1)}, bf16[18,8,512]{2,1,0:T(8,128)(2,1)S(1)}, u32[]{:S(2)}, u32[]{:S(2)}) collective-permute-start(bf16[18,8,512]{2,1,0:T(8,128)(2,1)S(1)} %pad_maximum_fusion.after_ref.refs_2_), channel_id=1, source_target_pairs={{0,6},{2,4},{4,2},{6,0},{8,14},{10,12},{12,10},{14,8},{1,7},{3,5},... | collective-permute-start | bytes 442376 | tf_op jit(solution)/shard_map/ppermute | solution.py:355
  9.0 1.8 %collective-permute-start.2 = (bf16[18,8,512]{2,1,0:T(8,128)(2,1)S(1)}, bf16[18,8,512]{2,1,0:T(8,128)(2,1)S(1)}, u32[]{:S(2)}, u32[]{:S(2)}) collective-permute-start(bf16[18,8,512]{2,1,0:T(8,128)(2,1)S(1)} %pad_maximum_fusion.after_ref.refs_2_), channel_id=1, source_target_pairs={{0,4},{2,6},{4,0},{6,2},{8,12},{10,14},{12,8},{14,10},{1,5},{3,7},... | collective-permute-start | bytes 442376 | tf_op jit(solution)/shard_map/ppermute | solution.py:355
  11.3 3.6 %load.2.after_ref.refs_0_ = bf16[112,64,576]{2,1,0:T(8,128)(2,1)S(1)} custom-call(s32[1]{0:T(128)} %bitcast.here_ref, bf16[224,64,576]{2,1,0:T(8,128)(2,1)} %cache_ref.3, bf16[18,8,512]{2,1,0:T(8,128)(2,1)S(1)} %pad_maximum_fusion.after_ref.refs_2_), custom_call_target="tpu_custom_call" | custom-call | bytes 8257536 | tf_op jit(solution)/shard_map/load/pallas_call | solution.py:52
  14.9 2.6 %collective-permute-done.4.block_ref = bf16[18,8,512]{2,1,0:T(8,128)(2,1)S(1)} collective-permute-done((bf16[18,8,512]{2,1,0:T(8,128)(2,1)S(1)}, bf16[18,8,512]{2,1,0:T(8,128)(2,1)S(1)}, u32[]{:S(2)}, u32[]{:S(2)}) %collective-permute-start.4) | collective-permute-done | bytes 147488 | tf_op jit(solution)/shard_map/ppermute | solution.py:355
  17.5 1.9 %collective-permute-start.5 = (bf16[18,8,512]{2,1,0:T(8,128)(2,1)S(1)}, bf16[18,8,512]{2,1,0:T(8,128)(2,1)S(1)}, u32[]{:S(2)}, u32[]{:S(2)}) collective-permute-start(bf16[18,8,512]{2,1,0:T(8,128)(2,1)S(1)} %gate.3.refs_6_), channel_id=1, source_target_pairs={{0,2},{2,0},{4,6},{6,4},{8,10},{10,8},{12,14},{14,12},{1,3},{3,1},... | collective-permute-start | bytes 442376 | tf_op jit(solution)/shard_map/ppermute | solution.py:355
  19.5 3.6 %load.3.refs_1_ = bf16[112,64,576]{2,1,0:T(8,128)(2,1)S(1)} custom-call(s32[1]{0:T(128)} %bitcast.here_ref, bf16[224,64,576]{2,1,0:T(8,128)(2,1)} %cache_ref.3, bf16[18,8,512]{2,1,0:T(8,128)(2,1)S(1)} %gate.2.after_ref.refs_8_), custom_call_target="tpu_custom_call" | custom-call | bytes 8257536 | tf_op jit(solution)/shard_map/load/pallas_call | solution.py:52
  24.1 1.6 %collective-permute-done.6.refs_9_ = bf16[18,8,512]{2,1,0:T(8,128)(2,1)S(1)} collective-permute-done((bf16[18,8,512]{2,1,0:T(8,128)(2,1)S(1)}, bf16[18,8,512]{2,1,0:T(8,128)(2,1)S(1)}, u32[]{:S(2)}, u32[]{:S(2)}) %collective-permute-start.6) | collective-permute-done | bytes 147488 | tf_op jit(solution)/shard_map/ppermute | solution.py:355
  25.7 13.2 %attend.1 = (bf16[17,8,512]{2,1,0:T(8,128)(2,1)S(1)}, bf16[17,8,512]{2,1,0:T(8,128)(2,1)S(1)}, bf16[17,8,512]{2,1,0:T(8,128)(2,1)S(1)}, bf16[17,8,512]{2,1,0:T(8...) custom-call(s32[224]{0:T(256)S(1)} %copy-done.3, ...), custom_call_target="tpu_custom_call" | custom-call | flops 7985954816 | bytes 16515072 | tf_op jit(solution)/shard_map/attend/pallas_call | solution.py:223
  38.9 1.2 %collective-permute-start.10 = (bf16[17,8,512]{2,1,0:T(8,128)(2,1)S(1)}, bf16[17,8,512]{2,1,0:T(8,128)(2,1)S(1)}, u32[]{:S(2)}, u32[]{:S(2)}) collective-permute-start(bf16[17,8,512]{2,1,0:T(8,128)(2,1)S(1)} %get-tuple-element.20), channel_id=1, source_target_pairs={{0,2},{2,0},{4,6},{6,4},{8,10},{10,8},{12,14},{14,12},{1,3},{3,1},... | collective-permute-start | bytes 417800 | tf_op jit(solution)/shard_map/ppermute | solution.py:355
  40.1 0.9 %collective-permute-start.12 = (bf16[17,8,512]{2,1,0:T(8,128)(2,1)S(1)}, bf16[17,8,512]{2,1,0:T(8,128)(2,1)S(1)}, u32[]{:S(2)}, u32[]{:S(2)}) collective-permute-start(bf16[17,8,512]{2,1,0:T(8,128)(2,1)S(1)} %get-tuple-element.22), channel_id=1, source_target_pairs={{0,2},{2,0},{4,6},{6,4},{8,10},{10,8},{12,14},{14,12},{1,3},{3,1},... | collective-permute-start | bytes 417800 | tf_op jit(solution)/shard_map/ppermute | solution.py:355
  41.0 1.1 %collective-permute-start.7 = (bf16[17,8,512]{2,1,0:T(8,128)(2,1)S(1)}, bf16[17,8,512]{2,1,0:T(8,128)(2,1)S(1)}, u32[]{:S(2)}, u32[]{:S(2)}) collective-permute-start(bf16[17,8,512]{2,1,0:T(8,128)(2,1)S(1)} %get-tuple-element.16), channel_id=1, source_target_pairs={{0,2},{2,0},{4,6},{6,4},{8,10},{10,8},{12,14},{14,12},{1,3},{3,1},... | collective-permute-start | bytes 417800 | tf_op jit(solution)/shard_map/ppermute | solution.py:355
  42.2 1.2 %collective-permute-start.8 = (bf16[17,8,512]{2,1,0:T(8,128)(2,1)S(1)}, bf16[17,8,512]{2,1,0:T(8,128)(2,1)S(1)}, u32[]{:S(2)}, u32[]{:S(2)}) collective-permute-start(bf16[17,8,512]{2,1,0:T(8,128)(2,1)S(1)} %get-tuple-element.17), channel_id=1, source_target_pairs={{0,6},{2,4},{4,2},{6,0},{8,14},{10,12},{12,10},{14,8},{1,7},{3,5},... | collective-permute-start | bytes 417800 | tf_op jit(solution)/shard_map/ppermute | solution.py:355
  43.4 1.1 %collective-permute-start.9 = (bf16[17,8,512]{2,1,0:T(8,128)(2,1)S(1)}, bf16[17,8,512]{2,1,0:T(8,128)(2,1)S(1)}, u32[]{:S(2)}, u32[]{:S(2)}) collective-permute-start(bf16[17,8,512]{2,1,0:T(8,128)(2,1)S(1)} %get-tuple-element.18), channel_id=1, source_target_pairs={{0,4},{2,6},{4,0},{6,2},{8,12},{10,14},{12,8},{14,10},{1,5},{3,7},... | collective-permute-start | bytes 417800 | tf_op jit(solution)/shard_map/ppermute | solution.py:355
  44.5 2.8 %collective-permute-done.10.got_ref = bf16[17,8,512]{2,1,0:T(8,128)(2,1)S(1)} collective-permute-done((bf16[17,8,512]{2,1,0:T(8,128)(2,1)S(1)}, bf16[17,8,512]{2,1,0:T(8,128)(2,1)S(1)}, u32[]{:S(2)}, u32[]{:S(2)}) %collective-permute-start.10) | collective-permute-done | bytes 139296 | tf_op jit(solution)/shard_map/ppermute | solution.py:355
  47.5 2.6 %collective-permute-start.11 = (bf16[17,8,512]{2,1,0:T(8,128)(2,1)S(1)}, bf16[17,8,512]{2,1,0:T(8,128)(2,1)S(1)}, u32[]{:S(2)}, u32[]{:S(2)}) collective-permute-start(bf16[17,8,512]{2,1,0:T(8,128)(2,1)S(1)} %merge.2), channel_id=1, source_target_pairs={{0,8},{2,10},{4,12},{6,14},{8,0},{10,2},{12,4},{14,6},{1,9},{3,11}... | collective-permute-start | bytes 417800 | tf_op jit(solution)/shard_map/ppermute | solution.py:355
  50.5 5.1 %collective-permute-start.13 = (bf16[17,8,512]{2,1,0:T(8,128)(2,1)S(1)}, bf16[17,8,512]{2,1,0:T(8,128)(2,1)S(1)}, u32[]{:S(2)}, u32[]{:S(2)}) collective-permute-start(bf16[17,8,512]{2,1,0:T(8,128)(2,1)S(1)} %merge.3), channel_id=1, source_target_pairs={{0,12},{2,14},{4,8},{6,10},{8,4},{10,6},{12,0},{14,2},{1,13},{3,15... | collective-permute-start | bytes 417800 | tf_op jit(solution)/shard_map/ppermute | solution.py:355
  55.6 3.3 %collective-permute-done.11.refs_4_ = bf16[17,8,512]{2,1,0:T(8,128)(2,1)S(1)} collective-permute-done((bf16[17,8,512]{2,1,0:T(8,128)(2,1)S(1)}, bf16[17,8,512]{2,1,0:T(8,128)(2,1)S(1)}, u32[]{:S(2)}, u32[]{:S(2)}) %collective-permute-start.11) | collective-permute-done | bytes 139296 | tf_op jit(solution)/shard_map/ppermute | solution.py:355
  58.9 3.4 %finish.1 = bf16[16,16,448]{2,1,0:T(8,128)(2,1)S(1)} custom-call(s32[1]{0:T(128)} %bitcast.here_ref, bf16[8,512,128]{2,1,0:T(8,128)(2,1)S(1)} %copy-done.2, bf16[1024,7168]{1,0:T(8,128)(2,1)S(1)} %get-tuple-element.14.weight_ref, bf16[17,8,512]{2,1,0:T(8,128)(2,1)S(1)} %get-tuple-element.15.refs_0_, bf16[17,8,512]{2,1,0:T(8,128)(2,1)S(1)} %collective-permute-done.7.refs_1_, ...), custom_call_target="tpu_custom_call" | custom-call | flops 3758096384 | tf_op jit(solution)/shard_map/finish/pallas_call | solution.py:326
  62.4 1.3 %collective-permute-done.14 = bf16[8,16,448]{2,1,0:T(8,128)(2,1)S(1)} collective-permute-done((bf16[8,16,448]{2,1,0:T(8,128)(2,1)S(1)}, bf16[8,16,448]{2,1,0:T(8,128)(2,1)S(1)}, u32[]{:S(2)}, u32[]{:S(2)}) %collective-permute-start.14) | collective-permute-done | bytes 114720 | tf_op jit(solution)/shard_map/ppermute | solution.py:389
  63.8 12.5 %all_to_all.5 = bf16[8,16,448]{2,1,0:T(8,128)(2,1)S(1)} all-to-all(bf16[8,16,448]{2,1,0:T(8,128)(2,1)S(1)} %add_convert_fusion), channel_id=1, replica_groups=mesh['groups'=2,'ctx'=8,'head'=2] {'ctx'}, dimensions={0} | all-to-all | bytes 229376 | tf_op jit(solution)/shard_map/all_to_all | solution.py:395
  (32 shorter events, 3.4 us)
Async XLA Ops:
  0.0 1.2 %copy-start = (bf16[8,128,512]{2,1,0:T(8,128)(2,1)S(1)}, bf16[8,128,512]{2,1,0:T(8,128)(2,1)}, u32[]{:S(2)}) copy-start(bf16[8,128,512]{2,1,0:T(8,128)(2,1)} %param.9) | copy-start | bytes 3145732
  2.4 15.1 %collective-permute-start.4 = (bf16[18,8,512]{2,1,0:T(8,128)(2,1)S(1)}, bf16[18,8,512]{2,1,0:T(8,128)(2,1)S(1)}, u32[]{:S(2)}, u32[]{:S(2)}) collective-permute-start(bf16[18,8,512]{2,1,0:T(8,128)(2,1)S(1)} %pad_maximum_fusion.after_ref.refs_2_), channel_id=1, source_target_pairs={{0,8},{2,10},{4,12},{6,14},{8,0},{10,2},{12,4},{14,6},{1,9},{3,11}... | collective-permute-start | bytes 442376 | tf_op jit(solution)/shard_map/ppermute | solution.py:355
  6.5 12.9 %collective-permute-start = (bf16[18,8,512]{2,1,0:T(8,128)(2,1)S(1)}, bf16[18,8,512]{2,1,0:T(8,128)(2,1)S(1)}, u32[]{:S(2)}, u32[]{:S(2)}) collective-permute-start(bf16[18,8,512]{2,1,0:T(8,128)(2,1)S(1)} %pad_maximum_fusion.after_ref.refs_2_), channel_id=1, source_target_pairs={{0,12},{2,14},{4,8},{6,10},{8,4},{10,6},{12,0},{14,2},{1,13},{3,15... | collective-permute-start | bytes 442376 | tf_op jit(solution)/shard_map/ppermute | solution.py:355
  7.8 15.4 %collective-permute-start.3 = (bf16[18,8,512]{2,1,0:T(8,128)(2,1)S(1)}, bf16[18,8,512]{2,1,0:T(8,128)(2,1)S(1)}, u32[]{:S(2)}, u32[]{:S(2)}) collective-permute-start(bf16[18,8,512]{2,1,0:T(8,128)(2,1)S(1)} %pad_maximum_fusion.after_ref.refs_2_), channel_id=1, source_target_pairs={{0,6},{2,4},{4,2},{6,0},{8,14},{10,12},{12,10},{14,8},{1,7},{3,5},... | collective-permute-start | bytes 442376 | tf_op jit(solution)/shard_map/ppermute | solution.py:355
  9.0 14.2 %collective-permute-start.2 = (bf16[18,8,512]{2,1,0:T(8,128)(2,1)S(1)}, bf16[18,8,512]{2,1,0:T(8,128)(2,1)S(1)}, u32[]{:S(2)}, u32[]{:S(2)}) collective-permute-start(bf16[18,8,512]{2,1,0:T(8,128)(2,1)S(1)} %pad_maximum_fusion.after_ref.refs_2_), channel_id=1, source_target_pairs={{0,4},{2,6},{4,0},{6,2},{8,12},{10,14},{12,8},{14,10},{1,5},{3,7},... | collective-permute-start | bytes 442376 | tf_op jit(solution)/shard_map/ppermute | solution.py:355
  10.8 12.4 %collective-permute-start.1 = (bf16[18,8,512]{2,1,0:T(8,128)(2,1)S(1)}, bf16[18,8,512]{2,1,0:T(8,128)(2,1)S(1)}, u32[]{:S(2)}, u32[]{:S(2)}) collective-permute-start(bf16[18,8,512]{2,1,0:T(8,128)(2,1)S(1)} %pad_maximum_fusion.after_ref.refs_2_), channel_id=1, source_target_pairs={{0,2},{2,0},{4,6},{6,4},{8,10},{10,8},{12,14},{14,12},{1,3},{3,1},... | collective-permute-start | bytes 442376 | tf_op jit(solution)/shard_map/ppermute | solution.py:355
  17.5 6.6 %collective-permute-start.5 = (bf16[18,8,512]{2,1,0:T(8,128)(2,1)S(1)}, bf16[18,8,512]{2,1,0:T(8,128)(2,1)S(1)}, u32[]{:S(2)}, u32[]{:S(2)}) collective-permute-start(bf16[18,8,512]{2,1,0:T(8,128)(2,1)S(1)} %gate.3.refs_6_), channel_id=1, source_target_pairs={{0,2},{2,0},{4,6},{6,4},{8,10},{10,8},{12,14},{14,12},{1,3},{3,1},... | collective-permute-start | bytes 442376 | tf_op jit(solution)/shard_map/ppermute | solution.py:355
  19.4 6.3 %copy-start.3 = (s32[224]{0:T(256)S(1)}, s32[224]{0:T(256)}, u32[]{:S(2)}) copy-start(s32[224]{0:T(256)} %owner_ref.1) | copy-start | bytes 2692
  19.4 6.3 %collective-permute-start.6 = (bf16[18,8,512]{2,1,0:T(8,128)(2,1)S(1)}, bf16[18,8,512]{2,1,0:T(8,128)(2,1)S(1)}, u32[]{:S(2)}, u32[]{:S(2)}) collective-permute-start(bf16[18,8,512]{2,1,0:T(8,128)(2,1)S(1)} %gate.2.after_ref.refs_8_), channel_id=1, source_target_pairs={{0,2},{2,0},{4,6},{6,4},{8,10},{10,8},{12,14},{14,12},{1,3},{3,1},... | collective-permute-start | bytes 442376 | tf_op jit(solution)/shard_map/ppermute | solution.py:355
  23.2 35.8 %copy-start.2 = (bf16[8,512,128]{2,1,0:T(8,128)(2,1)S(1)}, bf16[8,512,128]{2,1,0:T(8,128)(2,1)}, u32[]{:S(2)}) copy-start(bf16[8,512,128]{2,1,0:T(8,128)(2,1)} %value_ref.1) | copy-start | bytes 3145732
  25.7 51.2 %copy-start.1 = (bf16[8,128,512]{2,1,0:T(8,128)(2,1)S(1)}, bf16[8,128,512]{2,1,0:T(8,128)(2,1)}, u32[]{:S(2)}) copy-start(bf16[8,128,512]{2,1,0:T(8,128)(2,1)} %param.9) | copy-start | bytes 3145732
  38.9 8.4 %collective-permute-start.10 = (bf16[17,8,512]{2,1,0:T(8,128)(2,1)S(1)}, bf16[17,8,512]{2,1,0:T(8,128)(2,1)S(1)}, u32[]{:S(2)}, u32[]{:S(2)}) collective-permute-start(bf16[17,8,512]{2,1,0:T(8,128)(2,1)S(1)} %get-tuple-element.20), channel_id=1, source_target_pairs={{0,2},{2,0},{4,6},{6,4},{8,10},{10,8},{12,14},{14,12},{1,3},{3,1},... | collective-permute-start | bytes 417800 | tf_op jit(solution)/shard_map/ppermute | solution.py:355
  40.1 10.2 %collective-permute-start.12 = (bf16[17,8,512]{2,1,0:T(8,128)(2,1)S(1)}, bf16[17,8,512]{2,1,0:T(8,128)(2,1)S(1)}, u32[]{:S(2)}, u32[]{:S(2)}) collective-permute-start(bf16[17,8,512]{2,1,0:T(8,128)(2,1)S(1)} %get-tuple-element.22), channel_id=1, source_target_pairs={{0,2},{2,0},{4,6},{6,4},{8,10},{10,8},{12,14},{14,12},{1,3},{3,1},... | collective-permute-start | bytes 417800 | tf_op jit(solution)/shard_map/ppermute | solution.py:355
  41.0 14.6 %collective-permute-start.7 = (bf16[17,8,512]{2,1,0:T(8,128)(2,1)S(1)}, bf16[17,8,512]{2,1,0:T(8,128)(2,1)S(1)}, u32[]{:S(2)}, u32[]{:S(2)}) collective-permute-start(bf16[17,8,512]{2,1,0:T(8,128)(2,1)S(1)} %get-tuple-element.16), channel_id=1, source_target_pairs={{0,2},{2,0},{4,6},{6,4},{8,10},{10,8},{12,14},{14,12},{1,3},{3,1},... | collective-permute-start | bytes 417800 | tf_op jit(solution)/shard_map/ppermute | solution.py:355
  42.2 13.5 %collective-permute-start.8 = (bf16[17,8,512]{2,1,0:T(8,128)(2,1)S(1)}, bf16[17,8,512]{2,1,0:T(8,128)(2,1)S(1)}, u32[]{:S(2)}, u32[]{:S(2)}) collective-permute-start(bf16[17,8,512]{2,1,0:T(8,128)(2,1)S(1)} %get-tuple-element.17), channel_id=1, source_target_pairs={{0,6},{2,4},{4,2},{6,0},{8,14},{10,12},{12,10},{14,8},{1,7},{3,5},... | collective-permute-start | bytes 417800 | tf_op jit(solution)/shard_map/ppermute | solution.py:355
  43.4 12.2 %collective-permute-start.9 = (bf16[17,8,512]{2,1,0:T(8,128)(2,1)S(1)}, bf16[17,8,512]{2,1,0:T(8,128)(2,1)S(1)}, u32[]{:S(2)}, u32[]{:S(2)}) collective-permute-start(bf16[17,8,512]{2,1,0:T(8,128)(2,1)S(1)} %get-tuple-element.18), channel_id=1, source_target_pairs={{0,4},{2,6},{4,0},{6,2},{8,12},{10,14},{12,8},{14,10},{1,5},{3,7},... | collective-permute-start | bytes 417800 | tf_op jit(solution)/shard_map/ppermute | solution.py:355
  47.5 11.4 %collective-permute-start.11 = (bf16[17,8,512]{2,1,0:T(8,128)(2,1)S(1)}, bf16[17,8,512]{2,1,0:T(8,128)(2,1)S(1)}, u32[]{:S(2)}, u32[]{:S(2)}) collective-permute-start(bf16[17,8,512]{2,1,0:T(8,128)(2,1)S(1)} %merge.2), channel_id=1, source_target_pairs={{0,8},{2,10},{4,12},{6,14},{8,0},{10,2},{12,4},{14,6},{1,9},{3,11}... | collective-permute-start | bytes 417800 | tf_op jit(solution)/shard_map/ppermute | solution.py:355
  50.5 8.4 %collective-permute-start.13 = (bf16[17,8,512]{2,1,0:T(8,128)(2,1)S(1)}, bf16[17,8,512]{2,1,0:T(8,128)(2,1)S(1)}, u32[]{:S(2)}, u32[]{:S(2)}) collective-permute-start(bf16[17,8,512]{2,1,0:T(8,128)(2,1)S(1)} %merge.3), channel_id=1, source_target_pairs={{0,12},{2,14},{4,8},{6,10},{8,4},{10,6},{12,0},{14,2},{1,13},{3,15... | collective-permute-start | bytes 417800 | tf_op jit(solution)/shard_map/ppermute | solution.py:355
  62.4 1.4 %collective-permute-start.14 = (bf16[8,16,448]{2,1,0:T(8,128)(2,1)S(1)}, bf16[8,16,448]{2,1,0:T(8,128)(2,1)S(1)}, u32[]{:S(2)}, u32[]{:S(2)}) collective-permute-start(bf16[8,16,448]{2,1,0:T(8,128)(2,1)S(1)} %slice.9), channel_id=1, source_target_pairs={{0,1},{1,0},{2,3},{3,2},{4,5},{5,4},{6,7},{7,6},{8,9},{9,8},{10,11... | collective-permute-start | bytes 344072 | tf_op jit(solution)/shard_map/ppermute | solution.py:389
